TPU v7x, 32 devices: a whole 2x2x4 slice. The times are simulated.
32 devices in a mesh: row: 8 (over z, x), col: 4 (over y, core).
Axes of the slice: x: 2, y: 2, z: 4, core: 2. Of those that a mesh axis runs over, the one named last changes fastest.
Arguments:
- features: bfloat16 [512, 512, 128], P('row', 'col'), may hold values from -6 to 6
- kernels: bfloat16 [2, 3, 3, 128, 128], replicated, may hold values from -0.1875 to 0.1875
- length: int32 [1], replicated, may hold values from 256 to 512
- cotangent: bfloat16 [512, 512, 128], P('row', 'col'), may hold values from -6 to 6
Outputs:
- output_map: bfloat16 [512, 512, 128], P('row', 'col')
- feature_grad: bfloat16 [512, 512, 128], P('row', 'col')
- kernel_gradient: float32 [2, 3, 3, 128, 128], replicated
Inputs may be any that keep to these rules, and one draw needn't show every extreme that they name: The protein occupies the first length rows and columns of the pair map.
All inputs are finite; a program needn't handle non-finite values.
Results may differ from a plain program's by a relative error of at most 0.0039.
Values may be sent and summed in bfloat16 or wider, within the bound.
No kernel may reach another device: no remote copies, remote signals or barrier semaphores. Data moves between devices by JAX's collectives and lax.ppermute only.
A program may use at most 192 MiB of HBM per device.

v0:
```python
import functools

import jax
import jax.numpy as jnp
from jax import lax
from jax.experimental import pallas as pl
from jax.experimental.pallas import tpu as pltpu
from jax.sharding import PartitionSpec as P

H = 3
C = 128
F32 = jnp.float32
BF16 = jnp.bfloat16
VMEM_LIMIT = 56 * 1024 * 1024
ANY = pl.BlockSpec(memory_space=pl.ANY)
VMEM = pl.BlockSpec(memory_space=pltpu.VMEM)
SMEM = pl.BlockSpec(memory_space=pltpu.SMEM)


def params():
    return pltpu.CompilerParams(vmem_limit_bytes=VMEM_LIMIT)


def cost(flops, nbytes):
    return pl.CostEstimate(flops=int(flops), bytes_accessed=int(nbytes), transcendentals=0)


def to_blocks(rows):
    cols = rows[0].shape[0]
    v = [r.reshape(cols // 8, 8, C) for r in rows]
    low = lax.broadcasted_iota(jnp.int32, v[0].shape, 1) < 4

    def swap(a, b):
        return jnp.where(low, a, pltpu.roll(b, 4, 1)), jnp.where(low, pltpu.roll(a, 4, 1), b)

    a, b = swap(v[0], v[1])
    c, d = swap(v[2], v[3])
    y = jnp.stack([jnp.concatenate([a, c], axis=1), jnp.concatenate([b, d], axis=1)], axis=1)
    return y.reshape(4 * cols, C)


def from_blocks(y):
    cols = y.shape[0] // 4
    y = y.reshape(cols // 8, 2, 2, 8, C)
    a, b, c, d = y[:, 0, 0], y[:, 1, 0], y[:, 0, 1], y[:, 1, 1]
    low = lax.broadcasted_iota(jnp.int32, a.shape, 1) < 4

    def swap(a, b):
        return jnp.where(low, a, pltpu.roll(b, 4, 1)), jnp.where(low, pltpu.roll(a, 4, 1), b)

    r0, r1 = swap(a, b)
    r2, r3 = swap(c, d)
    return [r.reshape(cols, C) for r in (r0, r1, r2, r3)]


def column_mask(meta, nj):
    shape = (nj + 2 * H, 16, C)
    j = lax.broadcasted_iota(jnp.int32, shape, 0)
    s = lax.broadcasted_iota(jnp.int32, shape, 1)
    col = meta[1] + 4 * (j - H) + (s & 3)
    return ((col >= 0) & (col < meta[2])).astype(F32).reshape(-1, C)


def live(meta, cm, a, start, size):
    s = lax.broadcasted_iota(jnp.int32, (1, 16, C), 1)
    row = meta[0] + 4 * a + (s >> 2)
    row_mask = ((row >= 0) & (row < meta[2])).astype(F32)
    return (cm[start : start + size, :].reshape(size // 16, 16, C) * row_mask).reshape(size, C)


def elu_parts(v):
    e = jnp.exp(jnp.minimum(v, 0.0))
    return jnp.maximum(v, 0.0) + (e - 1.0), e


def conv_pairs(read, pairs, d, weights):
    parts = []
    for a in pairs:
        cells = []
        for q in range(3):
            cells += [read(a, q), read(a + d, q), read(a - d, q), read(a + 2 * d, q)]
        parts.append(jnp.concatenate(cells, axis=1))
    left = jnp.concatenate(parts, axis=0) if len(parts) > 1 else parts[0]
    return jnp.dot(left, weights, preferred_element_type=F32)


def outer(left, right):
    return lax.dot_general(left, right, (((0,), (0,)), ((), ())), preferred_element_type=F32)


def pack_kernel(k_ref, w_ref):
    zero = jnp.zeros((C, C), BF16)
    for layer in range(2):
        for back in range(2):
            def tap(p, q):
                if back:
                    return k_ref[layer, 2 - p, 2 - q].T
                return k_ref[layer, p, q]

            n = 2 * layer + back
            for q in range(3):
                t0, t1, t2 = tap(0, q), tap(1, q), tap(2, q)
                o = 4 * C * q
                blocks = ((t1, t0), (t2, t1), (t0, zero), (zero, t2))
                for i, (x, y) in enumerate(blocks):
                    w_ref[n, o + C * i : o + C * (i + 1), :C] = x
                    w_ref[n, o + C * i : o + C * (i + 1), C:] = y


def layout_kernel(meta, f_ref, g_ref, fx_ref, gx_ref, left_ref, right_ref, *, step, nj):
    m0 = 16 * nj
    base = pl.program_id(0) * step
    s = lax.broadcasted_iota(jnp.int32, (nj, 16, C), 1)
    j = lax.broadcasted_iota(jnp.int32, (nj, 16, C), 0)
    cm = (meta[1] + 4 * j + (s & 3) < meta[2]).astype(F32)
    s1 = lax.broadcasted_iota(jnp.int32, (1, 16, C), 1)
    for k in range(step):
        fb = to_blocks([f_ref[4 * k + i].astype(F32) for i in range(4)]).astype(BF16)
        gb = to_blocks([g_ref[4 * k + i].astype(F32) for i in range(4)])
        rm = (meta[0] + 4 * (base + k) + (s1 >> 2) < meta[2]).astype(F32)
        gb = (gb.reshape(nj, 16, C) * (cm * rm)).reshape(m0, C).astype(BF16)
        for n, (v, x_ref) in enumerate(((fb, fx_ref), (gb, gx_ref))):
            x_ref[k, 16 * H : 16 * H + m0] = v
            left_ref[n, k] = v[: 16 * H]
            right_ref[n, k] = v[m0 - 16 * H :]


def assemble_kernel(fx_in, gx_in, lh, rh, fx, gx, ua, ub, da, db, sem, *, na, nj):
    del fx_in, gx_in
    m0 = 16 * nj
    jobs = []

    def go(src, dst):
        c = pltpu.make_async_copy(src, dst, sem.at[len(jobs)])
        c.start()
        jobs.append(c)

    for n, x in enumerate((fx, gx)):
        go(lh.at[n], x.at[:, pl.ds(0, 16 * H)])
        go(rh.at[n], x.at[:, pl.ds(16 * H + m0, 16 * H)])
    for c in jobs:
        c.wait()
    first = len(jobs)
    go(fx.at[pl.ds(0, 1)], ua.at[pl.ds(0, 1)])
    go(gx.at[pl.ds(0, 2)], ua.at[pl.ds(1, 2)])
    go(fx.at[pl.ds(1, 2)], ub.at[pl.ds(0, 2)])
    go(gx.at[pl.ds(2, 1)], ub.at[pl.ds(2, 1)])
    go(fx.at[pl.ds(na - 1, 1)], da.at[pl.ds(0, 1)])
    go(gx.at[pl.ds(na - 2, 2)], da.at[pl.ds(1, 2)])
    go(fx.at[pl.ds(na - 3, 2)], db.at[pl.ds(0, 2)])
    go(gx.at[pl.ds(na - 3, 1)], db.at[pl.ds(2, 1)])
    for c in jobs[first:]:
        c.wait()


def inner_kernel(meta, fx, gx, wp, a1o, a2o, so, g1o, gfo, acc_o, a1, a2, st, es, g1, gf, cm, sem, *, na, nj):
    m0, m1, m2, w = 16 * nj, 16 * (nj + 2), 16 * (nj + 4), 16 * (nj + 6)
    ni = na - 4
    cm[...] = column_mask(meta, nj)

    def activate(a, _):
        v, _e = elu_parts(fx[a].astype(F32))
        a1[a] = (v * live(meta, cm, a, 0, w)).astype(BF16)
        return 0

    lax.fori_loop(0, na, activate, 0)
    out_a1 = pltpu.make_async_copy(a1, a1o, sem.at[0])
    out_a1.start()

    def quad(t, _):
        r = 2 + 4 * t
        acc = conv_pairs(lambda row, q: a1[row, pl.ds(16 * q, m2), :], [r, r + 2], 1, wp[0])
        for k in range(2):
            for b in range(2):
                row = r + 2 * k + b
                v = fx[row, pl.ds(16, m2), :].astype(F32) + acc[k * m2 : (k + 1) * m2, b * C : (b + 1) * C]
                act, e = elu_parts(v)
                a2[row + 2] = (act * live(meta, cm, row, 16, m2)).astype(BF16)
                es[row - 2] = e[16 : 16 + m1]
                st[row - 2] = v[32 : 32 + m0]
        acc = conv_pairs(lambda row, q: gx[row, pl.ds(32 * q, m1), :], [r, r + 1], 2, wp[3])
        for k in range(2):
            for b in range(2):
                row = r + k + 2 * b
                back = acc[k * m1 : (k + 1) * m1, b * C : (b + 1) * C]
                full = gx[row, pl.ds(32, m1), :].astype(F32) + live(meta, cm, row, 32, m1) * es[row - 2] * back
                g1[row + 1] = full.astype(BF16)
                gf[row - 2] = full[16 : 16 + m0]
        return 0

    lax.fori_loop(0, ni // 4, quad, 0)
    copies = [
        pltpu.make_async_copy(a2.at[pl.ds(4, ni)], a2o.at[pl.ds(4, ni)], sem.at[1]),
        pltpu.make_async_copy(st, so.at[pl.ds(2, ni)], sem.at[2]),
        pltpu.make_async_copy(g1.at[pl.ds(3, ni)], g1o.at[pl.ds(3, ni)], sem.at[3]),
        pltpu.make_async_copy(gf, gfo.at[pl.ds(2, ni)], sem.at[4]),
    ]
    for c in copies:
        c.start()
    for i in (0, 1, 2, 3):
        a2[i] = jnp.zeros((m2, C), BF16)
        a2[na + i] = jnp.zeros((m2, C), BF16)
    for i in (0, 1, 2):
        g1[i] = jnp.zeros((m1, C), BF16)
        g1[na - 1 + i] = jnp.zeros((m1, C), BF16)

    def second(rows):
        left = [jnp.concatenate([a2[b + 2 + s, 32 : 32 + m0] for s in (2, 0, -2)], axis=1) for b in rows]
        right = [jnp.concatenate([gx[b, 16 + 32 * q : 16 + 32 * q + m0] for q in range(3)], axis=1) for b in rows]
        return outer(jnp.concatenate(left, axis=0), jnp.concatenate(right, axis=0))

    def first(rows):
        left = [jnp.concatenate([g1[b + 1 + s, 16 : 16 + m0] for s in (1, 0, -1)], axis=1) for b in rows]
        right = [jnp.concatenate([a1[b, 32 + 16 * q : 32 + 16 * q + m0] for q in range(3)], axis=1) for b in rows]
        return outer(jnp.concatenate(left, axis=0), jnp.concatenate(right, axis=0))

    half = na // 2
    acc_o[1] = second(range(half))
    acc_o[1] += second(range(half, na))
    acc_o[0] = first(range(1, half))
    acc_o[0] += first(range(half, na - 1))
    out_a1.wait()
    for c in copies:
        c.wait()


def edge_kernel(
    meta, fx, gx, a1i, up, dn, wp, acc_i, _a2, _s, _g1, _gf, a2o, so, g1o, gfo, kg,
    a1, g, f, fh, a2, st, es, g1, gf, cm, sem, *, na, nj,
):
    m0, m1, m2, w = 16 * nj, 16 * (nj + 2), 16 * (nj + 4), 16 * (nj + 6)
    jobs = []

    def go(src, dst):
        c = pltpu.make_async_copy(src, dst, sem.at[len(jobs)])
        c.start()
        jobs.append(c)

    go(up.at[pl.ds(0, 1)], fh.at[0])
    go(dn.at[pl.ds(0, 1)], fh.at[1])
    go(up.at[pl.ds(1, 2)], g.at[0, pl.ds(0, 2)])
    go(gx.at[pl.ds(0, 6)], g.at[0, pl.ds(2, 6)])
    go(gx.at[pl.ds(na - 6, 6)], g.at[1, pl.ds(0, 6)])
    go(dn.at[pl.ds(1, 2)], g.at[1, pl.ds(6, 2)])
    go(a1i.at[pl.ds(0, 3)], a1.at[0, pl.ds(1, 3)])
    go(a1i.at[pl.ds(na - 3, 3)], a1.at[1, pl.ds(0, 3)])
    go(fx.at[pl.ds(0, 2)], f.at[0])
    go(fx.at[pl.ds(na - 2, 2)], f.at[1])
    cm[...] = column_mask(meta, nj)
    for c in jobs:
        c.wait()
    for s, row, slot in ((0, -1, 0), (1, na, 3)):
        v, _e = elu_parts(fh[s, 0].astype(F32))
        a1[s, slot] = (v * live(meta, cm, row, 0, w)).astype(BF16)

    acc = conv_pairs(lambda i, q: a1[i // 8, i % 8, 16 * q : 16 * q + m2], [1, 9], 1, wp[0])
    for s in range(2):
        for b in range(2):
            row = (na - 2) * s + b
            v = f[s, b, 16 : 16 + m2].astype(F32) + acc[s * m2 : (s + 1) * m2, b * C : (b + 1) * C]
            act, e = elu_parts(v)
            a2[s, b] = (act * live(meta, cm, row, 16, m2)).astype(BF16)
            es[s, b] = e[16 : 16 + m1]
            st[s, b] = v[32 : 32 + m0]
    acc = conv_pairs(lambda i, q: g[i // 16, i % 16, 32 * q : 32 * q + m1], [2, 3, 18, 19], 2, wp[3])
    for s in range(2):
        for b in range(2):
            row = (na - 2) * s + b
            k = 2 * s + b
            back = acc[k * m1 : (k + 1) * m1, s * C : (s + 1) * C]
            full = g[s, 2 + 2 * s + b, 32 : 32 + m1].astype(F32) + live(meta, cm, row, 32, m1) * es[s, b] * back
            g1[s, b] = full.astype(BF16)
            gf[s, b] = full[16 : 16 + m0]
    outs = len(jobs)
    for s in range(2):
        go(a2.at[s], a2o.at[pl.ds(2 + (na - 2) * s, 2)])
        go(st.at[s], so.at[pl.ds((na - 2) * s, 2)])
        go(g1.at[s], g1o.at[pl.ds(1 + (na - 2) * s, 2)])
        go(gf.at[s], gfo.at[pl.ds((na - 2) * s, 2)])

    rows = [(s, b) for s in range(2) for b in range(2)]
    left = jnp.concatenate([a2[s, b, 32 : 32 + m0] for s, b in rows], axis=0)
    for p in range(3):
        right = [
            jnp.concatenate([g[s, 2 * s + b + 2 * p, 16 + 32 * q : 16 + 32 * q + m0] for q in range(3)], axis=1)
            for s, b in rows
        ]
        total = acc_i[1, C * p : C * (p + 1)] + outer(left, jnp.concatenate(right, axis=0))
        for q in range(3):
            kg[1, 2 - p, 2 - q] = total[:, C * q : C * (q + 1)].astype(BF16)
    left = jnp.concatenate([g1[s, b, 16 : 16 + m0] for s, b in rows], axis=0)
    for p in range(3):
        right = [
            jnp.concatenate([a1[s, b + p, 32 + 16 * q : 32 + 16 * q + m0] for q in range(3)], axis=1) for s, b in rows
        ]
        total = acc_i[0, C * p : C * (p + 1)] + outer(left, jnp.concatenate(right, axis=0))
        for q in range(3):
            kg[0, p, q] = total[:, C * q : C * (q + 1)].T.astype(BF16)
    for c in jobs[outs:]:
        c.wait()


def last_kernel(
    meta, fx, gx, a1i, upa, dna, upb, dnb, wp, a2i, si, g1i, gfi, out, fg,
    a1, g, f, fm, a2, st, es, g1, gf, cm, ot, ft, sem, osem, *, na, nj,
):
    m0, m1, m2, w = 16 * nj, 16 * (nj + 2), 16 * (nj + 4), 16 * (nj + 6)
    jobs = []

    def go(src, dst):
        c = pltpu.make_async_copy(src, dst, sem.at[len(jobs)])
        c.start()
        jobs.append(c)

    go(upb.at[pl.ds(0, 2)], f.at[0, pl.ds(0, 2)])
    go(upa.at[pl.ds(0, 1)], f.at[0, pl.ds(2, 1)])
    go(dna.at[pl.ds(0, 1)], f.at[1, pl.ds(0, 1)])
    go(dnb.at[pl.ds(0, 2)], f.at[1, pl.ds(1, 2)])
    go(upb.at[pl.ds(2, 1)], g.at[0, pl.ds(0, 1)])
    go(upa.at[pl.ds(2, 1)], g.at[0, pl.ds(1, 1)])
    go(gx.at[pl.ds(1, 1)], g.at[0, pl.ds(2, 1)])
    go(gx.at[pl.ds(3, 1)], g.at[0, pl.ds(3, 1)])
    go(gx.at[pl.ds(na - 4, 1)], g.at[1, pl.ds(0, 1)])
    go(gx.at[pl.ds(na - 2, 1)], g.at[1, pl.ds(1, 1)])
    go(dna.at[pl.ds(1, 1)], g.at[1, pl.ds(2, 1)])
    go(dnb.at[pl.ds(2, 1)], g.at[1, pl.ds(3, 1)])
    go(a1i.at[pl.ds(0, 1)], a1.at[0, pl.ds(3, 1)])
    go(a1i.at[pl.ds(na - 1, 1)], a1.at[1, pl.ds(0, 1)])
    early = len(jobs)
    go(a2i.at[pl.ds(2, na)], a2.at[pl.ds(2, na)])
    go(si, st)
    go(g1i.at[pl.ds(1, na)], g1.at[pl.ds(1, na)])
    go(fx.at[:, pl.ds(16 * H, m0)], fm)
    go(gfi, gf)
    cm[...] = column_mask(meta, nj)
    for c in jobs[:early]:
        c.wait()
    for s in range(2):
        for i in range(3):
            row = i - 3 if s == 0 else na + i
            v, _e = elu_parts(f[s, i].astype(F32))
            a1[s, i + s] = (v * live(meta, cm, row, 0, w)).astype(BF16)
    acc = conv_pairs(lambda i, q: a1[i // 8, i % 8, 16 * q : 16 * q + m2], [1, 9], 1, wp[0])
    for s in range(2):
        for b in range(2):
            row = b - 2 if s == 0 else na + b
            v = f[s, 1 - s + b, 16 : 16 + m2].astype(F32) + acc[s * m2 : (s + 1) * m2, b * C : (b + 1) * C]
            act, e = elu_parts(v)
            a2[row + 2] = (act * live(meta, cm, row, 16, m2)).astype(BF16)
            if b != s:
                es[s] = e[16 : 16 + m1]
    acc = conv_pairs(lambda i, q: g[i // 8, i % 8, 32 * q : 32 * q + m1], [1, 9], 1, wp[3])
    for s in range(2):
        row = -1 if s == 0 else na
        back = acc[s * m1 : (s + 1) * m1, s * C : (s + 1) * C]
        full = g[s, 1 + s, 32 : 32 + m1].astype(F32) + live(meta, cm, row, 32, m1) * es[s] * back
        g1[row + 1] = full.astype(BF16)
    for c in jobs[early:]:
        c.wait()

    def quad(t, _):
        r = 4 * t
        acc = conv_pairs(lambda row, q: a2[row + 2, pl.ds(32 * q, m0), :], [r, r + 1], 2, wp[2])
        for k in range(2):
            for b in range(2):
                row = r + k + 2 * b
                v = (st[row] + acc[k * m0 : (k + 1) * m0, b * C : (b + 1) * C]) * live(meta, cm, row, 16 * H, m0)
                for i, x in enumerate(from_blocks(v)):
                    ot[4 * row + i] = x.astype(BF16)
        acc = conv_pairs(lambda row, q: g1[row + 1, pl.ds(16 * q, m0), :], [r, r + 2], 1, wp[1])
        for k in range(2):
            for b in range(2):
                row = r + 2 * k + b
                slope = jnp.exp(jnp.minimum(fm[row].astype(F32), 0.0))
                back = acc[k * m0 : (k + 1) * m0, b * C : (b + 1) * C]
                v = gf[row] + live(meta, cm, row, 16 * H, m0) * slope * back
                for i, x in enumerate(from_blocks(v)):
                    ft[4 * row + i] = x.astype(BF16)
        pltpu.make_async_copy(ot.at[pl.ds(16 * t, 16)], out.at[pl.ds(16 * t, 16)], osem.at[0]).start()
        pltpu.make_async_copy(ft.at[pl.ds(16 * t, 16)], fg.at[pl.ds(16 * t, 16)], osem.at[1]).start()
        return 0

    lax.fori_loop(0, na // 4, quad, 0)
    pltpu.make_async_copy(ot, out, osem.at[0]).wait()
    pltpu.make_async_copy(ft, fg, osem.at[1]).wait()


def sum_kernel(meta, x_ref, o_ref):
    total = jnp.sum(x_ref[...].astype(F32), axis=0) / meta[2].astype(F32)
    o_ref[...] = jnp.broadcast_to(total.astype(BF16)[None], o_ref.shape)


def shift(x, axis, step):
    n = lax.axis_size(axis)
    return lax.ppermute(x, axis, [(i, i + step) for i in range(n) if 0 <= i + step < n])


def body(features, kernels, length, cotangent):
    rows, cols, _ = features.shape
    na, nj = rows // 4, cols // 4
    m0, m1, m2, w = 16 * nj, 16 * (nj + 2), 16 * (nj + 4), 16 * (nj + 6)
    ni = na - 4
    meta = jnp.stack([lax.axis_index("row") * rows, lax.axis_index("col") * cols, length[0]]).astype(jnp.int32)
    sds = jax.ShapeDtypeStruct

    step = 4
    fx, gx, to_left, to_right = pl.pallas_call(
        functools.partial(layout_kernel, step=step, nj=nj),
        grid=(na // step,),
        in_specs=[SMEM] + [pl.BlockSpec((4 * step, cols, C), lambda i: (i, 0, 0))] * 2,
        out_specs=[pl.BlockSpec((step, w, C), lambda i: (i, 0, 0))] * 2
        + [pl.BlockSpec((2, step, 16 * H, C), lambda i: (0, i, 0, 0))] * 2,
        out_shape=[sds((na, w, C), BF16)] * 2 + [sds((2, na, 16 * H, C), BF16)] * 2,
        compiler_params=params(),
        cost_estimate=cost(0, 16 << 20),
    )(meta, features, cotangent)
    rh = shift(to_left, "col", -1)
    lh = shift(to_right, "col", 1)
    wp = pl.pallas_call(
        pack_kernel,
        in_specs=[VMEM],
        out_specs=VMEM,
        out_shape=sds((4, 12 * C, 2 * C), BF16),
        compiler_params=params(),
        cost_estimate=cost(0, 8 << 20),
    )(kernels)
    fx, gx, ua, ub, da, db = pl.pallas_call(
        functools.partial(assemble_kernel, na=na, nj=nj),
        in_specs=[ANY] * 4,
        out_specs=[ANY] * 6,
        out_shape=[sds((na, w, C), BF16)] * 2 + [sds((3, w, C), BF16)] * 4,
        scratch_shapes=[pltpu.SemaphoreType.DMA((12,))],
        input_output_aliases={0: 0, 1: 1},
        compiler_params=params(),
        cost_estimate=cost(0, 4 << 20),
    )(fx, gx, lh, rh)
    dna = shift(ua, "row", -1)
    upa = shift(da, "row", 1)
    dnb = shift(ub, "row", -1)
    upb = shift(db, "row", 1)

    conv_flops = 2 * rows * cols * 9 * C * C
    a1, a2, st, g1, gf, acc = pl.pallas_call(
        functools.partial(inner_kernel, na=na, nj=nj),
        in_specs=[SMEM] + [VMEM] * 3,
        out_specs=[ANY] * 5 + [VMEM],
        out_shape=[
            sds((na, w, C), BF16),
            sds((na + 4, m2, C), BF16),
            sds((na, m0, C), F32),
            sds((na + 2, m1, C), BF16),
            sds((na, m0, C), F32),
            sds((2, 3 * C, 3 * C), F32),
        ],
        scratch_shapes=[
            pltpu.VMEM((na, w, C), BF16),
            pltpu.VMEM((na + 4, m2, C), BF16),
            pltpu.VMEM((ni, m0, C), F32),
            pltpu.VMEM((ni, m1, C), F32),
            pltpu.VMEM((na + 2, m1, C), BF16),
            pltpu.VMEM((ni, m0, C), F32),
            pltpu.VMEM((w, C), F32),
            pltpu.SemaphoreType.DMA((5,)),
        ],
        compiler_params=params(),
        cost_estimate=cost(4 * conv_flops, 24 << 20),
    )(meta, fx, gx, wp)

    a2, st, g1, gf, kg = pl.pallas_call(
        functools.partial(edge_kernel, na=na, nj=nj),
        in_specs=[SMEM] + [ANY] * 5 + [VMEM] * 2 + [ANY] * 4,
        out_specs=[ANY] * 4 + [VMEM],
        out_shape=[
            sds((na + 4, m2, C), BF16),
            sds((na, m0, C), F32),
            sds((na + 2, m1, C), BF16),
            sds((na, m0, C), F32),
            sds((2, 3, 3, C, C), BF16),
        ],
        scratch_shapes=[
            pltpu.VMEM((2, 4, w, C), BF16),
            pltpu.VMEM((2, 8, w, C), BF16),
            pltpu.VMEM((2, 2, w, C), BF16),
            pltpu.VMEM((2, 1, w, C), BF16),
            pltpu.VMEM((2, 2, m2, C), BF16),
            pltpu.VMEM((2, 2, m0, C), F32),
            pltpu.VMEM((2, 2, m1, C), F32),
            pltpu.VMEM((2, 2, m1, C), BF16),
            pltpu.VMEM((2, 2, m0, C), F32),
            pltpu.VMEM((w, C), F32),
            pltpu.SemaphoreType.DMA((18,)),
        ],
        input_output_aliases={8: 0, 9: 1, 10: 2, 11: 3},
        compiler_params=params(),
        cost_estimate=cost(conv_flops, 12 << 20),
    )(meta, fx, gx, a1, upa, dna, wp, acc, a2, st, g1, gf)

    axes = ("row", "col")
    parts = lax.axis_size(axes)
    shares = lax.all_to_all(kg.reshape(parts, -1, C), axes, 0, 0, tiled=True)
    spread = pl.pallas_call(
        sum_kernel,
        in_specs=[SMEM, VMEM],
        out_specs=VMEM,
        out_shape=sds(shares.shape, BF16),
        compiler_params=params(),
        cost_estimate=cost(0, 2 << 20),
    )(meta, shares)
    whole = lax.all_to_all(spread, axes, 0, 0, tiled=True)
    kernel_gradient = whole.reshape(kernels.shape).astype(F32)

    out, fg = pl.pallas_call(
        functools.partial(last_kernel, na=na, nj=nj),
        in_specs=[SMEM] + [ANY] * 7 + [VMEM] + [ANY] * 4,
        out_specs=[ANY] * 2,
        out_shape=[sds(features.shape, BF16)] * 2,
        scratch_shapes=[
            pltpu.VMEM((2, 4, w, C), BF16),
            pltpu.VMEM((2, 4, w, C), BF16),
            pltpu.VMEM((2, 3, w, C), BF16),
            pltpu.VMEM((na, m0, C), BF16),
            pltpu.VMEM((na + 4, m2, C), BF16),
            pltpu.VMEM((na, m0, C), F32),
            pltpu.VMEM((2, m1, C), F32),
            pltpu.VMEM((na + 2, m1, C), BF16),
            pltpu.VMEM((na, m0, C), F32),
            pltpu.VMEM((w, C), F32),
            pltpu.VMEM(features.shape, BF16),
            pltpu.VMEM(features.shape, BF16),
            pltpu.SemaphoreType.DMA((19,)),
            pltpu.SemaphoreType.DMA((2,)),
        ],
        compiler_params=params(),
        cost_estimate=cost(2 * conv_flops, 24 << 20),
    )(meta, fx, gx, a1, upa, dna, upb, dnb, wp, a2, st, g1, gf)
    return out, fg, kernel_gradient


def solution(mesh):
    spec = P("row", "col", None)
    return jax.shard_map(
        body, mesh=mesh, in_specs=(spec, P(), P(), spec), out_specs=(spec, spec, P()), check_vma=False
    )
```

profile of v0, /device:TPU:0, one launch (start us, length us, event | category | flops | bytes accessed | tf_op | source)
XLA Modules:
  0.0 215.6 jit_solution(17305101931624930021)
XLA Ops:
  1.3 0.7 pad_add_fusion.meta
  1.9 5.5 %shard_map.67 = (bf16[16,608,128]{2,1,0:T(8,128)(2,1)}, bf16[16,608,128]{2,1,0:T(8,128)(2,1)}, bf16[2,16,48,128]{3,2,1,0:T(8,128)(2,1)}, bf16[2,16,48,128]{3,2,1,0:T(8,128)(2,1)}) custom-call(s32[3]{0:T(128)} %pad_add_fusion.meta, bf16[64,128,128]{2,1,0:T(8,128)(2,1)} %f_ref.1, bf16[64,128,128]{2,1,0:T(8,128)(2,1)} %g_ref.1), custom_call_target="tpu_custom_call" | custom-call | bytes 16777216 | tf_op jit(solution)/shard_map/pallas_call | solution.py:407
  7.4 2.4 %collective-permute-start = (bf16[2,16,48,128]{3,2,1,0:T(8,128)(2,1)}, bf16[2,16,48,128]{3,2,1,0:T(8,128)(2,1)S(1)}, u32[]{:S(2)}, u32[]{:S(2)}) collective-permute-start(bf16[2,16,48,128]{3,2,1,0:T(8,128)(2,1)} %get-tuple-element.28), channel_id=1, source_target_pairs={{0,1},{1,2},{2,3},{4,5},{5,6},{6,7},{8,9},{9,10},{10,11},{12,13},{... | collective-permute-start | bytes 1179656 | tf_op jit(solution)/shard_map/ppermute | solution.py:395
  9.8 1.3 collective-permute-start.1
  11.1 3.2 %shard_map.69.wp = bf16[4,1536,256]{2,1,0:T(8,128)(2,1)} custom-call(bf16[2,3,3,128,128]{4,3,2,1,0:T(8,128)(2,1)} %k_ref.1), custom_call_target="tpu_custom_call" | custom-call | bytes 8388608 | tf_op jit(solution)/shard_map/pallas_call | solution.py:419
  14.4 0.0 collective-permute-done.lh
  14.4 1.4 collective-permute-done.1.rh
  15.8 0.0 copy-done.4
  15.8 0.7 copy-done.5
  16.5 82.7 %shard_map.68 = (bf16[16,608,128]{2,1,0:T(8,128)(2,1)}, bf16[16,608,128]{2,1,0:T(8,128)(2,1)}, bf16[3,608,128]{2,1,0:T(8,128)(2,1)}, bf16[3,608,128]{2,1,0:T(8,1...) custom-call(bf16[16,608,128]{2,1,0:T(8,128)(2,1)} %get-tuple-element, ...), custom_call_target="tpu_custom_call", output_to_operand_aliasing={{0}: (0, {}), {1}: (1, {})} | custom-call | bytes 4194304 | tf_op jit(solution)/shard_map/pallas_call | solution.py:427
  99.2 3.4 %collective-permute-start.2 = (bf16[3,608,128]{2,1,0:T(8,128)(2,1)}, bf16[3,608,128]{2,1,0:T(8,128)(2,1)S(1)}, u32[]{:S(2)}, u32[]{:S(2)}) collective-permute-start(bf16[3,608,128]{2,1,0:T(8,128)(2,1)} %get-tuple-element.33), channel_id=1, source_target_pairs={{0,4},{4,8},{8,12},{12,16},{16,20},{20,24},{24,28},{1,5},{5,9},{9,... | collective-permute-start | bytes 1400840 | tf_op jit(solution)/shard_map/ppermute | solution.py:395
  102.7 1.3 collective-permute-start.3
  104.0 19.4 %shard_map.70 = (bf16[16,608,128]{2,1,0:T(8,128)(2,1)}, bf16[20,576,128]{2,1,0:T(8,128)(2,1)}, f32[16,512,128]{2,1,0:T(8,128)}, bf16[18,544,128]{2,1,0:T(8,128)(...) custom-call(s32[3]{0:T(128)} %pad_add_fusion.meta, bf16[16,608,128]{2,1,0:T(8,128)(2,1)} %get-tuple-element.30.fx, ...), custom_call_target="tpu_custom_call" | custom-call | flops 9663676416 | bytes 25165824 | tf_op jit(solution)/shard_map/pallas_call | solution.py:443
  123.4 0.0 collective-permute-done.2.up.upa
  123.4 0.0 copy-start
  123.4 0.0 collective-permute-done.3.dn.dna
  123.4 0.8 copy-done
  124.2 0.2 copy-done.1
  124.4 10.9 %shard_map.71 = (bf16[20,576,128]{2,1,0:T(8,128)(2,1)}, f32[16,512,128]{2,1,0:T(8,128)}, bf16[18,544,128]{2,1,0:T(8,128)(2,1)}, f32[16,512,128]{2,1,0:T(8,128)}, bf16[2,3,3,128,128]{4,3,2,1,0:T(8,128)(2,1)}) custom-call(s32[3]{0:T(128)} %pad_add_fusion.meta, ...), custom_call_target="tpu_custom_call", output_to_operand_aliasing={{0}: (8, {}), {1}: (9, {}), {2}: (10, {}), {3}: (11, {})} | custom-call | flops 2415919104 | bytes 12582912 | tf_op jit(solution)/shard_map/pallas_call | solution.py:469
  135.3 0.0 copy-start.6
  135.3 28.1 %all_to_all.10.x_ref = bf16[32,72,128]{2,1,0:T(8,128)(2,1)} all-to-all(bf16[32,72,128]{2,1,0:T(8,128)(2,1)} %bitcast.6), channel_id=1, replica_groups=mesh['row'=8,'col'=4] {'row','col'}, dimensions={0} | all-to-all | bytes 1179648 | tf_op jit(solution)/shard_map/all_to_all | solution.py:500
  163.5 2.0 shard_map.73
  165.5 3.3 %all-to-all-start.1 = ((bf16[32,72,128]{2,1,0:T(8,128)(2,1)}), bf16[32,72,128]{2,1,0:T(8,128)(2,1)S(1)}, u32[]{:S(2)}, u32[]{:S(2)}) async-start(bf16[32,72,128]{2,1,0:T(8,128)(2,1)} %shard_map.73), calls=%async_computation.1 | async-start | bytes 1179648 | tf_op jit(solution)/shard_map/all_to_all | solution.py:509
  168.8 3.7 %collective-permute-start.4 = (bf16[3,608,128]{2,1,0:T(8,128)(2,1)S(1)}, bf16[3,608,128]{2,1,0:T(8,128)(2,1)S(1)}, u32[]{:S(2)}, u32[]{:S(2)}) collective-permute-start(bf16[3,608,128]{2,1,0:T(8,128)(2,1)S(1)} %copy-done.7), channel_id=1, source_target_pairs={{0,4},{4,8},{8,12},{12,16},{16,20},{20,24},{24,28},{1,5},{5,9},{9,... | collective-permute-start | bytes 1400840 | tf_op jit(solution)/shard_map/ppermute | solution.py:395
  172.5 1.5 collective-permute-start.5
  174.0 22.2 %collective-permute-done.4.upb = bf16[3,608,128]{2,1,0:T(8,128)(2,1)S(1)} collective-permute-done((bf16[3,608,128]{2,1,0:T(8,128)(2,1)S(1)}, bf16[3,608,128]{2,1,0:T(8,128)(2,1)S(1)}, u32[]{:S(2)}, u32[]{:S(2)}) %collective-permute-start.4) | collective-permute-done | bytes 466976 | tf_op jit(solution)/shard_map/ppermute | solution.py:395
  196.2 0.0 collective-permute-done.5.dnb
  196.2 0.8 copy-done.2
  197.0 0.2 copy-done.3
  197.2 17.2 %shard_map.72 = (bf16[64,128,128]{2,1,0:T(8,128)(2,1)}, bf16[64,128,128]{2,1,0:T(8,128)(2,1)}) custom-call(s32[3]{0:T(128)} %pad_add_fusion.meta, bf16[16,608,128]{2,1,0:T(8,128)(2,1)} %get-tuple-element.30.fx, bf16[16,608,128]{2,1,0:T(8,128)(2,1)} %get-tuple-element.31.gx, bf16[16,608,128]{2,1,0:T(8,128)(2,1)} %get-tuple-element.32.a1i, ...), custom_call_target="tpu_custom_call" | custom-call | flops 4831838208 | bytes 25165824 | tf_op jit(solution)/shard_map/pallas_call | solution.py:512
  214.4 0.0 all-to-all-done.1
  214.5 1.1 convert.1
  (8 shorter events, 0.0 us)
Async XLA Ops:
  7.4 6.9 %collective-permute-start = (bf16[2,16,48,128]{3,2,1,0:T(8,128)(2,1)}, bf16[2,16,48,128]{3,2,1,0:T(8,128)(2,1)S(1)}, u32[]{:S(2)}, u32[]{:S(2)}) collective-permute-start(bf16[2,16,48,128]{3,2,1,0:T(8,128)(2,1)} %get-tuple-element.28), channel_id=1, source_target_pairs={{0,1},{1,2},{2,3},{4,5},{5,6},{6,7},{8,9},{9,10},{10,11},{12,13},{... | collective-permute-start | bytes 1179656 | tf_op jit(solution)/shard_map/ppermute | solution.py:395
  9.8 5.9 %collective-permute-start.1 = (bf16[2,16,48,128]{3,2,1,0:T(8,128)(2,1)}, bf16[2,16,48,128]{3,2,1,0:T(8,128)(2,1)S(1)}, u32[]{:S(2)}, u32[]{:S(2)}) collective-permute-start(bf16[2,16,48,128]{3,2,1,0:T(8,128)(2,1)} %get-tuple-element.29), channel_id=1, source_target_pairs={{1,0},{2,1},{3,2},{5,4},{6,5},{7,6},{9,8},{10,9},{11,10},{13,12},{... | collective-permute-start | bytes 1179656 | tf_op jit(solution)/shard_map/ppermute | solution.py:395
  14.4 1.4 copy-start.4
  15.8 0.7 copy-start.5
  99.2 24.2 %collective-permute-start.2 = (bf16[3,608,128]{2,1,0:T(8,128)(2,1)}, bf16[3,608,128]{2,1,0:T(8,128)(2,1)S(1)}, u32[]{:S(2)}, u32[]{:S(2)}) collective-permute-start(bf16[3,608,128]{2,1,0:T(8,128)(2,1)} %get-tuple-element.33), channel_id=1, source_target_pairs={{0,4},{4,8},{8,12},{12,16},{16,20},{20,24},{24,28},{1,5},{5,9},{9,... | collective-permute-start | bytes 1400840 | tf_op jit(solution)/shard_map/ppermute | solution.py:395
  102.7 20.7 %collective-permute-start.3 = (bf16[3,608,128]{2,1,0:T(8,128)(2,1)}, bf16[3,608,128]{2,1,0:T(8,128)(2,1)S(1)}, u32[]{:S(2)}, u32[]{:S(2)}) collective-permute-start(bf16[3,608,128]{2,1,0:T(8,128)(2,1)} %get-tuple-element.34), channel_id=1, source_target_pairs={{4,0},{8,4},{12,8},{16,12},{20,16},{24,20},{28,24},{5,1},{9,5},{13... | collective-permute-start | bytes 1400840 | tf_op jit(solution)/shard_map/ppermute | solution.py:395
  123.4 0.8 copy-start
  123.4 1.0 copy-start.1
  135.3 33.5 %copy-start.7 = (bf16[3,608,128]{2,1,0:T(8,128)(2,1)S(1)}, bf16[3,608,128]{2,1,0:T(8,128)(2,1)}, u32[]{:S(2)}) copy-start(bf16[3,608,128]{2,1,0:T(8,128)(2,1)} %get-tuple-element.35) | copy-start | bytes 1400836
  135.3 37.2 %copy-start.6 = (bf16[3,608,128]{2,1,0:T(8,128)(2,1)S(1)}, bf16[3,608,128]{2,1,0:T(8,128)(2,1)}, u32[]{:S(2)}) copy-start(bf16[3,608,128]{2,1,0:T(8,128)(2,1)} %get-tuple-element.36) | copy-start | bytes 1400836
  165.5 49.0 %all-to-all-start.1 = ((bf16[32,72,128]{2,1,0:T(8,128)(2,1)}), bf16[32,72,128]{2,1,0:T(8,128)(2,1)S(1)}, u32[]{:S(2)}, u32[]{:S(2)}) async-start(bf16[32,72,128]{2,1,0:T(8,128)(2,1)} %shard_map.73), calls=%async_computation.1 | async-start | bytes 1179648 | tf_op jit(solution)/shard_map/all_to_all | solution.py:509
  168.8 27.4 %collective-permute-start.4 = (bf16[3,608,128]{2,1,0:T(8,128)(2,1)S(1)}, bf16[3,608,128]{2,1,0:T(8,128)(2,1)S(1)}, u32[]{:S(2)}, u32[]{:S(2)}) collective-permute-start(bf16[3,608,128]{2,1,0:T(8,128)(2,1)S(1)} %copy-done.7), channel_id=1, source_target_pairs={{0,4},{4,8},{8,12},{12,16},{16,20},{20,24},{24,28},{1,5},{5,9},{9,... | collective-permute-start | bytes 1400840 | tf_op jit(solution)/shard_map/ppermute | solution.py:395
  172.5 23.7 %collective-permute-start.5 = (bf16[3,608,128]{2,1,0:T(8,128)(2,1)S(1)}, bf16[3,608,128]{2,1,0:T(8,128)(2,1)S(1)}, u32[]{:S(2)}, u32[]{:S(2)}) collective-permute-start(bf16[3,608,128]{2,1,0:T(8,128)(2,1)S(1)} %copy-done.6), channel_id=1, source_target_pairs={{4,0},{8,4},{12,8},{16,12},{20,16},{24,20},{28,24},{5,1},{9,5},{13... | collective-permute-start | bytes 1400840 | tf_op jit(solution)/shard_map/ppermute | solution.py:395
  196.2 0.8 copy-start.2
  196.2 1.0 copy-start.3
where the time goes:
time: 218 us; the launch traced here: 216 us
  Pallas kernels  141 us (65%)
  blocking collectives  28.1 us (13%)
  waiting for transfers between devices  23.6 us (11%)
  starting transfers between devices  16.8 us (8%)
  local copies, waits for them, and re-layouts  2.74 us (1%)
    pallas_call x1, Pallas kernels, body(): pl.pallas_call(functools.partial(assemble_kernel, na=na, nj=nj), in_specs...  82.7 us
    all_to_all x1, blocking collectives, body(): shares = lax.all_to_all(kg.reshape(parts, -1, C), axes, 0, 0, tiled=True)  28.1 us
    ppermute x6, waiting for transfers between devices, shift(): lax.ppermute(x, axis, [(i, i + step) for i in range(n) if 0 <= i + step <...  23.6 us
    pallas_call x1, Pallas kernels, body(): pl.pallas_call(functools.partial(inner_kernel, na=na, nj=nj), in_specs=[S...  19.4 us
    pallas_call x1, Pallas kernels, body(): pl.pallas_call(functools.partial(last_kernel, na=na, nj=nj), in_specs=[SM...  17.2 us
    ppermute x6, starting transfers between devices, shift(): lax.ppermute(x, axis, [(i, i + step) for i in range(n) if 0 <= i + step <...  13.5 us
    pallas_call x1, Pallas kernels, body(): pl.pallas_call(functools.partial(edge_kernel, na=na, nj=nj), in_specs=[SM...  10.9 us
    pallas_call x1, Pallas kernels, body(): pl.pallas_call(functools.partial(layout_kernel, step=step, nj=nj), grid=(...  5.51 us
  transfers between devices with their start and end apart: 7, of which 2 were waited for; matrix products, arithmetic and copies ran while one was open for 0% of the time, Pallas kernels for 19%

commit v1 on v0

--- a/solution.py
+++ b/solution.py
@@ -120,43 +120,60 @@
         rm = (meta[0] + 4 * (base + k) + (s1 >> 2) < meta[2]).astype(F32)
         gb = (gb.reshape(nj, 16, C) * (cm * rm)).reshape(m0, C).astype(BF16)
         for n, (v, x_ref) in enumerate(((fb, fx_ref), (gb, gx_ref))):
-            x_ref[k, 16 * H : 16 * H + m0] = v
+            x_ref[k] = v
             left_ref[n, k] = v[: 16 * H]
             right_ref[n, k] = v[m0 - 16 * H :]
 
 
-def assemble_kernel(fx_in, gx_in, lh, rh, fx, gx, ua, ub, da, db, sem, *, na, nj):
-    del fx_in, gx_in
-    m0 = 16 * nj
-    jobs = []
-
+def gather_rows(go, own, lh, rh, n, row, count, dst, m0):
+    go(own.at[pl.ds(row, count)], dst.at[:, pl.ds(16 * H, m0)])
+    go(lh.at[n, pl.ds(row, count)], dst.at[:, pl.ds(0, 16 * H)])
+    go(rh.at[n, pl.ds(row, count)], dst.at[:, pl.ds(16 * H + m0, 16 * H)])
+
+
+def copier(sem, jobs):
     def go(src, dst):
         c = pltpu.make_async_copy(src, dst, sem.at[len(jobs)])
         c.start()
         jobs.append(c)
 
-    for n, x in enumerate((fx, gx)):
-        go(lh.at[n], x.at[:, pl.ds(0, 16 * H)])
-        go(rh.at[n], x.at[:, pl.ds(16 * H + m0, 16 * H)])
-    for c in jobs:
-        c.wait()
+    return go
+
+
+def assemble_kernel(fo, xo, lh, rh, ua, ub, da, db, buf, sem, *, na, nj):
+    m0 = 16 * nj
+    jobs = []
+    go = copier(sem, jobs)
+    gather_rows(go, fo, lh, rh, 0, 0, 1, buf.at[0, pl.ds(0, 1)], m0)
+    gather_rows(go, xo, lh, rh, 1, 0, 2, buf.at[0, pl.ds(1, 2)], m0)
+    gather_rows(go, fo, lh, rh, 0, na - 1, 1, buf.at[1, pl.ds(0, 1)], m0)
+    gather_rows(go, xo, lh, rh, 1, na - 2, 2, buf.at[1, pl.ds(1, 2)], m0)
+    gather_rows(go, fo, lh, rh, 0, 1, 2, buf.at[2, pl.ds(0, 2)], m0)
+    gather_rows(go, xo, lh, rh, 1, 2, 1, buf.at[2, pl.ds(2, 1)], m0)
+    gather_rows(go, fo, lh, rh, 0, na - 3, 2, buf.at[3, pl.ds(0, 2)], m0)
+    gather_rows(go, xo, lh, rh, 1, na - 3, 1, buf.at[3, pl.ds(2, 1)], m0)
     first = len(jobs)
-    go(fx.at[pl.ds(0, 1)], ua.at[pl.ds(0, 1)])
-    go(gx.at[pl.ds(0, 2)], ua.at[pl.ds(1, 2)])
-    go(fx.at[pl.ds(1, 2)], ub.at[pl.ds(0, 2)])
-    go(gx.at[pl.ds(2, 1)], ub.at[pl.ds(2, 1)])
-    go(fx.at[pl.ds(na - 1, 1)], da.at[pl.ds(0, 1)])
-    go(gx.at[pl.ds(na - 2, 2)], da.at[pl.ds(1, 2)])
-    go(fx.at[pl.ds(na - 3, 2)], db.at[pl.ds(0, 2)])
-    go(gx.at[pl.ds(na - 3, 1)], db.at[pl.ds(2, 1)])
+    for i, out in enumerate((ua, da, ub, db)):
+        for c in jobs[6 * i : 6 * i + 6]:
+            c.wait()
+        go(buf.at[i], out)
     for c in jobs[first:]:
         c.wait()
 
 
-def inner_kernel(meta, fx, gx, wp, a1o, a2o, so, g1o, gfo, acc_o, a1, a2, st, es, g1, gf, cm, sem, *, na, nj):
+def inner_kernel(
+    meta, fo, xo, lh, rh, wp, a1o, a2o, so, g1o, gfo, acc_o,
+    fx, gx, a1, a2, st, es, g1, gf, cm, sem, insem, *, na, nj,
+):
     m0, m1, m2, w = 16 * nj, 16 * (nj + 2), 16 * (nj + 4), 16 * (nj + 6)
     ni = na - 4
+    jobs = []
+    go = copier(insem, jobs)
+    gather_rows(go, fo, lh, rh, 0, 0, na, fx, m0)
+    gather_rows(go, xo, lh, rh, 1, 0, na, gx, m0)
     cm[...] = column_mask(meta, nj)
+    for c in jobs[:3]:
+        c.wait()
 
     def activate(a, _):
         v, _e = elu_parts(fx[a].astype(F32))
@@ -166,6 +183,8 @@
     lax.fori_loop(0, na, activate, 0)
     out_a1 = pltpu.make_async_copy(a1, a1o, sem.at[0])
     out_a1.start()
+    for c in jobs[3:]:
+        c.wait()
 
     def quad(t, _):
         r = 2 + 4 * t
@@ -225,27 +244,23 @@
 
 
 def edge_kernel(
-    meta, fx, gx, a1i, up, dn, wp, acc_i, _a2, _s, _g1, _gf, a2o, so, g1o, gfo, kg,
+    meta, fo, xo, lh, rh, a1i, up, dn, wp, acc_i, _a2, _s, _g1, _gf, a2o, so, g1o, gfo, kg,
     a1, g, f, fh, a2, st, es, g1, gf, cm, sem, *, na, nj,
 ):
     m0, m1, m2, w = 16 * nj, 16 * (nj + 2), 16 * (nj + 4), 16 * (nj + 6)
     jobs = []
 
-    def go(src, dst):
-        c = pltpu.make_async_copy(src, dst, sem.at[len(jobs)])
-        c.start()
-        jobs.append(c)
-
+    go = copier(sem, jobs)
     go(up.at[pl.ds(0, 1)], fh.at[0])
     go(dn.at[pl.ds(0, 1)], fh.at[1])
     go(up.at[pl.ds(1, 2)], g.at[0, pl.ds(0, 2)])
-    go(gx.at[pl.ds(0, 6)], g.at[0, pl.ds(2, 6)])
-    go(gx.at[pl.ds(na - 6, 6)], g.at[1, pl.ds(0, 6)])
+    gather_rows(go, xo, lh, rh, 1, 0, 6, g.at[0, pl.ds(2, 6)], m0)
+    gather_rows(go, xo, lh, rh, 1, na - 6, 6, g.at[1, pl.ds(0, 6)], m0)
     go(dn.at[pl.ds(1, 2)], g.at[1, pl.ds(6, 2)])
     go(a1i.at[pl.ds(0, 3)], a1.at[0, pl.ds(1, 3)])
     go(a1i.at[pl.ds(na - 3, 3)], a1.at[1, pl.ds(0, 3)])
-    go(fx.at[pl.ds(0, 2)], f.at[0])
-    go(fx.at[pl.ds(na - 2, 2)], f.at[1])
+    gather_rows(go, fo, lh, rh, 0, 0, 2, f.at[0], m0)
+    gather_rows(go, fo, lh, rh, 0, na - 2, 2, f.at[1], m0)
     cm[...] = column_mask(meta, nj)
     for c in jobs:
         c.wait()
@@ -301,27 +316,23 @@
 
 
 def last_kernel(
-    meta, fx, gx, a1i, upa, dna, upb, dnb, wp, a2i, si, g1i, gfi, out, fg,
+    meta, fo, xo, lh, rh, a1i, upa, dna, upb, dnb, wp, a2i, si, g1i, gfi, out, fg,
     a1, g, f, fm, a2, st, es, g1, gf, cm, ot, ft, sem, osem, *, na, nj,
 ):
     m0, m1, m2, w = 16 * nj, 16 * (nj + 2), 16 * (nj + 4), 16 * (nj + 6)
     jobs = []
 
-    def go(src, dst):
-        c = pltpu.make_async_copy(src, dst, sem.at[len(jobs)])
-        c.start()
-        jobs.append(c)
-
+    go = copier(sem, jobs)
     go(upb.at[pl.ds(0, 2)], f.at[0, pl.ds(0, 2)])
     go(upa.at[pl.ds(0, 1)], f.at[0, pl.ds(2, 1)])
     go(dna.at[pl.ds(0, 1)], f.at[1, pl.ds(0, 1)])
     go(dnb.at[pl.ds(0, 2)], f.at[1, pl.ds(1, 2)])
     go(upb.at[pl.ds(2, 1)], g.at[0, pl.ds(0, 1)])
     go(upa.at[pl.ds(2, 1)], g.at[0, pl.ds(1, 1)])
-    go(gx.at[pl.ds(1, 1)], g.at[0, pl.ds(2, 1)])
-    go(gx.at[pl.ds(3, 1)], g.at[0, pl.ds(3, 1)])
-    go(gx.at[pl.ds(na - 4, 1)], g.at[1, pl.ds(0, 1)])
-    go(gx.at[pl.ds(na - 2, 1)], g.at[1, pl.ds(1, 1)])
+    gather_rows(go, xo, lh, rh, 1, 1, 1, g.at[0, pl.ds(2, 1)], m0)
+    gather_rows(go, xo, lh, rh, 1, 3, 1, g.at[0, pl.ds(3, 1)], m0)
+    gather_rows(go, xo, lh, rh, 1, na - 4, 1, g.at[1, pl.ds(0, 1)], m0)
+    gather_rows(go, xo, lh, rh, 1, na - 2, 1, g.at[1, pl.ds(1, 1)], m0)
     go(dna.at[pl.ds(1, 1)], g.at[1, pl.ds(2, 1)])
     go(dnb.at[pl.ds(2, 1)], g.at[1, pl.ds(3, 1)])
     go(a1i.at[pl.ds(0, 1)], a1.at[0, pl.ds(3, 1)])
@@ -330,7 +341,7 @@
     go(a2i.at[pl.ds(2, na)], a2.at[pl.ds(2, na)])
     go(si, st)
     go(g1i.at[pl.ds(1, na)], g1.at[pl.ds(1, na)])
-    go(fx.at[:, pl.ds(16 * H, m0)], fm)
+    go(fo, fm)
     go(gfi, gf)
     cm[...] = column_mask(meta, nj)
     for c in jobs[:early]:
@@ -385,7 +396,7 @@
     pltpu.make_async_copy(ft, fg, osem.at[1]).wait()
 
 
-def sum_kernel(meta, x_ref, o_ref):
+def sum_kernel(meta, x_ref, _up, _dn, o_ref):
     total = jnp.sum(x_ref[...].astype(F32), axis=0) / meta[2].astype(F32)
     o_ref[...] = jnp.broadcast_to(total.astype(BF16)[None], o_ref.shape)
 
@@ -408,9 +419,9 @@
         functools.partial(layout_kernel, step=step, nj=nj),
         grid=(na // step,),
         in_specs=[SMEM] + [pl.BlockSpec((4 * step, cols, C), lambda i: (i, 0, 0))] * 2,
-        out_specs=[pl.BlockSpec((step, w, C), lambda i: (i, 0, 0))] * 2
+        out_specs=[pl.BlockSpec((step, m0, C), lambda i: (i, 0, 0))] * 2
         + [pl.BlockSpec((2, step, 16 * H, C), lambda i: (0, i, 0, 0))] * 2,
-        out_shape=[sds((na, w, C), BF16)] * 2 + [sds((2, na, 16 * H, C), BF16)] * 2,
+        out_shape=[sds((na, m0, C), BF16)] * 2 + [sds((2, na, 16 * H, C), BF16)] * 2,
         compiler_params=params(),
         cost_estimate=cost(0, 16 << 20),
     )(meta, features, cotangent)
@@ -424,13 +435,12 @@
         compiler_params=params(),
         cost_estimate=cost(0, 8 << 20),
     )(kernels)
-    fx, gx, ua, ub, da, db = pl.pallas_call(
+    ua, ub, da, db = pl.pallas_call(
         functools.partial(assemble_kernel, na=na, nj=nj),
         in_specs=[ANY] * 4,
-        out_specs=[ANY] * 6,
-        out_shape=[sds((na, w, C), BF16)] * 2 + [sds((3, w, C), BF16)] * 4,
-        scratch_shapes=[pltpu.SemaphoreType.DMA((12,))],
-        input_output_aliases={0: 0, 1: 1},
+        out_specs=[ANY] * 4,
+        out_shape=[sds((3, w, C), BF16)] * 4,
+        scratch_shapes=[pltpu.VMEM((4, 3, w, C), BF16), pltpu.SemaphoreType.DMA((28,))],
         compiler_params=params(),
         cost_estimate=cost(0, 4 << 20),
     )(fx, gx, lh, rh)
@@ -442,7 +452,7 @@
     conv_flops = 2 * rows * cols * 9 * C * C
     a1, a2, st, g1, gf, acc = pl.pallas_call(
         functools.partial(inner_kernel, na=na, nj=nj),
-        in_specs=[SMEM] + [VMEM] * 3,
+        in_specs=[SMEM] + [ANY] * 4 + [VMEM],
         out_specs=[ANY] * 5 + [VMEM],
         out_shape=[
             sds((na, w, C), BF16),
@@ -454,6 +464,8 @@
         ],
         scratch_shapes=[
             pltpu.VMEM((na, w, C), BF16),
+            pltpu.VMEM((na, w, C), BF16),
+            pltpu.VMEM((na, w, C), BF16),
             pltpu.VMEM((na + 4, m2, C), BF16),
             pltpu.VMEM((ni, m0, C), F32),
             pltpu.VMEM((ni, m1, C), F32),
@@ -461,14 +473,15 @@
             pltpu.VMEM((ni, m0, C), F32),
             pltpu.VMEM((w, C), F32),
             pltpu.SemaphoreType.DMA((5,)),
+            pltpu.SemaphoreType.DMA((6,)),
         ],
         compiler_params=params(),
         cost_estimate=cost(4 * conv_flops, 24 << 20),
-    )(meta, fx, gx, wp)
+    )(meta, fx, gx, lh, rh, wp)
 
     a2, st, g1, gf, kg = pl.pallas_call(
         functools.partial(edge_kernel, na=na, nj=nj),
-        in_specs=[SMEM] + [ANY] * 5 + [VMEM] * 2 + [ANY] * 4,
+        in_specs=[SMEM] + [ANY] * 7 + [VMEM] * 2 + [ANY] * 4,
         out_specs=[ANY] * 4 + [VMEM],
         out_shape=[
             sds((na + 4, m2, C), BF16),
@@ -488,30 +501,30 @@
             pltpu.VMEM((2, 2, m1, C), BF16),
             pltpu.VMEM((2, 2, m0, C), F32),
             pltpu.VMEM((w, C), F32),
-            pltpu.SemaphoreType.DMA((18,)),
+            pltpu.SemaphoreType.DMA((26,)),
         ],
-        input_output_aliases={8: 0, 9: 1, 10: 2, 11: 3},
+        input_output_aliases={10: 0, 11: 1, 12: 2, 13: 3},
         compiler_params=params(),
         cost_estimate=cost(conv_flops, 12 << 20),
-    )(meta, fx, gx, a1, upa, dna, wp, acc, a2, st, g1, gf)
+    )(meta, fx, gx, lh, rh, a1, upa, dna, wp, acc, a2, st, g1, gf)
 
     axes = ("row", "col")
     parts = lax.axis_size(axes)
     shares = lax.all_to_all(kg.reshape(parts, -1, C), axes, 0, 0, tiled=True)
     spread = pl.pallas_call(
         sum_kernel,
-        in_specs=[SMEM, VMEM],
+        in_specs=[SMEM, VMEM, ANY, ANY],
         out_specs=VMEM,
         out_shape=sds(shares.shape, BF16),
         compiler_params=params(),
         cost_estimate=cost(0, 2 << 20),
-    )(meta, shares)
+    )(meta, shares, upb, dnb)
     whole = lax.all_to_all(spread, axes, 0, 0, tiled=True)
     kernel_gradient = whole.reshape(kernels.shape).astype(F32)
 
     out, fg = pl.pallas_call(
         functools.partial(last_kernel, na=na, nj=nj),
-        in_specs=[SMEM] + [ANY] * 7 + [VMEM] + [ANY] * 4,
+        in_specs=[SMEM] + [ANY] * 9 + [VMEM] + [ANY] * 4,
         out_specs=[ANY] * 2,
         out_shape=[sds(features.shape, BF16)] * 2,
         scratch_shapes=[
@@ -527,12 +540,12 @@
             pltpu.VMEM((w, C), F32),
             pltpu.VMEM(features.shape, BF16),
             pltpu.VMEM(features.shape, BF16),
-            pltpu.SemaphoreType.DMA((19,)),
+            pltpu.SemaphoreType.DMA((27,)),
             pltpu.SemaphoreType.DMA((2,)),
         ],
         compiler_params=params(),
         cost_estimate=cost(2 * conv_flops, 24 << 20),
-    )(meta, fx, gx, a1, upa, dna, upb, dnb, wp, a2, st, g1, gf)
+    )(meta, fx, gx, lh, rh, a1, upa, dna, upb, dnb, wp, a2, st, g1, gf)
     return out, fg, kernel_gradient
 
 

time: 218 us -> 124 us (0.57); the launches traced: 216 us -> 124 us
  Pallas kernels: 141 us -> 61.1 us
  blocking collectives: 28.1 us -> 0 us
  starting transfers between devices: 16.8 us -> 32.2 us
    pallas_call x1, Pallas kernels: 82.7 us -> 2.57 us  [body(): pl.pallas_call(functools.partial(assemble_kernel, na=na, nj=nj), in_specs...]
    all_to_all x1 -> x0, blocking collectives: 28.1 us -> none  [body(): shares = lax.all_to_all(kg.reshape(parts, -1, C), axes, 0, 0, tiled=True)]
    all_to_all x0 -> x1, starting transfers between devices: none -> 11.3 us  [body(): shares = lax.all_to_all(kg.reshape(parts, -1, C), axes, 0, 0, tiled=True)]
    all_to_all x1, starting transfers between devices: 3.29 us -> 7.49 us  [body(): whole = lax.all_to_all(spread, axes, 0, 0, tiled=True)]
  transfers between devices with their start and end apart: 7 -> 8, of which waited for: 2 -> 2; matrix products, arithmetic and copies ran while one was open for 0% -> 0% of each run, Pallas kernels for 19% -> 32%
where the time goes in v1:
time: 124 us
  Pallas kernels  61.1 us (49%)
  starting transfers between devices  32.2 us (26%)
  waiting for transfers between devices  23.8 us (19%)
  local copies, waits for them, and re-layouts  3.6 us (3%)
  other arithmetic  1.75 us (1%)
  between operations  1.45 us (1%)
    ppermute x6, waiting for transfers between devices, shift(): lax.ppermute(x, axis, [(i, i + step) for i in range(n) if 0 <= i + step <...  23.8 us
    pallas_call x1, Pallas kernels, body(): pl.pallas_call(functools.partial(inner_kernel, na=na, nj=nj), in_specs=[S...  19.5 us
    pallas_call x1, Pallas kernels, body(): pl.pallas_call(functools.partial(last_kernel, na=na, nj=nj), in_specs=[SM...  17.3 us
    ppermute x6, starting transfers between devices, shift(): lax.ppermute(x, axis, [(i, i + step) for i in range(n) if 0 <= i + step <...  13.4 us
    all_to_all x1, starting transfers between devices, body(): shares = lax.all_to_all(kg.reshape(parts, -1, C), axes, 0, 0, tiled=True)  11.3 us
    pallas_call x1, Pallas kernels, body(): pl.pallas_call(functools.partial(edge_kernel, na=na, nj=nj), in_specs=[SM...  11.1 us
    all_to_all x1, starting transfers between devices, body(): whole = lax.all_to_all(spread, axes, 0, 0, tiled=True)  7.49 us
    pallas_call x1, Pallas kernels, body(): pl.pallas_call(functools.partial(layout_kernel, step=step, nj=nj), grid=(...  5.33 us
  transfers between devices with their start and end apart: 8, of which 2 were waited for; matrix products, arithmetic and copies ran while one was open for 0% of the time, Pallas kernels for 32%

profile of v1, /device:TPU:0, one launch (start us, length us, event | category | flops | bytes accessed | tf_op | source)
XLA Modules:
  0.0 123.8 jit_solution(8878561313014123194)
XLA Ops:
  1.3 0.6 pad_add_fusion.meta
  1.9 5.3 %shard_map.67 = (bf16[16,512,128]{2,1,0:T(8,128)(2,1)}, bf16[16,512,128]{2,1,0:T(8,128)(2,1)}, bf16[2,16,48,128]{3,2,1,0:T(8,128)(2,1)}, bf16[2,16,48,128]{3,2,1,0:T(8,128)(2,1)}) custom-call(s32[3]{0:T(128)} %pad_add_fusion.meta, bf16[64,128,128]{2,1,0:T(8,128)(2,1)} %f_ref.1, bf16[64,128,128]{2,1,0:T(8,128)(2,1)} %g_ref.1), custom_call_target="tpu_custom_call" | custom-call | bytes 16777216 | tf_op jit(solution)/shard_map/pallas_call | solution.py:418
  7.2 2.4 %collective-permute-start = (bf16[2,16,48,128]{3,2,1,0:T(8,128)(2,1)}, bf16[2,16,48,128]{3,2,1,0:T(8,128)(2,1)S(1)}, u32[]{:S(2)}, u32[]{:S(2)}) collective-permute-start(bf16[2,16,48,128]{3,2,1,0:T(8,128)(2,1)} %get-tuple-element.26), channel_id=1, source_target_pairs={{0,1},{1,2},{2,3},{4,5},{5,6},{6,7},{8,9},{9,10},{10,11},{12,13},{... | collective-permute-start | bytes 1179656 | tf_op jit(solution)/shard_map/ppermute | solution.py:406
  9.6 1.3 %collective-permute-start.1 = (bf16[2,16,48,128]{3,2,1,0:T(8,128)(2,1)}, bf16[2,16,48,128]{3,2,1,0:T(8,128)(2,1)S(1)}, u32[]{:S(2)}, u32[]{:S(2)}) collective-permute-start(bf16[2,16,48,128]{3,2,1,0:T(8,128)(2,1)} %get-tuple-element.27), channel_id=1, source_target_pairs={{1,0},{2,1},{3,2},{5,4},{6,5},{7,6},{9,8},{10,9},{11,10},{13,12},{... | collective-permute-start | bytes 1179656 | tf_op jit(solution)/shard_map/ppermute | solution.py:406
  10.9 3.2 %shard_map.68.wp = bf16[4,1536,256]{2,1,0:T(8,128)(2,1)} custom-call(bf16[2,3,3,128,128]{4,3,2,1,0:T(8,128)(2,1)} %k_ref.1), custom_call_target="tpu_custom_call" | custom-call | bytes 8388608 | tf_op jit(solution)/shard_map/pallas_call | solution.py:430
  14.1 0.0 collective-permute-done.lh
  14.1 1.4 %collective-permute-done.1.rh = bf16[2,16,48,128]{3,2,1,0:T(8,128)(2,1)S(1)} collective-permute-done((bf16[2,16,48,128]{3,2,1,0:T(8,128)(2,1)}, bf16[2,16,48,128]{3,2,1,0:T(8,128)(2,1)S(1)}, u32[]{:S(2)}, u32[]{:S(2)}) %collective-permute-start.1) | collective-permute-done | bytes 393248 | tf_op jit(solution)/shard_map/ppermute | solution.py:406
  15.5 0.7 copy-done.1
  16.3 2.6 %shard_map.70 = (bf16[3,608,128]{2,1,0:T(8,128)(2,1)}, bf16[3,608,128]{2,1,0:T(8,128)(2,1)}, bf16[3,608,128]{2,1,0:T(8,128)(2,1)}, bf16[3,608,128]{2,1,0:T(8,128)(2,1)}) custom-call(bf16[16,512,128]{2,1,0:T(8,128)(2,1)} %get-tuple-element.24.fo, bf16[16,512,128]{2,1,0:T(8,128)(2,1)} %get-tuple-element.25.xo, bf16[2,16,48,128]{3,2,1,0:T(8,128)(2,1)} %copy-done, ...), custom_call_target="tpu_custom_call" | custom-call | bytes 4194304 | tf_op jit(solution)/shard_map/pallas_call | solution.py:438
  18.9 3.4 %collective-permute-start.2 = (bf16[3,608,128]{2,1,0:T(8,128)(2,1)}, bf16[3,608,128]{2,1,0:T(8,128)(2,1)S(1)}, u32[]{:S(2)}, u32[]{:S(2)}) collective-permute-start(bf16[3,608,128]{2,1,0:T(8,128)(2,1)} %get-tuple-element.29), channel_id=1, source_target_pairs={{0,4},{4,8},{8,12},{12,16},{16,20},{20,24},{24,28},{1,5},{5,9},{9,... | collective-permute-start | bytes 1400840 | tf_op jit(solution)/shard_map/ppermute | solution.py:406
  22.3 1.3 %collective-permute-start.3 = (bf16[3,608,128]{2,1,0:T(8,128)(2,1)}, bf16[3,608,128]{2,1,0:T(8,128)(2,1)S(1)}, u32[]{:S(2)}, u32[]{:S(2)}) collective-permute-start(bf16[3,608,128]{2,1,0:T(8,128)(2,1)} %get-tuple-element.30), channel_id=1, source_target_pairs={{4,0},{8,4},{12,8},{16,12},{20,16},{24,20},{28,24},{5,1},{9,5},{13... | collective-permute-start | bytes 1400840 | tf_op jit(solution)/shard_map/ppermute | solution.py:406
  23.6 19.5 %shard_map.69 = (bf16[16,608,128]{2,1,0:T(8,128)(2,1)}, bf16[20,576,128]{2,1,0:T(8,128)(2,1)}, f32[16,512,128]{2,1,0:T(8,128)}, bf16[18,544,128]{2,1,0:T(8,128)(...) custom-call(s32[3]{0:T(128)} %pad_add_fusion.meta, bf16[16,512,128]{2,1,0:T(8,128)(2,1)} %get-tuple-element.24.fo, ...), custom_call_target="tpu_custom_call" | custom-call | flops 9663676416 | bytes 25165824 | tf_op jit(solution)/shard_map/pallas_call | solution.py:453
  43.1 0.0 collective-permute-done.2.up.upa
  43.1 0.0 collective-permute-done.3.dn.dna
  43.1 0.0 copy-start.6
  43.1 0.8 copy-done.5
  43.9 0.3 copy-done.6
  44.2 11.1 %shard_map.71 = (bf16[20,576,128]{2,1,0:T(8,128)(2,1)}, f32[16,512,128]{2,1,0:T(8,128)}, bf16[18,544,128]{2,1,0:T(8,128)(2,1)}, f32[16,512,128]{2,1,0:T(8,128)}, bf16[2,3,3,128,128]{4,3,2,1,0:T(8,128)(2,1)}) custom-call(s32[3]{0:T(128)} %pad_add_fusion.meta, ...), custom_call_target="tpu_custom_call", output_to_operand_aliasing={{0}: (10, {}), {1}: (11, {}), {2}: (12, {}), {3}: (13, {})} | custom-call | flops 2415919104 | bytes 12582912 | tf_op jit(solution)/shard_map/pallas_call | solution.py:482
  55.3 11.3 %all-to-all-start = ((bf16[32,72,128]{2,1,0:T(8,128)(2,1)}), bf16[32,72,128]{2,1,0:T(8,128)(2,1)S(1)}, u32[]{:S(2)}, u32[]{:S(2)}) async-start(bf16[32,72,128]{2,1,0:T(8,128)(2,1)} %bitcast.6), calls=%async_computation | async-start | bytes 1179648 | tf_op jit(solution)/shard_map/all_to_all | solution.py:513
  66.6 3.7 %collective-permute-start.4 = (bf16[3,608,128]{2,1,0:T(8,128)(2,1)S(1)}, bf16[3,608,128]{2,1,0:T(8,128)(2,1)S(1)}, u32[]{:S(2)}, u32[]{:S(2)}) collective-permute-start(bf16[3,608,128]{2,1,0:T(8,128)(2,1)S(1)} %copy-done.8), channel_id=1, source_target_pairs={{0,4},{4,8},{8,12},{12,16},{16,20},{20,24},{24,28},{1,5},{5,9},{9,... | collective-permute-start | bytes 1400840 | tf_op jit(solution)/shard_map/ppermute | solution.py:406
  70.3 1.3 %collective-permute-start.5 = (bf16[3,608,128]{2,1,0:T(8,128)(2,1)S(1)}, bf16[3,608,128]{2,1,0:T(8,128)(2,1)S(1)}, u32[]{:S(2)}, u32[]{:S(2)}) collective-permute-start(bf16[3,608,128]{2,1,0:T(8,128)(2,1)S(1)} %copy-done.7), channel_id=1, source_target_pairs={{4,0},{8,4},{12,8},{16,12},{20,16},{24,20},{28,24},{5,1},{9,5},{13... | collective-permute-start | bytes 1400840 | tf_op jit(solution)/shard_map/ppermute | solution.py:406
  71.6 22.4 %collective-permute-done.4.upb._up = bf16[3,608,128]{2,1,0:T(8,128)(2,1)S(1)} collective-permute-done((bf16[3,608,128]{2,1,0:T(8,128)(2,1)S(1)}, bf16[3,608,128]{2,1,0:T(8,128)(2,1)S(1)}, u32[]{:S(2)}, u32[]{:S(2)}) %collective-permute-start.4) | collective-permute-done | bytes 466976 | tf_op jit(solution)/shard_map/ppermute | solution.py:406
  94.0 0.0 collective-permute-done.5.dnb._dn
  94.0 0.0 all-to-all-done.x_ref
  94.0 0.8 copy-done.3
  94.8 0.2 copy-done.4
  95.0 0.8 copy-done.2
  95.8 2.0 %shard_map.73 = bf16[32,72,128]{2,1,0:T(8,128)(2,1)} custom-call(s32[3]{0:T(128)} %pad_add_fusion.meta, bf16[32,72,128]{2,1,0:T(8,128)(2,1)} %copy-done.2, bf16[3,608,128]{2,1,0:T(8,128)(2,1)} %copy-done.3, bf16[3,608,128]{2,1,0:T(8,128)(2,1)} %copy-done.4), custom_call_target="tpu_custom_call" | custom-call | bytes 2097152 | tf_op jit(solution)/shard_map/pallas_call | solution.py:514
  97.8 7.5 %all-to-all-start.1 = ((bf16[32,72,128]{2,1,0:T(8,128)(2,1)}), bf16[32,72,128]{2,1,0:T(8,128)(2,1)S(1)}, u32[]{:S(2)}, u32[]{:S(2)}) async-start(bf16[32,72,128]{2,1,0:T(8,128)(2,1)} %shard_map.73), calls=%async_computation.1 | async-start | bytes 1179648 | tf_op jit(solution)/shard_map/all_to_all | solution.py:522
  105.3 17.3 %shard_map.72 = (bf16[64,128,128]{2,1,0:T(8,128)(2,1)}, bf16[64,128,128]{2,1,0:T(8,128)(2,1)}) custom-call(s32[3]{0:T(128)} %pad_add_fusion.meta, bf16[16,512,128]{2,1,0:T(8,128)(2,1)} %get-tuple-element.24.fo, bf16[16,512,128]{2,1,0:T(8,128)(2,1)} %get-tuple-element.25.xo, bf16[2,16,48,128]{3,2,1,0:T(8,128)(2,1)} %copy-done, ...), custom_call_target="tpu_custom_call" | custom-call | flops 4831838208 | bytes 25165824 | tf_op jit(solution)/shard_map/pallas_call | solution.py:525
  122.6 0.0 all-to-all-done.1
  122.7 1.1 convert.1
  (11 shorter events, 0.0 us)
Async XLA Ops:
  7.2 6.9 %collective-permute-start = (bf16[2,16,48,128]{3,2,1,0:T(8,128)(2,1)}, bf16[2,16,48,128]{3,2,1,0:T(8,128)(2,1)S(1)}, u32[]{:S(2)}, u32[]{:S(2)}) collective-permute-start(bf16[2,16,48,128]{3,2,1,0:T(8,128)(2,1)} %get-tuple-element.26), channel_id=1, source_target_pairs={{0,1},{1,2},{2,3},{4,5},{5,6},{6,7},{8,9},{9,10},{10,11},{12,13},{... | collective-permute-start | bytes 1179656 | tf_op jit(solution)/shard_map/ppermute | solution.py:406
  9.6 5.9 %collective-permute-start.1 = (bf16[2,16,48,128]{3,2,1,0:T(8,128)(2,1)}, bf16[2,16,48,128]{3,2,1,0:T(8,128)(2,1)S(1)}, u32[]{:S(2)}, u32[]{:S(2)}) collective-permute-start(bf16[2,16,48,128]{3,2,1,0:T(8,128)(2,1)} %get-tuple-element.27), channel_id=1, source_target_pairs={{1,0},{2,1},{3,2},{5,4},{6,5},{7,6},{9,8},{10,9},{11,10},{13,12},{... | collective-permute-start | bytes 1179656 | tf_op jit(solution)/shard_map/ppermute | solution.py:406
  14.1 1.4 %copy-start = (bf16[2,16,48,128]{3,2,1,0:T(8,128)(2,1)}, bf16[2,16,48,128]{3,2,1,0:T(8,128)(2,1)S(1)}, u32[]{:S(2)}) copy-start(bf16[2,16,48,128]{3,2,1,0:T(8,128)(2,1)S(1)} %collective-permute-done.lh) | copy-start | bytes 1179652
  15.5 0.7 copy-start.1
  18.9 24.3 %collective-permute-start.2 = (bf16[3,608,128]{2,1,0:T(8,128)(2,1)}, bf16[3,608,128]{2,1,0:T(8,128)(2,1)S(1)}, u32[]{:S(2)}, u32[]{:S(2)}) collective-permute-start(bf16[3,608,128]{2,1,0:T(8,128)(2,1)} %get-tuple-element.29), channel_id=1, source_target_pairs={{0,4},{4,8},{8,12},{12,16},{16,20},{20,24},{24,28},{1,5},{5,9},{9,... | collective-permute-start | bytes 1400840 | tf_op jit(solution)/shard_map/ppermute | solution.py:406
  22.3 20.8 %collective-permute-start.3 = (bf16[3,608,128]{2,1,0:T(8,128)(2,1)}, bf16[3,608,128]{2,1,0:T(8,128)(2,1)S(1)}, u32[]{:S(2)}, u32[]{:S(2)}) collective-permute-start(bf16[3,608,128]{2,1,0:T(8,128)(2,1)} %get-tuple-element.30), channel_id=1, source_target_pairs={{4,0},{8,4},{12,8},{16,12},{20,16},{24,20},{28,24},{5,1},{9,5},{13... | collective-permute-start | bytes 1400840 | tf_op jit(solution)/shard_map/ppermute | solution.py:406
  43.1 0.8 copy-start.5
  43.1 1.0 copy-start.6
  44.2 22.4 %copy-start.8 = (bf16[3,608,128]{2,1,0:T(8,128)(2,1)S(1)}, bf16[3,608,128]{2,1,0:T(8,128)(2,1)}, u32[]{:S(2)}) copy-start(bf16[3,608,128]{2,1,0:T(8,128)(2,1)} %get-tuple-element.31) | copy-start | bytes 1400836
  44.2 26.1 %copy-start.7 = (bf16[3,608,128]{2,1,0:T(8,128)(2,1)S(1)}, bf16[3,608,128]{2,1,0:T(8,128)(2,1)}, u32[]{:S(2)}) copy-start(bf16[3,608,128]{2,1,0:T(8,128)(2,1)} %get-tuple-element.32) | copy-start | bytes 1400836
  55.3 38.7 %all-to-all-start = ((bf16[32,72,128]{2,1,0:T(8,128)(2,1)}), bf16[32,72,128]{2,1,0:T(8,128)(2,1)S(1)}, u32[]{:S(2)}, u32[]{:S(2)}) async-start(bf16[32,72,128]{2,1,0:T(8,128)(2,1)} %bitcast.6), calls=%async_computation | async-start | bytes 1179648 | tf_op jit(solution)/shard_map/all_to_all | solution.py:513
  66.6 27.4 %collective-permute-start.4 = (bf16[3,608,128]{2,1,0:T(8,128)(2,1)S(1)}, bf16[3,608,128]{2,1,0:T(8,128)(2,1)S(1)}, u32[]{:S(2)}, u32[]{:S(2)}) collective-permute-start(bf16[3,608,128]{2,1,0:T(8,128)(2,1)S(1)} %copy-done.8), channel_id=1, source_target_pairs={{0,4},{4,8},{8,12},{12,16},{16,20},{20,24},{24,28},{1,5},{5,9},{9,... | collective-permute-start | bytes 1400840 | tf_op jit(solution)/shard_map/ppermute | solution.py:406
  70.3 23.7 %collective-permute-start.5 = (bf16[3,608,128]{2,1,0:T(8,128)(2,1)S(1)}, bf16[3,608,128]{2,1,0:T(8,128)(2,1)S(1)}, u32[]{:S(2)}, u32[]{:S(2)}) collective-permute-start(bf16[3,608,128]{2,1,0:T(8,128)(2,1)S(1)} %copy-done.7), channel_id=1, source_target_pairs={{4,0},{8,4},{12,8},{16,12},{20,16},{24,20},{28,24},{5,1},{9,5},{13... | collective-permute-start | bytes 1400840 | tf_op jit(solution)/shard_map/ppermute | solution.py:406
  94.0 0.8 copy-start.3
  94.0 1.0 copy-start.4
  95.0 0.8 copy-start.2
  97.8 24.8 %all-to-all-start.1 = ((bf16[32,72,128]{2,1,0:T(8,128)(2,1)}), bf16[32,72,128]{2,1,0:T(8,128)(2,1)S(1)}, u32[]{:S(2)}, u32[]{:S(2)}) async-start(bf16[32,72,128]{2,1,0:T(8,128)(2,1)} %shard_map.73), calls=%async_computation.1 | async-start | bytes 1179648 | tf_op jit(solution)/shard_map/all_to_all | solution.py:522

commit v2 on v1

v2 whole, which is shorter than its diff:
```python
import functools

import jax
import jax.numpy as jnp
from jax import lax
from jax.experimental import pallas as pl
from jax.experimental.pallas import tpu as pltpu
from jax.sharding import PartitionSpec as P

H = 3
C = 128
F32 = jnp.float32
BF16 = jnp.bfloat16
ANY = pl.BlockSpec(memory_space=pl.ANY)
VMEM = pl.BlockSpec(memory_space=pltpu.VMEM)
SMEM = pl.BlockSpec(memory_space=pltpu.SMEM)


def params(mib):
    return pltpu.CompilerParams(vmem_limit_bytes=mib << 20)


def cost(flops, nbytes):
    return pl.CostEstimate(flops=int(flops), bytes_accessed=int(nbytes), transcendentals=0)


def to_blocks(rows):
    cols = rows[0].shape[0]
    v = [r.reshape(cols // 8, 8, C) for r in rows]
    low = lax.broadcasted_iota(jnp.int32, v[0].shape, 1) < 4

    def swap(a, b):
        return jnp.where(low, a, pltpu.roll(b, 4, 1)), jnp.where(low, pltpu.roll(a, 4, 1), b)

    a, b = swap(v[0], v[1])
    c, d = swap(v[2], v[3])
    y = jnp.stack([jnp.concatenate([a, c], axis=1), jnp.concatenate([b, d], axis=1)], axis=1)
    return y.reshape(4 * cols, C)


def from_blocks(y):
    cols = y.shape[0] // 4
    y = y.reshape(cols // 8, 2, 2, 8, C)
    a, b, c, d = y[:, 0, 0], y[:, 1, 0], y[:, 0, 1], y[:, 1, 1]
    low = lax.broadcasted_iota(jnp.int32, a.shape, 1) < 4

    def swap(a, b):
        return jnp.where(low, a, pltpu.roll(b, 4, 1)), jnp.where(low, pltpu.roll(a, 4, 1), b)

    r0, r1 = swap(a, b)
    r2, r3 = swap(c, d)
    return [r.reshape(cols, C) for r in (r0, r1, r2, r3)]


def column_mask(meta, nj):
    shape = (nj + 2 * H, 16, C)
    j = lax.broadcasted_iota(jnp.int32, shape, 0)
    s = lax.broadcasted_iota(jnp.int32, shape, 1)
    col = meta[1] + 4 * (j - H) + (s & 3)
    return ((col >= 0) & (col < meta[2])).astype(F32).reshape(-1, C)


def live(meta, cm, a, start, size):
    s = lax.broadcasted_iota(jnp.int32, (1, 16, C), 1)
    row = meta[0] + 4 * a + (s >> 2)
    row_mask = ((row >= 0) & (row < meta[2])).astype(F32)
    return (cm[start : start + size, :].reshape(size // 16, 16, C) * row_mask).reshape(size, C)


def elu_parts(v):
    e = jnp.exp(jnp.minimum(v, 0.0))
    return jnp.maximum(v, 0.0) + (e - 1.0), e


def conv_pairs(read, pairs, d, weights):
    parts = []
    for a in pairs:
        cells = []
        for q in range(3):
            cells += [read(a, q), read(a + d, q), read(a - d, q), read(a + 2 * d, q)]
        parts.append(jnp.concatenate(cells, axis=1))
    left = jnp.concatenate(parts, axis=0) if len(parts) > 1 else parts[0]
    return jnp.dot(left, weights, preferred_element_type=F32)


def outer(left, right):
    return lax.dot_general(left, right, (((0,), (0,)), ((), ())), preferred_element_type=F32)


def pack_kernel(k_ref, *w_refs):
    zero = jnp.zeros((C, C), BF16)
    for layer in range(2):
        for back in range(2):
            def tap(p, q):
                if back:
                    return k_ref[layer, 2 - p, 2 - q].T
                return k_ref[layer, p, q]

            w_ref = w_refs[2 * layer + back]
            for q in range(3):
                t0, t1, t2 = tap(0, q), tap(1, q), tap(2, q)
                o = 4 * C * q
                blocks = ((t1, t0), (t2, t1), (t0, zero), (zero, t2))
                for i, (x, y) in enumerate(blocks):
                    w_ref[o + C * i : o + C * (i + 1), :C] = x
                    w_ref[o + C * i : o + C * (i + 1), C:] = y


def layout_kernel(meta, f_ref, g_ref, fx, gx, ua, da, ub, db, *, step, nj, na):
    m0 = 16 * nj
    i = pl.program_id(0)
    base = i * step
    shape = (nj, 16, C)
    s = lax.broadcasted_iota(jnp.int32, shape, 1)
    j = lax.broadcasted_iota(jnp.int32, shape, 0)
    cm = (meta[1] + 4 * j + (s & 3) < meta[2]).astype(F32)
    s1 = lax.broadcasted_iota(jnp.int32, (1, 16, C), 1)
    own = pl.ds(16 * H, m0)

    def blocks(ref, k):
        return to_blocks([ref[4 * k + t].astype(F32) for t in range(4)])

    for k in range(step):
        fx[k, own] = blocks(f_ref, k).astype(BF16)
        rm = (meta[0] + 4 * (base + k) + (s1 >> 2) < meta[2]).astype(F32)
        g = blocks(g_ref, k).reshape(shape)
        gx[k, own] = (g * (cm * rm)).reshape(m0, C).astype(BF16)

    @pl.when(i == 0)
    def _():
        for out, rows in ((ua, (fx.at[0], gx.at[0], gx.at[1])), (ub, (fx.at[1], fx.at[2], gx.at[2]))):
            for t in range(3):
                out[t, own] = rows[t][own]

    @pl.when(i == na // step - 1)
    def _():
        for out, rows in (
            (da, (fx.at[step - 1], gx.at[step - 2], gx.at[step - 1])),
            (db, (fx.at[step - 3], fx.at[step - 2], gx.at[step - 3])),
        ):
            for t in range(3):
                out[t, own] = rows[t][own]


def halo_kernel(meta, ev_ref, od_ref, _w, *refs, nj, na):
    fx, gx, ua, da, ub, db, buf, sem = refs[6:]
    m0 = 16 * nj
    odd = meta[3] == 1
    shape = (2 * H, 16, C)
    s = lax.broadcasted_iota(jnp.int32, shape, 1)
    j = lax.broadcasted_iota(jnp.int32, shape, 0) - H
    col = meta[1] + 4 * jnp.where(j < 0, j, j + nj) + (s & 3)
    cm = ((col >= 0) & (col < meta[2])).astype(F32)
    s1 = lax.broadcasted_iota(jnp.int32, (1, 16, C), 1)

    def halos(n, k):
        def blocks(ref):
            return to_blocks([ref[n, 4 * k + t].astype(F32) for t in range(4)])

        ev, od = blocks(ev_ref), blocks(od_ref)
        low = jnp.where(odd, ev, od)[16 * (4 - H) :]
        high = jnp.where(odd, od, ev)[: 16 * H]
        return jnp.concatenate([low, high], axis=0)

    for k in range(na):
        f = halos(0, k).astype(BF16)
        rm = (meta[0] + 4 * k + (s1 >> 2) < meta[2]).astype(F32)
        g = (halos(1, k).reshape(shape) * (cm * rm)).reshape(2 * H * 16, C).astype(BF16)
        for n, v in enumerate((f, g)):
            buf[n, 0, k] = v[: 16 * H]
            buf[n, 1, k] = v[16 * H :]
    jobs = []
    go = copier(sem, jobs)
    for side, start in ((0, 0), (1, 16 * H + m0)):
        to = pl.ds(start, 16 * H)
        for out, f0, fn, g0, gn in ((ua, 0, 1, 0, 2), (da, na - 1, 1, na - 2, 2), (ub, 1, 2, 2, 1), (db, na - 3, 2, na - 3, 1)):
            go(buf.at[0, side, pl.ds(f0, fn)], out.at[pl.ds(0, fn), to])
            go(buf.at[1, side, pl.ds(g0, gn)], out.at[pl.ds(fn, gn), to])
        go(buf.at[0, side], fx.at[:, to])
        go(buf.at[1, side], gx.at[:, to])
    for c in jobs:
        c.wait()


def copier(sem, jobs):
    def go(src, dst):
        c = pltpu.make_async_copy(src, dst, sem.at[len(jobs)])
        c.start()
        jobs.append(c)

    return go


def inner_kernel(
    meta, fxi, gxi, wc, wb, a1o, a2o, so, g1o, gfo, acc_o,
    fx, gx, a1, a2, st, es, g1, gf, cm, sem, insem, *, na, nj,
):
    m0, m1, m2, w = 16 * nj, 16 * (nj + 2), 16 * (nj + 4), 16 * (nj + 6)
    ni = na - 4
    jobs = []
    go = copier(insem, jobs)
    go(fxi, fx)
    go(gxi, gx)
    cm[...] = column_mask(meta, nj)
    jobs[0].wait()

    def activate(a, _):
        v, _e = elu_parts(fx[a].astype(F32))
        a1[a] = (v * live(meta, cm, a, 0, w)).astype(BF16)
        return 0

    lax.fori_loop(0, na, activate, 0)
    out_a1 = pltpu.make_async_copy(a1, a1o, sem.at[0])
    out_a1.start()
    jobs[1].wait()

    def quad(t, _):
        r = 2 + 4 * t
        acc = conv_pairs(lambda row, q: a1[row, pl.ds(16 * q, m2), :], [r, r + 2], 1, wc[...])
        for k in range(2):
            for b in range(2):
                row = r + 2 * k + b
                v = fx[row, pl.ds(16, m2), :].astype(F32) + acc[k * m2 : (k + 1) * m2, b * C : (b + 1) * C]
                act, e = elu_parts(v)
                a2[row + 2] = (act * live(meta, cm, row, 16, m2)).astype(BF16)
                es[row - 2] = e[16 : 16 + m1]
                st[row - 2] = v[32 : 32 + m0]
        acc = conv_pairs(lambda row, q: gx[row, pl.ds(32 * q, m1), :], [r, r + 1], 2, wb[...])
        for k in range(2):
            for b in range(2):
                row = r + k + 2 * b
                back = acc[k * m1 : (k + 1) * m1, b * C : (b + 1) * C]
                full = gx[row, pl.ds(32, m1), :].astype(F32) + live(meta, cm, row, 32, m1) * es[row - 2] * back
                g1[row + 1] = full.astype(BF16)
                gf[row - 2] = full[16 : 16 + m0]
        return 0

    lax.fori_loop(0, ni // 4, quad, 0)
    copies = [
        pltpu.make_async_copy(a2.at[pl.ds(4, ni)], a2o.at[pl.ds(4, ni)], sem.at[1]),
        pltpu.make_async_copy(st, so.at[pl.ds(2, ni)], sem.at[2]),
        pltpu.make_async_copy(g1.at[pl.ds(3, ni)], g1o.at[pl.ds(3, ni)], sem.at[3]),
        pltpu.make_async_copy(gf, gfo.at[pl.ds(2, ni)], sem.at[4]),
    ]
    for c in copies:
        c.start()
    for i in (0, 1, 2, 3):
        a2[i] = jnp.zeros((m2, C), BF16)
        a2[na + i] = jnp.zeros((m2, C), BF16)
    for i in (0, 1, 2):
        g1[i] = jnp.zeros((m1, C), BF16)
        g1[na - 1 + i] = jnp.zeros((m1, C), BF16)

    def second(rows):
        left = [jnp.concatenate([a2[b + 2 + s, 32 : 32 + m0] for s in (2, 0, -2)], axis=1) for b in rows]
        right = [jnp.concatenate([gx[b, 16 + 32 * q : 16 + 32 * q + m0] for q in range(3)], axis=1) for b in rows]
        return outer(jnp.concatenate(left, axis=0), jnp.concatenate(right, axis=0))

    def first(rows):
        left = [jnp.concatenate([g1[b + 1 + s, 16 : 16 + m0] for s in (1, 0, -1)], axis=1) for b in rows]
        right = [jnp.concatenate([a1[b, 32 + 16 * q : 32 + 16 * q + m0] for q in range(3)], axis=1) for b in rows]
        return outer(jnp.concatenate(left, axis=0), jnp.concatenate(right, axis=0))

    half = na // 2
    acc_o[1] = second(range(half))
    acc_o[1] += second(range(half, na))
    acc_o[0] = first(range(1, half))
    acc_o[0] += first(range(half, na - 1))
    out_a1.wait()
    for c in copies:
        c.wait()


def edge_kernel(
    meta, fxi, gxi, a1i, up, dn, wc, wb, acc_i, _a2, _s, _g1, _gf, a2o, so, g1o, gfo, kg,
    a1, g, f, fh, a2, st, es, g1, gf, cm, sem, *, na, nj,
):
    m0, m1, m2, w = 16 * nj, 16 * (nj + 2), 16 * (nj + 4), 16 * (nj + 6)
    jobs = []

    go = copier(sem, jobs)
    go(up.at[pl.ds(0, 1)], fh.at[0])
    go(dn.at[pl.ds(0, 1)], fh.at[1])
    go(up.at[pl.ds(1, 2)], g.at[0, pl.ds(0, 2)])
    go(gxi.at[pl.ds(0, 6)], g.at[0, pl.ds(2, 6)])
    go(gxi.at[pl.ds(na - 6, 6)], g.at[1, pl.ds(0, 6)])
    go(dn.at[pl.ds(1, 2)], g.at[1, pl.ds(6, 2)])
    go(a1i.at[pl.ds(0, 3)], a1.at[0, pl.ds(1, 3)])
    go(a1i.at[pl.ds(na - 3, 3)], a1.at[1, pl.ds(0, 3)])
    go(fxi.at[pl.ds(0, 2)], f.at[0])
    go(fxi.at[pl.ds(na - 2, 2)], f.at[1])
    cm[...] = column_mask(meta, nj)
    for c in jobs:
        c.wait()
    for s, row, slot in ((0, -1, 0), (1, na, 3)):
        v, _e = elu_parts(fh[s, 0].astype(F32))
        a1[s, slot] = (v * live(meta, cm, row, 0, w)).astype(BF16)

    acc = conv_pairs(lambda i, q: a1[i // 8, i % 8, 16 * q : 16 * q + m2], [1, 9], 1, wc[...])
    for s in range(2):
        for b in range(2):
            row = (na - 2) * s + b
            v = f[s, b, 16 : 16 + m2].astype(F32) + acc[s * m2 : (s + 1) * m2, b * C : (b + 1) * C]
            act, e = elu_parts(v)
            a2[s, b] = (act * live(meta, cm, row, 16, m2)).astype(BF16)
            es[s, b] = e[16 : 16 + m1]
            st[s, b] = v[32 : 32 + m0]
    acc = conv_pairs(lambda i, q: g[i // 16, i % 16, 32 * q : 32 * q + m1], [2, 3, 18, 19], 2, wb[...])
    for s in range(2):
        for b in range(2):
            row = (na - 2) * s + b
            k = 2 * s + b
            back = acc[k * m1 : (k + 1) * m1, s * C : (s + 1) * C]
            full = g[s, 2 + 2 * s + b, 32 : 32 + m1].astype(F32) + live(meta, cm, row, 32, m1) * es[s, b] * back
            g1[s, b] = full.astype(BF16)
            gf[s, b] = full[16 : 16 + m0]
    outs = len(jobs)
    for s in range(2):
        go(a2.at[s], a2o.at[pl.ds(2 + (na - 2) * s, 2)])
        go(st.at[s], so.at[pl.ds((na - 2) * s, 2)])
        go(g1.at[s], g1o.at[pl.ds(1 + (na - 2) * s, 2)])
        go(gf.at[s], gfo.at[pl.ds((na - 2) * s, 2)])

    rows = [(s, b) for s in range(2) for b in range(2)]
    left = jnp.concatenate([a2[s, b, 32 : 32 + m0] for s, b in rows], axis=0)
    for p in range(3):
        right = [
            jnp.concatenate([g[s, 2 * s + b + 2 * p, 16 + 32 * q : 16 + 32 * q + m0] for q in range(3)], axis=1)
            for s, b in rows
        ]
        total = acc_i[1, C * p : C * (p + 1)] + outer(left, jnp.concatenate(right, axis=0))
        for q in range(3):
            kg[1, 2 - p, 2 - q] = total[:, C * q : C * (q + 1)].astype(BF16)
    left = jnp.concatenate([g1[s, b, 16 : 16 + m0] for s, b in rows], axis=0)
    for p in range(3):
        right = [
            jnp.concatenate([a1[s, b + p, 32 + 16 * q : 32 + 16 * q + m0] for q in range(3)], axis=1) for s, b in rows
        ]
        total = acc_i[0, C * p : C * (p + 1)] + outer(left, jnp.concatenate(right, axis=0))
        for q in range(3):
            kg[0, p, q] = total[:, C * q : C * (q + 1)].T.astype(BF16)
    for c in jobs[outs:]:
        c.wait()


def finish_rows(meta, cm, rows, acc2, acc1, state, grads, feats, put):
    m0 = feats(rows[0]).shape[0]
    for row in rows:
        mask = live(meta, cm, row, 16 * H, m0)
        put(0, row, from_blocks((state(row) + acc2(row)) * mask))
        slope = jnp.exp(jnp.minimum(feats(row).astype(F32), 0.0))
        put(1, row, from_blocks(grads(row) + mask * slope * acc1(row)))


def middle_kernel(meta, fxi, wc2, wb1, a2i, si, g1i, gfi, out, fg, fm, a2, st, g1, gf, cm, ot, ft, sem, osem, *, na, nj):
    m0 = 16 * nj
    ni = na - 4
    jobs = []
    go = copier(sem, jobs)
    go(a2i.at[pl.ds(2, na)], a2)
    go(g1i.at[pl.ds(2, na - 2)], g1)
    go(si.at[pl.ds(2, ni)], st)
    go(fxi.at[pl.ds(2, ni), pl.ds(16 * H, m0)], fm)
    go(gfi.at[pl.ds(2, ni)], gf)
    cm[...] = column_mask(meta, nj)
    for c in jobs:
        c.wait()

    def quad(t, _):
        r = 2 + 4 * t
        acc2 = conv_pairs(lambda row, q: a2[row, pl.ds(32 * q, m0), :], [r, r + 1], 2, wc2[...])
        acc1 = conv_pairs(lambda row, q: g1[row - 1, pl.ds(16 * q, m0), :], [r, r + 2], 1, wb1[...])

        def put(n, row, parts):
            for i, x in enumerate(parts):
                (ot, ft)[n][4 * (row - 2) + i] = x.astype(BF16)

        for k in range(4):
            i2, j2, i1, j1 = k % 2, k // 2, k // 2, k % 2
            finish_rows(
                meta, cm, [r + k],
                lambda _: acc2[i2 * m0 : (i2 + 1) * m0, j2 * C : (j2 + 1) * C],
                lambda _: acc1[i1 * m0 : (i1 + 1) * m0, j1 * C : (j1 + 1) * C],
                lambda row: st[row - 2], lambda row: gf[row - 2], lambda row: fm[row - 2], put,
            )
        here, there = pl.ds(16 * t, 16), pl.ds(16 * t + 8, 16)
        pltpu.make_async_copy(ot.at[here], out.at[there], osem.at[0]).start()
        pltpu.make_async_copy(ft.at[here], fg.at[there], osem.at[1]).start()
        return 0

    lax.fori_loop(0, ni // 4, quad, 0)
    pltpu.make_async_copy(ot, out.at[pl.ds(8, 4 * ni)], osem.at[0]).wait()
    pltpu.make_async_copy(ft, fg.at[pl.ds(8, 4 * ni)], osem.at[1]).wait()


def mask_kernel(meta, cm, *, nj):
    cm[...] = column_mask(meta, nj)


def last_kernel(
    meta, cm, fxi, gxi, a1i, upa, dna, upb, dnb, wc, wb, wc2, wb1, a2i, si, g1i, gfi, _out, _fg, out, fg,
    a1, g, f, fm, a2, st, es, g1, gf, ot, ft, sem, *, na, nj,
):
    m0, m1, m2, w = 16 * nj, 16 * (nj + 2), 16 * (nj + 4), 16 * (nj + 6)
    jobs = []
    go = copier(sem, jobs)
    go(upb.at[pl.ds(0, 2)], f.at[0, pl.ds(0, 2)])
    go(upa.at[pl.ds(0, 1)], f.at[0, pl.ds(2, 1)])
    go(dna.at[pl.ds(0, 1)], f.at[1, pl.ds(0, 1)])
    go(dnb.at[pl.ds(0, 2)], f.at[1, pl.ds(1, 2)])
    go(upb.at[pl.ds(2, 1)], g.at[0, pl.ds(0, 1)])
    go(upa.at[pl.ds(2, 1)], g.at[0, pl.ds(1, 1)])
    go(gxi.at[pl.ds(1, 1)], g.at[0, pl.ds(2, 1)])
    go(gxi.at[pl.ds(3, 1)], g.at[0, pl.ds(3, 1)])
    go(gxi.at[pl.ds(na - 4, 1)], g.at[1, pl.ds(0, 1)])
    go(gxi.at[pl.ds(na - 2, 1)], g.at[1, pl.ds(1, 1)])
    go(dna.at[pl.ds(1, 1)], g.at[1, pl.ds(2, 1)])
    go(dnb.at[pl.ds(2, 1)], g.at[1, pl.ds(3, 1)])
    go(a1i.at[pl.ds(0, 1)], a1.at[0, pl.ds(3, 1)])
    go(a1i.at[pl.ds(na - 1, 1)], a1.at[1, pl.ds(0, 1)])
    early = len(jobs)
    go(a2i.at[pl.ds(2, 6)], a2.at[0, pl.ds(2, 6)])
    go(a2i.at[pl.ds(na - 4, 6)], a2.at[1, pl.ds(0, 6)])
    go(g1i.at[pl.ds(1, 3)], g1.at[0, pl.ds(1, 3)])
    go(g1i.at[pl.ds(na - 2, 3)], g1.at[1, pl.ds(0, 3)])
    for s in range(2):
        two = pl.ds((na - 2) * s, 2)
        go(si.at[two], st.at[s])
        go(fxi.at[two, pl.ds(16 * H, m0)], fm.at[s])
        go(gfi.at[two], gf.at[s])
    for c in jobs[:early]:
        c.wait()
    for s in range(2):
        for i in range(3):
            row = i - 3 if s == 0 else na + i
            v, _e = elu_parts(f[s, i].astype(F32))
            a1[s, i + s] = (v * live(meta, cm, row, 0, w)).astype(BF16)
    acc = conv_pairs(lambda i, q: a1[i // 8, i % 8, 16 * q : 16 * q + m2], [1, 9], 1, wc[...])
    for s in range(2):
        for b in range(2):
            row = b - 2 if s == 0 else na + b
            v = f[s, 1 - s + b, 16 : 16 + m2].astype(F32) + acc[s * m2 : (s + 1) * m2, b * C : (b + 1) * C]
            act, e = elu_parts(v)
            a2[s, 6 * s + b] = (act * live(meta, cm, row, 16, m2)).astype(BF16)
            if b != s:
                es[s] = e[16 : 16 + m1]
    acc = conv_pairs(lambda i, q: g[i // 8, i % 8, 32 * q : 32 * q + m1], [1, 9], 1, wb[...])
    for s in range(2):
        row = -1 if s == 0 else na
        back = acc[s * m1 : (s + 1) * m1, s * C : (s + 1) * C]
        full = g[s, 1 + s, 32 : 32 + m1].astype(F32) + live(meta, cm, row, 32, m1) * es[s] * back
        g1[s, 3 * s] = full.astype(BF16)
    for c in jobs[early:]:
        c.wait()
    acc2 = conv_pairs(lambda i, q: a2[i // 16, i % 16, 32 * q : 32 * q + m0], [2, 3, 18, 19], 2, wc2[...])
    acc1 = conv_pairs(lambda i, q: g1[i // 8, i % 8, 16 * q : 16 * q + m0], [1, 9], 1, wb1[...])
    for s in range(2):
        for b in range(2):
            row = (na - 2) * s + b
            k = 2 * s + b

            def put(n, row, parts):
                for i, x in enumerate(parts):
                    (ot, ft)[n][s, 4 * b + i] = x.astype(BF16)

            finish_rows(
                meta, cm, [row],
                lambda _: acc2[k * m0 : (k + 1) * m0, s * C : (s + 1) * C],
                lambda _: acc1[s * m0 : (s + 1) * m0, b * C : (b + 1) * C],
                lambda _: st[s, b], lambda _: gf[s, b], lambda _: fm[s, b], put,
            )
    done = len(jobs)
    for s in range(2):
        go(ot.at[s], out.at[pl.ds(4 * (na - 2) * s, 8)])
        go(ft.at[s], fg.at[pl.ds(4 * (na - 2) * s, 8)])
    for c in jobs[done:]:
        c.wait()


def sum_kernel(meta, x_ref, _out, o_ref):
    total = jnp.sum(x_ref[...].astype(F32), axis=0) / meta[2].astype(F32)
    o_ref[...] = jnp.broadcast_to(total.astype(BF16)[None], o_ref.shape)


def shift(x, axis, step):
    n = lax.axis_size(axis)
    return lax.ppermute(x, axis, [(i, i + step) for i in range(n) if 0 <= i + step < n])


def body(features, kernels, length, cotangent):
    rows, cols, _ = features.shape
    na, nj = rows // 4, cols // 4
    m0, m1, m2, w = 16 * nj, 16 * (nj + 2), 16 * (nj + 4), 16 * (nj + 6)
    ni = na - 4
    odd = lax.rem(lax.axis_index("col"), 2)
    meta = jnp.stack([lax.axis_index("row") * rows, lax.axis_index("col") * cols, length[0], odd]).astype(jnp.int32)
    sds = jax.ShapeDtypeStruct

    near = jnp.where(odd == 1, 0, cols - 16)
    far = jnp.where(odd == 1, cols - 16, 0)

    def edges(start):
        return jnp.stack([lax.dynamic_slice_in_dim(x, start, 16, axis=1) for x in (features, cotangent)])

    n = lax.axis_size("col")
    inner = [(i, i ^ 1) for i in range(n)]
    outer_pairs = [(i, i + 1) for i in range(1, n - 1, 2)]
    od = lax.ppermute(edges(far), "col", outer_pairs + [(j, i) for i, j in outer_pairs])
    ev = lax.ppermute(edges(near), "col", inner)
    w_one, w_one_back, w_two, w_two_back = pl.pallas_call(
        pack_kernel,
        in_specs=[VMEM],
        out_specs=[VMEM] * 4,
        out_shape=[sds((12 * C, 2 * C), BF16)] * 4,
        compiler_params=params(56),
        cost_estimate=cost(0, 8 << 20),
    )(kernels)
    step = 4
    row_block = pl.BlockSpec((4 * step, cols, C), lambda i: (i, 0, 0))
    shapes = [sds((na, w, C), BF16)] * 2 + [sds((3, w, C), BF16)] * 4
    extended = pl.pallas_call(
        functools.partial(layout_kernel, step=step, nj=nj, na=na),
        grid=(na // step,),
        in_specs=[SMEM, row_block, row_block],
        out_specs=[pl.BlockSpec((step, w, C), lambda i: (i, 0, 0))] * 2
        + [pl.BlockSpec((3, w, C), lambda i: (0, 0, 0))] * 4,
        out_shape=shapes,
        compiler_params=params(56),
        cost_estimate=cost(0, 12 << 20),
    )(meta, features, cotangent)
    fx, gx, ua, da, ub, db = pl.pallas_call(
        functools.partial(halo_kernel, nj=nj, na=na),
        in_specs=[SMEM, VMEM, VMEM, ANY] + [ANY] * 6,
        out_specs=[ANY] * 6,
        out_shape=shapes,
        scratch_shapes=[pltpu.VMEM((2, 2, na, 16 * H, C), BF16), pltpu.SemaphoreType.DMA((20,))],
        input_output_aliases={4 + i: i for i in range(6)},
        compiler_params=params(56),
        cost_estimate=cost(0, 4 << 20),
    )(meta, ev, od, w_one, *extended)
    dna = shift(ua, "row", -1)
    upa = shift(da, "row", 1)
    dnb = shift(ub, "row", -1)
    upb = shift(db, "row", 1)

    conv_flops = 2 * rows * cols * 9 * C * C
    a1, a2, st, g1, gf, acc = pl.pallas_call(
        functools.partial(inner_kernel, na=na, nj=nj),
        in_specs=[SMEM] + [ANY] * 2 + [VMEM] * 2,
        out_specs=[ANY] * 5 + [VMEM],
        out_shape=[
            sds((na, w, C), BF16),
            sds((na + 4, m2, C), BF16),
            sds((na, m0, C), F32),
            sds((na + 2, m1, C), BF16),
            sds((na, m0, C), F32),
            sds((2, 3 * C, 3 * C), F32),
        ],
        scratch_shapes=[
            pltpu.VMEM((na, w, C), BF16),
            pltpu.VMEM((na, w, C), BF16),
            pltpu.VMEM((na, w, C), BF16),
            pltpu.VMEM((na + 4, m2, C), BF16),
            pltpu.VMEM((ni, m0, C), F32),
            pltpu.VMEM((ni, m1, C), F32),
            pltpu.VMEM((na + 2, m1, C), BF16),
            pltpu.VMEM((ni, m0, C), F32),
            pltpu.VMEM((w, C), F32),
            pltpu.SemaphoreType.DMA((5,)),
            pltpu.SemaphoreType.DMA((2,)),
        ],
        compiler_params=params(56),
        cost_estimate=cost(0, 1 << 20),
    )(meta, fx, gx, w_one, w_two_back)

    a2, st, g1, gf, kg = pl.pallas_call(
        functools.partial(edge_kernel, na=na, nj=nj),
        in_specs=[SMEM] + [ANY] * 2 + [ANY] + [ANY] * 2 + [VMEM] * 3 + [ANY] * 4,
        out_specs=[ANY] * 4 + [VMEM],
        out_shape=[
            sds((na + 4, m2, C), BF16),
            sds((na, m0, C), F32),
            sds((na + 2, m1, C), BF16),
            sds((na, m0, C), F32),
            sds((2, 3, 3, C, C), BF16),
        ],
        scratch_shapes=[
            pltpu.VMEM((2, 4, w, C), BF16),
            pltpu.VMEM((2, 8, w, C), BF16),
            pltpu.VMEM((2, 2, w, C), BF16),
            pltpu.VMEM((2, 1, w, C), BF16),
            pltpu.VMEM((2, 2, m2, C), BF16),
            pltpu.VMEM((2, 2, m0, C), F32),
            pltpu.VMEM((2, 2, m1, C), F32),
            pltpu.VMEM((2, 2, m1, C), BF16),
            pltpu.VMEM((2, 2, m0, C), F32),
            pltpu.VMEM((w, C), F32),
            pltpu.SemaphoreType.DMA((18,)),
        ],
        input_output_aliases={9: 0, 10: 1, 11: 2, 12: 3},
        compiler_params=params(56),
        cost_estimate=cost(0, 1 << 20),
    )(meta, fx, gx, a1, upa, dna, w_one, w_two_back, acc, a2, st, g1, gf)

    out, fg = pl.pallas_call(
        functools.partial(middle_kernel, na=na, nj=nj),
        in_specs=[SMEM, ANY] + [VMEM] * 2 + [ANY] * 4,
        out_specs=[ANY] * 2,
        out_shape=[sds(features.shape, BF16)] * 2,
        scratch_shapes=[
            pltpu.VMEM((ni, m0, C), BF16),
            pltpu.VMEM((na, m2, C), BF16),
            pltpu.VMEM((ni, m0, C), F32),
            pltpu.VMEM((na - 2, m1, C), BF16),
            pltpu.VMEM((ni, m0, C), F32),
            pltpu.VMEM((w, C), F32),
            pltpu.VMEM((4 * ni, cols, C), BF16),
            pltpu.VMEM((4 * ni, cols, C), BF16),
            pltpu.SemaphoreType.DMA((5,)),
            pltpu.SemaphoreType.DMA((2,)),
        ],
        compiler_params=params(56),
        cost_estimate=cost(0, 1 << 20),
    )(meta, fx, w_two, w_one_back, a2, st, g1, gf)
    axes = ("row", "col")
    parts = lax.axis_size(axes)
    shares = lax.all_to_all(kg.reshape(parts, -1, C), axes, 0, 0, tiled=True)
    spread = pl.pallas_call(
        sum_kernel,
        in_specs=[SMEM, VMEM, ANY],
        out_specs=VMEM,
        out_shape=sds(shares.shape, BF16),
        compiler_params=params(56),
        cost_estimate=cost(0, 2 << 20),
    )(meta, shares, out)
    whole = lax.all_to_all(spread, axes, 0, 0, tiled=True)
    kernel_gradient = whole.reshape(kernels.shape).astype(F32)

    cm = pl.pallas_call(
        functools.partial(mask_kernel, nj=nj),
        in_specs=[SMEM],
        out_specs=VMEM,
        out_shape=sds((w, C), F32),
        compiler_params=params(56),
        cost_estimate=cost(20 * conv_flops, 1 << 20),
    )(meta)
    out, fg = pl.pallas_call(
        functools.partial(last_kernel, na=na, nj=nj),
        in_specs=[SMEM, VMEM] + [ANY] * 7 + [VMEM] * 4 + [ANY] * 6,
        out_specs=[ANY] * 2,
        out_shape=[sds(features.shape, BF16)] * 2,
        scratch_shapes=[
            pltpu.VMEM((2, 4, w, C), BF16),
            pltpu.VMEM((2, 4, w, C), BF16),
            pltpu.VMEM((2, 3, w, C), BF16),
            pltpu.VMEM((2, 2, m0, C), BF16),
            pltpu.VMEM((2, 8, m2, C), BF16),
            pltpu.VMEM((2, 2, m0, C), F32),
            pltpu.VMEM((2, m1, C), F32),
            pltpu.VMEM((2, 4, m1, C), BF16),
            pltpu.VMEM((2, 2, m0, C), F32),
            pltpu.VMEM((2, 8, cols, C), BF16),
            pltpu.VMEM((2, 8, cols, C), BF16),
            pltpu.SemaphoreType.DMA((28,)),
        ],
        input_output_aliases={17: 0, 18: 1},
        compiler_params=params(56),
        cost_estimate=cost(conv_flops, 12 << 20),
    )(meta, cm, fx, gx, a1, upa, dna, upb, dnb, w_one, w_two_back, w_two, w_one_back, a2, st, g1, gf, out, fg)
    return out, fg, kernel_gradient


def solution(mesh):
    spec = P("row", "col", None)
    return jax.shard_map(
        body, mesh=mesh, in_specs=(spec, P(), P(), spec), out_specs=(spec, spec, P()), check_vma=False
    )
```

time: 124 us -> 109 us (0.88)
  waiting for transfers between devices: 23.8 us -> 4.19 us
  Pallas kernels: 61.1 us -> 68.1 us
  starting transfers between devices: 32.2 us -> 27.9 us
  local copies, waits for them, and re-layouts: 3.6 us -> 5.09 us
    ppermute x6 -> x4, waiting for transfers between devices: 23.8 us -> 0.01 us  [shift(): lax.ppermute(x, axis, [(i, i + step) for i in range(n) if 0 <= i + step <...]
    pallas_call x4 -> x6, Pallas kernels: 13.1 us -> 28.2 us  [the longest x1 12.9 us: body(): pl.pallas_call(functools.partial(middle_kernel, na=na, nj=nj), in_specs=[...]
    pallas_call x1, Pallas kernels: 17.3 us -> 10.2 us  [body(): pl.pallas_call(functools.partial(last_kernel, na=na, nj=nj), in_specs=[SM...]
    all_to_all x1, starting transfers between devices: 11.3 us -> 6.05 us  [body(): shares = lax.all_to_all(kg.reshape(parts, -1, C), axes, 0, 0, tiled=True)]
    ppermute x0 -> x2, starting transfers between devices: none -> 5.06 us  [the longest x1 4.36 us: body(): ev = lax.ppermute(edges(near), 'col', inner)]
    all_to_all x1, waiting for transfers between devices: 0.01 us -> 4.17 us  [body(): whole = lax.all_to_all(spread, axes, 0, 0, tiled=True)]
    ppermute x6 -> x4, starting transfers between devices: 13.4 us -> 10.1 us  [shift(): lax.ppermute(x, axis, [(i, i + step) for i in range(n) if 0 <= i + step <...]
    another operation x0 -> x1, local copies, waits for them, and re-layouts: none -> 1.4 us  [edges(): jnp.stack([lax.dynamic_slice_in_dim(x, start, 16, axis=1) for x in (featu...]
  transfers between devices with their start and end apart: 8 -> 8, of which waited for: 2 -> 1; matrix products, arithmetic and copies ran while one was open for 0% -> 1% of each run, Pallas kernels for 32% -> 50%
where the time goes in v2:
time: 109 us
  Pallas kernels  68.1 us (62%)
  starting transfers between devices  27.9 us (26%)
  local copies, waits for them, and re-layouts  5.09 us (5%)
  waiting for transfers between devices  4.19 us (4%)
  other arithmetic  1.83 us (2%)
  between operations  1.5 us (1%)
    pallas_call x1, Pallas kernels, body(): pl.pallas_call(functools.partial(inner_kernel, na=na, nj=nj), in_specs=[S...  19 us
    pallas_call x1, Pallas kernels, body(): pl.pallas_call(functools.partial(middle_kernel, na=na, nj=nj), in_specs=[...  12.9 us
    pallas_call x1, Pallas kernels, body(): pl.pallas_call(functools.partial(edge_kernel, na=na, nj=nj), in_specs=[SM...  10.6 us
    pallas_call x1, Pallas kernels, body(): pl.pallas_call(functools.partial(last_kernel, na=na, nj=nj), in_specs=[SM...  10.2 us
    ppermute x4, starting transfers between devices, shift(): lax.ppermute(x, axis, [(i, i + step) for i in range(n) if 0 <= i + step <...  10.1 us
    all_to_all x1, starting transfers between devices, body(): whole = lax.all_to_all(spread, axes, 0, 0, tiled=True)  6.71 us
    pallas_call x1, Pallas kernels, body(): pl.pallas_call(functools.partial(layout_kernel, step=step, nj=nj, na=na),...  6.13 us
    all_to_all x1, starting transfers between devices, body(): shares = lax.all_to_all(kg.reshape(parts, -1, C), axes, 0, 0, tiled=True)  6.05 us
  transfers between devices with their start and end apart: 8, of which 1 were waited for; matrix products, arithmetic and copies ran while one was open for 1% of the time, Pallas kernels for 50%

profile of v2, /device:TPU:0, one launch (start us, length us, event | category | flops | bytes accessed | tf_op | source)
XLA Modules:
  0.0 108.6 jit_solution(15985953828759618017)
XLA Ops:
  0.6 1.4 %dynamic-slice_bitcast_fusion = (bf16[1,64,16,128]{3,2,1,0:T(8,128)(2,1)S(1)}, bf16[1,64,16,128]{3,2,1,0:T(8,128)(2,1)S(1)}, bf16[1,64,16,128]{3,2,1,0:T(8,128)(2,1)S(1)}, bf16[1,64,16,128]{3,2,1,0:T(8,128)(2,1)S(1)}) fusion(bf16[64,128,128]{2,1,0:T(8,128)(2,1)} %g_ref.1, s32[]{:T(128)S(6)} %select_n.12, s32[]{:T(128)S(6)} %select_n.11, ...), kind=kLoop, calls=%fused_computation.2 | loop fusion | bytes 2097160 | tf_op jit(solution)/shard_map/stack | solution.py:503
  2.0 0.1 pad_maximum_fusion.1
  2.1 0.7 collective-permute-start.1
  2.8 0.1 pad_maximum_fusion
  2.9 4.4 %collective-permute-start = (bf16[2,64,16,128]{3,2,1,0:T(8,128)(2,1)S(1)}, bf16[2,64,16,128]{3,2,1,0:T(8,128)(2,1)S(1)}, u32[]{:S(2)}, u32[]{:S(2)}) collective-permute-start(bf16[2,64,16,128]{3,2,1,0:T(8,128)(2,1)S(1)} %pad_maximum_fusion), channel_id=1, source_target_pairs={{0,1},{1,0},{2,3},{3,2},{4,5},{5,4},{6,7},{7,6},{8,9},{9,8},{10,11... | collective-permute-start | bytes 1572872 | tf_op jit(solution)/shard_map/ppermute | solution.py:509
  7.9 0.6 pad_add_fusion.meta
  8.5 6.1 %shard_map.69 = (bf16[16,608,128]{2,1,0:T(8,128)(2,1)}, bf16[16,608,128]{2,1,0:T(8,128)(2,1)}, bf16[3,608,128]{2,1,0:T(8,128)(2,1)}, bf16[3,608,128]{2,1,0:T(8,1...) custom-call(s32[4]{0:T(128)} %pad_add_fusion.meta, bf16[64,128,128]{2,1,0:T(8,128)(2,1)} %f_ref.1, ...), custom_call_target="tpu_custom_call" | custom-call | bytes 12582912 | tf_op jit(solution)/shard_map/pallas_call | solution.py:521
  14.6 3.0 %shard_map.68 = (bf16[1536,256]{1,0:T(8,128)(2,1)}, bf16[1536,256]{1,0:T(8,128)(2,1)}, bf16[1536,256]{1,0:T(8,128)(2,1)}, bf16[1536,256]{1,0:T(8,128)(2,1)}) custom-call(bf16[2,3,3,128,128]{4,3,2,1,0:T(8,128)(2,1)} %k_ref.1), custom_call_target="tpu_custom_call" | custom-call | bytes 8388608 | tf_op jit(solution)/shard_map/pallas_call | solution.py:510
  17.6 0.0 copy-start.4
  17.6 0.8 copy-done.3
  18.4 0.2 copy-done.4
  18.5 2.7 %shard_map.70 = (bf16[16,608,128]{2,1,0:T(8,128)(2,1)}, bf16[16,608,128]{2,1,0:T(8,128)(2,1)}, bf16[3,608,128]{2,1,0:T(8,128)(2,1)}, bf16[3,608,128]{2,1,0:T(8,1...) custom-call(s32[4]{0:T(128)} %pad_add_fusion.meta, ...), custom_call_target="tpu_custom_call", output_to_operand_aliasing={{0}: (4, {}), {1}: (5, {}), {2}: (6, {}), {3}: (7, {}), {4}... | custom-call | bytes 4194304 | tf_op jit(solution)/shard_map/pallas_call | solution.py:531
  21.3 3.4 %collective-permute-start.2 = (bf16[3,608,128]{2,1,0:T(8,128)(2,1)}, bf16[3,608,128]{2,1,0:T(8,128)(2,1)S(1)}, u32[]{:S(2)}, u32[]{:S(2)}) collective-permute-start(bf16[3,608,128]{2,1,0:T(8,128)(2,1)} %get-tuple-element.45), channel_id=1, source_target_pairs={{0,4},{4,8},{8,12},{12,16},{16,20},{20,24},{24,28},{1,5},{5,9},{9,... | collective-permute-start | bytes 1400840 | tf_op jit(solution)/shard_map/ppermute | solution.py:487
  24.7 1.5 %collective-permute-start.3 = (bf16[3,608,128]{2,1,0:T(8,128)(2,1)}, bf16[3,608,128]{2,1,0:T(8,128)(2,1)S(1)}, u32[]{:S(2)}, u32[]{:S(2)}) collective-permute-start(bf16[3,608,128]{2,1,0:T(8,128)(2,1)} %get-tuple-element.46), channel_id=1, source_target_pairs={{4,0},{8,4},{12,8},{16,12},{20,16},{24,20},{28,24},{5,1},{9,5},{13... | collective-permute-start | bytes 1400840 | tf_op jit(solution)/shard_map/ppermute | solution.py:487
  26.2 19.0 %shard_map.71 = (bf16[16,608,128]{2,1,0:T(8,128)(2,1)}, bf16[20,576,128]{2,1,0:T(8,128)(2,1)}, f32[16,512,128]{2,1,0:T(8,128)}, bf16[18,544,128]{2,1,0:T(8,128)(...) custom-call(s32[4]{0:T(128)} %pad_add_fusion.meta, bf16[16,608,128]{2,1,0:T(8,128)(2,1)} %get-tuple-element.41.fxi, ...), custom_call_target="tpu_custom_call" | custom-call | bytes 1048576 | tf_op jit(solution)/shard_map/pallas_call | solution.py:547
  45.3 0.8 copy-done.1
  46.1 0.2 copy-done.2
  46.3 10.6 %shard_map.72 = (bf16[20,576,128]{2,1,0:T(8,128)(2,1)}, f32[16,512,128]{2,1,0:T(8,128)}, bf16[18,544,128]{2,1,0:T(8,128)(2,1)}, f32[16,512,128]{2,1,0:T(8,128)}, bf16[2,3,3,128,128]{4,3,2,1,0:T(8,128)(2,1)}) custom-call(s32[4]{0:T(128)} %pad_add_fusion.meta, ...), custom_call_target="tpu_custom_call", output_to_operand_aliasing={{0}: (9, {}), {1}: (10, {}), {2}: (11, {}), {3}: (12, {})} | custom-call | bytes 1048576 | tf_op jit(solution)/shard_map/pallas_call | solution.py:576
  56.9 6.1 %all-to-all-start = ((bf16[32,72,128]{2,1,0:T(8,128)(2,1)}), bf16[32,72,128]{2,1,0:T(8,128)(2,1)S(1)}, u32[]{:S(2)}, u32[]{:S(2)}) async-start(bf16[32,72,128]{2,1,0:T(8,128)(2,1)} %bitcast.15), calls=%async_computation | async-start | bytes 1179648 | tf_op jit(solution)/shard_map/all_to_all | solution.py:627
  63.0 3.7 %collective-permute-start.4 = (bf16[3,608,128]{2,1,0:T(8,128)(2,1)S(1)}, bf16[3,608,128]{2,1,0:T(8,128)(2,1)S(1)}, u32[]{:S(2)}, u32[]{:S(2)}) collective-permute-start(bf16[3,608,128]{2,1,0:T(8,128)(2,1)S(1)} %copy-done.8), channel_id=1, source_target_pairs={{0,4},{4,8},{8,12},{12,16},{16,20},{20,24},{24,28},{1,5},{5,9},{9,... | collective-permute-start | bytes 1400840 | tf_op jit(solution)/shard_map/ppermute | solution.py:487
  66.7 1.5 %collective-permute-start.5 = (bf16[3,608,128]{2,1,0:T(8,128)(2,1)S(1)}, bf16[3,608,128]{2,1,0:T(8,128)(2,1)S(1)}, u32[]{:S(2)}, u32[]{:S(2)}) collective-permute-start(bf16[3,608,128]{2,1,0:T(8,128)(2,1)S(1)} %copy-done.7), channel_id=1, source_target_pairs={{4,0},{8,4},{12,8},{16,12},{20,16},{24,20},{28,24},{5,1},{9,5},{13... | collective-permute-start | bytes 1400840 | tf_op jit(solution)/shard_map/ppermute | solution.py:487
  68.2 12.9 %shard_map.73 = (bf16[64,128,128]{2,1,0:T(8,128)(2,1)}, bf16[64,128,128]{2,1,0:T(8,128)(2,1)}) custom-call(s32[4]{0:T(128)} %pad_add_fusion.meta, bf16[16,608,128]{2,1,0:T(8,128)(2,1)} %get-tuple-element.41.fxi, bf16[1536,256]{1,0:T(8,128)(2,1)} %get-tuple-element.49.wc2, bf16[1536,256]{1,0:T(8,128)(2,1)} %get-tuple-element.50.wb1, ...), custom_call_target="tpu_custom_call" | custom-call | bytes 1048576 | tf_op jit(solution)/shard_map/pallas_call | solution.py:605
  81.2 0.0 copy-start
  81.2 0.8 copy-done
  82.0 2.0 %shard_map.75 = bf16[32,72,128]{2,1,0:T(8,128)(2,1)} custom-call(s32[4]{0:T(128)} %pad_add_fusion.meta, bf16[32,72,128]{2,1,0:T(8,128)(2,1)} %copy-done, bf16[64,128,128]{2,1,0:T(8,128)(2,1)} %get-tuple-element.60._out), custom_call_target="tpu_custom_call" | custom-call | bytes 2097152 | tf_op jit(solution)/shard_map/pallas_call | solution.py:628
  84.0 6.7 %all-to-all-start.1 = ((bf16[32,72,128]{2,1,0:T(8,128)(2,1)}), bf16[32,72,128]{2,1,0:T(8,128)(2,1)S(1)}, u32[]{:S(2)}, u32[]{:S(2)}) async-start(bf16[32,72,128]{2,1,0:T(8,128)(2,1)} %shard_map.75), calls=%async_computation.1 | async-start | bytes 1179648 | tf_op jit(solution)/shard_map/all_to_all | solution.py:636
  90.7 1.4 %shard_map.67.cm = f32[608,128]{1,0:T(8,128)} custom-call(s32[4]{0:T(128)} %pad_add_fusion.meta), custom_call_target="tpu_custom_call" | custom-call | flops 48318382080 | bytes 1048576 | tf_op jit(solution)/shard_map/pallas_call | solution.py:639
  92.2 0.8 copy-done.5
  92.9 0.2 copy-done.6
  93.1 10.2 %shard_map.74 = (bf16[64,128,128]{2,1,0:T(8,128)(2,1)}, bf16[64,128,128]{2,1,0:T(8,128)(2,1)}) custom-call(s32[4]{0:T(128)} %pad_add_fusion.meta, f32[608,128]{1,0:T(8,128)} %shard_map.67.cm, bf16[16,608,128]{2,1,0:T(8,128)(2,1)} %get-tuple-element.41.fxi, ...), custom_call_target="tpu_custom_call", output_to_operand_aliasing={{0}: (17, {}), {1}: (18, {})} | custom-call | flops 2415919104 | bytes 12582912 | tf_op jit(solution)/shard_map/pallas_call | solution.py:647
  103.3 4.2 %all-to-all-done.1 = bf16[32,72,128]{2,1,0:T(8,128)(2,1)S(1)} async-done(((bf16[32,72,128]{2,1,0:T(8,128)(2,1)}), bf16[32,72,128]{2,1,0:T(8,128)(2,1)S(1)}, u32[]{:S(2)}, u32[]{:S(2)}) %all-to-all-start.1) | async-done | bytes 589856 | tf_op jit(solution)/shard_map/all_to_all | solution.py:636
  107.5 1.1 %convert.1 = f32[2,3,3,128,128]{4,3,2,1,0:T(8,128)} convert(bf16[2,3,3,128,128]{4,3,2,1,0:T(8,128)(2,1)S(1)} %bitcast.14) | non-fusion elementwise | flops 294912 | bytes 1769472 | tf_op jit(solution)/shard_map/convert_element_type | solution.py:637
  (16 shorter events, 0.0 us)
Async XLA Ops:
  2.1 15.5 %collective-permute-start.1 = (bf16[2,64,16,128]{3,2,1,0:T(8,128)(2,1)S(1)}, bf16[2,64,16,128]{3,2,1,0:T(8,128)(2,1)S(1)}, u32[]{:S(2)}, u32[]{:S(2)}) collective-permute-start(bf16[2,64,16,128]{3,2,1,0:T(8,128)(2,1)S(1)} %pad_maximum_fusion.1), channel_id=1, source_target_pairs={{1,2},{2,1},{5,6},{6,5},{9,10},{10,9},{13,14},{14,13},{17,18},{18,... | collective-permute-start | bytes 1572872 | tf_op jit(solution)/shard_map/ppermute | solution.py:508
  2.9 14.7 %collective-permute-start = (bf16[2,64,16,128]{3,2,1,0:T(8,128)(2,1)S(1)}, bf16[2,64,16,128]{3,2,1,0:T(8,128)(2,1)S(1)}, u32[]{:S(2)}, u32[]{:S(2)}) collective-permute-start(bf16[2,64,16,128]{3,2,1,0:T(8,128)(2,1)S(1)} %pad_maximum_fusion), channel_id=1, source_target_pairs={{0,1},{1,0},{2,3},{3,2},{4,5},{5,4},{6,7},{7,6},{8,9},{9,8},{10,11... | collective-permute-start | bytes 1572872 | tf_op jit(solution)/shard_map/ppermute | solution.py:509
  17.6 0.8 copy-start.3
  17.6 1.0 copy-start.4
  21.3 24.0 %collective-permute-start.2 = (bf16[3,608,128]{2,1,0:T(8,128)(2,1)}, bf16[3,608,128]{2,1,0:T(8,128)(2,1)S(1)}, u32[]{:S(2)}, u32[]{:S(2)}) collective-permute-start(bf16[3,608,128]{2,1,0:T(8,128)(2,1)} %get-tuple-element.45), channel_id=1, source_target_pairs={{0,4},{4,8},{8,12},{12,16},{16,20},{20,24},{24,28},{1,5},{5,9},{9,... | collective-permute-start | bytes 1400840 | tf_op jit(solution)/shard_map/ppermute | solution.py:487
  24.7 20.6 %collective-permute-start.3 = (bf16[3,608,128]{2,1,0:T(8,128)(2,1)}, bf16[3,608,128]{2,1,0:T(8,128)(2,1)S(1)}, u32[]{:S(2)}, u32[]{:S(2)}) collective-permute-start(bf16[3,608,128]{2,1,0:T(8,128)(2,1)} %get-tuple-element.46), channel_id=1, source_target_pairs={{4,0},{8,4},{12,8},{16,12},{20,16},{24,20},{28,24},{5,1},{9,5},{13... | collective-permute-start | bytes 1400840 | tf_op jit(solution)/shard_map/ppermute | solution.py:487
  45.3 0.8 copy-start.1
  45.3 1.0 copy-start.2
  46.3 16.7 %copy-start.8 = (bf16[3,608,128]{2,1,0:T(8,128)(2,1)S(1)}, bf16[3,608,128]{2,1,0:T(8,128)(2,1)}, u32[]{:S(2)}) copy-start(bf16[3,608,128]{2,1,0:T(8,128)(2,1)} %get-tuple-element.47) | copy-start | bytes 1400836
  46.3 20.4 %copy-start.7 = (bf16[3,608,128]{2,1,0:T(8,128)(2,1)S(1)}, bf16[3,608,128]{2,1,0:T(8,128)(2,1)}, u32[]{:S(2)}) copy-start(bf16[3,608,128]{2,1,0:T(8,128)(2,1)} %get-tuple-element.48) | copy-start | bytes 1400836
  56.9 24.2 %all-to-all-start = ((bf16[32,72,128]{2,1,0:T(8,128)(2,1)}), bf16[32,72,128]{2,1,0:T(8,128)(2,1)S(1)}, u32[]{:S(2)}, u32[]{:S(2)}) async-start(bf16[32,72,128]{2,1,0:T(8,128)(2,1)} %bitcast.15), calls=%async_computation | async-start | bytes 1179648 | tf_op jit(solution)/shard_map/all_to_all | solution.py:627
  63.0 29.2 %collective-permute-start.4 = (bf16[3,608,128]{2,1,0:T(8,128)(2,1)S(1)}, bf16[3,608,128]{2,1,0:T(8,128)(2,1)S(1)}, u32[]{:S(2)}, u32[]{:S(2)}) collective-permute-start(bf16[3,608,128]{2,1,0:T(8,128)(2,1)S(1)} %copy-done.8), channel_id=1, source_target_pairs={{0,4},{4,8},{8,12},{12,16},{16,20},{20,24},{24,28},{1,5},{5,9},{9,... | collective-permute-start | bytes 1400840 | tf_op jit(solution)/shard_map/ppermute | solution.py:487
  66.7 25.5 %collective-permute-start.5 = (bf16[3,608,128]{2,1,0:T(8,128)(2,1)S(1)}, bf16[3,608,128]{2,1,0:T(8,128)(2,1)S(1)}, u32[]{:S(2)}, u32[]{:S(2)}) collective-permute-start(bf16[3,608,128]{2,1,0:T(8,128)(2,1)S(1)} %copy-done.7), channel_id=1, source_target_pairs={{4,0},{8,4},{12,8},{16,12},{20,16},{24,20},{28,24},{5,1},{9,5},{13... | collective-permute-start | bytes 1400840 | tf_op jit(solution)/shard_map/ppermute | solution.py:487
  81.2 0.8 copy-start
  84.0 23.4 %all-to-all-start.1 = ((bf16[32,72,128]{2,1,0:T(8,128)(2,1)}), bf16[32,72,128]{2,1,0:T(8,128)(2,1)S(1)}, u32[]{:S(2)}, u32[]{:S(2)}) async-start(bf16[32,72,128]{2,1,0:T(8,128)(2,1)} %shard_map.75), calls=%async_computation.1 | async-start | bytes 1179648 | tf_op jit(solution)/shard_map/all_to_all | solution.py:636
  92.2 0.8 copy-start.5
  92.2 0.9 copy-start.6

commit v3 on v2

--- a/solution.py
+++ b/solution.py
@@ -87,23 +87,23 @@
     return lax.dot_general(left, right, (((0,), (0,)), ((), ())), preferred_element_type=F32)
 
 
-def pack_kernel(k_ref, *w_refs):
+def pack_kernel(k_ref, conv_ref, back_ref, *, conv_layer, back_layer):
     zero = jnp.zeros((C, C), BF16)
-    for layer in range(2):
-        for back in range(2):
-            def tap(p, q):
-                if back:
-                    return k_ref[layer, 2 - p, 2 - q].T
-                return k_ref[layer, p, q]
-
-            w_ref = w_refs[2 * layer + back]
-            for q in range(3):
-                t0, t1, t2 = tap(0, q), tap(1, q), tap(2, q)
-                o = 4 * C * q
-                blocks = ((t1, t0), (t2, t1), (t0, zero), (zero, t2))
-                for i, (x, y) in enumerate(blocks):
-                    w_ref[o + C * i : o + C * (i + 1), :C] = x
-                    w_ref[o + C * i : o + C * (i + 1), C:] = y
+
+    def conv_tap(p, q):
+        return k_ref[conv_layer, p, q]
+
+    def back_tap(p, q):
+        return k_ref[back_layer, 2 - p, 2 - q].T
+
+    for tap, w_ref in ((conv_tap, conv_ref), (back_tap, back_ref)):
+        for q in range(3):
+            t0, t1, t2 = tap(0, q), tap(1, q), tap(2, q)
+            o = 4 * C * q
+            blocks = ((t1, t0), (t2, t1), (t0, zero), (zero, t2))
+            for i, (x, y) in enumerate(blocks):
+                w_ref[o + C * i : o + C * (i + 1), :C] = x
+                w_ref[o + C * i : o + C * (i + 1), C:] = y
 
 
 def layout_kernel(meta, f_ref, g_ref, fx, gx, ua, da, ub, db, *, step, nj, na):
@@ -142,7 +142,7 @@
                 out[t, own] = rows[t][own]
 
 
-def halo_kernel(meta, ev_ref, od_ref, _w, *refs, nj, na):
+def halo_kernel(meta, ev_ref, od_ref, *refs, nj, na):
     fx, gx, ua, da, ub, db, buf, sem = refs[6:]
     m0 = 16 * nj
     odd = meta[3] == 1
@@ -192,27 +192,31 @@
 
 
 def inner_kernel(
-    meta, fxi, gxi, wc, wb, a1o, a2o, so, g1o, gfo, acc_o,
+    meta, fxi, gxi, wc, wb, _ub, _db, a1o, a2o, so, g1o, gfo, acc_o, _ubo, _dbo,
     fx, gx, a1, a2, st, es, g1, gf, cm, sem, insem, *, na, nj,
 ):
     m0, m1, m2, w = 16 * nj, 16 * (nj + 2), 16 * (nj + 4), 16 * (nj + 6)
     ni = na - 4
     jobs = []
     go = copier(insem, jobs)
-    go(fxi, fx)
+    group = na // 4
+    for i in range(4):
+        go(fxi.at[pl.ds(group * i, group)], fx.at[pl.ds(group * i, group)])
     go(gxi, gx)
     cm[...] = column_mask(meta, nj)
-    jobs[0].wait()
 
     def activate(a, _):
         v, _e = elu_parts(fx[a].astype(F32))
         a1[a] = (v * live(meta, cm, a, 0, w)).astype(BF16)
         return 0
 
-    lax.fori_loop(0, na, activate, 0)
+    for i in range(4):
+        jobs[i].wait()
+        lax.fori_loop(group * i, group * (i + 1), activate, 0)
     out_a1 = pltpu.make_async_copy(a1, a1o, sem.at[0])
     out_a1.start()
-    jobs[1].wait()
+    for c in jobs[4:]:
+        c.wait()
 
     def quad(t, _):
         r = 2 + 4 * t
@@ -235,7 +239,8 @@
                 gf[row - 2] = full[16 : 16 + m0]
         return 0
 
-    lax.fori_loop(0, ni // 4, quad, 0)
+    for t in range(ni // 4):
+        quad(t, 0)
     copies = [
         pltpu.make_async_copy(a2.at[pl.ds(4, ni)], a2o.at[pl.ds(4, ni)], sem.at[1]),
         pltpu.make_async_copy(st, so.at[pl.ds(2, ni)], sem.at[2]),
@@ -272,8 +277,8 @@
 
 
 def edge_kernel(
-    meta, fxi, gxi, a1i, up, dn, wc, wb, acc_i, _a2, _s, _g1, _gf, a2o, so, g1o, gfo, kg,
-    a1, g, f, fh, a2, st, es, g1, gf, cm, sem, *, na, nj,
+    meta, fxi, gxi, a1i, up, dn, wc, wb, acc_i, _a2, _s, _g1, _gf, a2o, so, g1o, gfo, keep, send,
+    a1, g, f, fh, a2, st, es, g1, gf, cm, kg, sem, *, na, nj,
 ):
     m0, m1, m2, w = 16 * nj, 16 * (nj + 2), 16 * (nj + 4), 16 * (nj + 6)
     jobs = []
@@ -281,21 +286,20 @@
     go = copier(sem, jobs)
     go(up.at[pl.ds(0, 1)], fh.at[0])
     go(dn.at[pl.ds(0, 1)], fh.at[1])
+    go(a1i.at[pl.ds(0, 3)], a1.at[0, pl.ds(1, 3)])
+    go(a1i.at[pl.ds(na - 3, 3)], a1.at[1, pl.ds(0, 3)])
+    go(fxi.at[pl.ds(0, 2)], f.at[0])
+    go(fxi.at[pl.ds(na - 2, 2)], f.at[1])
     go(up.at[pl.ds(1, 2)], g.at[0, pl.ds(0, 2)])
     go(gxi.at[pl.ds(0, 6)], g.at[0, pl.ds(2, 6)])
     go(gxi.at[pl.ds(na - 6, 6)], g.at[1, pl.ds(0, 6)])
     go(dn.at[pl.ds(1, 2)], g.at[1, pl.ds(6, 2)])
-    go(a1i.at[pl.ds(0, 3)], a1.at[0, pl.ds(1, 3)])
-    go(a1i.at[pl.ds(na - 3, 3)], a1.at[1, pl.ds(0, 3)])
-    go(fxi.at[pl.ds(0, 2)], f.at[0])
-    go(fxi.at[pl.ds(na - 2, 2)], f.at[1])
     cm[...] = column_mask(meta, nj)
     for c in jobs:
         c.wait()
     for s, row, slot in ((0, -1, 0), (1, na, 3)):
         v, _e = elu_parts(fh[s, 0].astype(F32))
         a1[s, slot] = (v * live(meta, cm, row, 0, w)).astype(BF16)
-
     acc = conv_pairs(lambda i, q: a1[i // 8, i % 8, 16 * q : 16 * q + m2], [1, 9], 1, wc[...])
     for s in range(2):
         for b in range(2):
@@ -330,7 +334,7 @@
         ]
         total = acc_i[1, C * p : C * (p + 1)] + outer(left, jnp.concatenate(right, axis=0))
         for q in range(3):
-            kg[1, 2 - p, 2 - q] = total[:, C * q : C * (q + 1)].astype(BF16)
+            kg[1, 3 * (2 - p) + 2 - q] = total[:, C * q : C * (q + 1)]
     left = jnp.concatenate([g1[s, b, 16 : 16 + m0] for s, b in rows], axis=0)
     for p in range(3):
         right = [
@@ -338,7 +342,10 @@
         ]
         total = acc_i[0, C * p : C * (p + 1)] + outer(left, jnp.concatenate(right, axis=0))
         for q in range(3):
-            kg[0, p, q] = total[:, C * q : C * (q + 1)].T.astype(BF16)
+            kg[0, 3 * p + q] = total[:, C * q : C * (q + 1)].T
+    mine = meta[3]
+    keep[...] = kg[mine]
+    send[...] = kg[1 - mine].astype(BF16)
     for c in jobs[outs:]:
         c.wait()
 
@@ -352,22 +359,39 @@
         put(1, row, from_blocks(grads(row) + mask * slope * acc1(row)))
 
 
-def middle_kernel(meta, fxi, wc2, wb1, a2i, si, g1i, gfi, out, fg, fm, a2, st, g1, gf, cm, ot, ft, sem, osem, *, na, nj):
+def middle_kernel(
+    meta, fxi, wc2i, wb1i, a2i, si, g1i, gfi, out, fg,
+    fm, a2, st, g1, gf, cm, ot, ft, wc2, wb1, sem, osem, *, na, nj,
+):
     m0 = 16 * nj
     ni = na - 4
+    quads = ni // 4
     jobs = []
     go = copier(sem, jobs)
-    go(a2i.at[pl.ds(2, na)], a2)
-    go(g1i.at[pl.ds(2, na - 2)], g1)
-    go(si.at[pl.ds(2, ni)], st)
-    go(fxi.at[pl.ds(2, ni), pl.ds(16 * H, m0)], fm)
-    go(gfi.at[pl.ds(2, ni)], gf)
+
+    def later(t, first, per):
+        return (0, first) if t == 0 else (first + per * (t - 1), per)
+
+    go(wc2i, wc2)
+    go(wb1i, wb1)
+    for t in range(quads):
+        r, n = later(t, 8, 4)
+        go(a2i.at[pl.ds(2 + r, n)], a2.at[pl.ds(r, n)])
+        r, n = later(t, 6, 4)
+        go(g1i.at[pl.ds(2 + r, n)], g1.at[pl.ds(r, n)])
+        here, there = pl.ds(4 * t, 4), pl.ds(2 + 4 * t, 4)
+        go(si.at[there], st.at[here])
+        go(fxi.at[there, pl.ds(16 * H, m0)], fm.at[here])
+        go(gfi.at[there], gf.at[here])
     cm[...] = column_mask(meta, nj)
-    for c in jobs:
+    for c in jobs[:2]:
         c.wait()
 
     def quad(t, _):
         r = 2 + 4 * t
+        if t < 2:
+            for c in jobs[2:7] if t == 0 else jobs[7:]:
+                c.wait()
         acc2 = conv_pairs(lambda row, q: a2[row, pl.ds(32 * q, m0), :], [r, r + 1], 2, wc2[...])
         acc1 = conv_pairs(lambda row, q: g1[row - 1, pl.ds(16 * q, m0), :], [r, r + 2], 1, wb1[...])
 
@@ -388,7 +412,8 @@
         pltpu.make_async_copy(ft.at[here], fg.at[there], osem.at[1]).start()
         return 0
 
-    lax.fori_loop(0, ni // 4, quad, 0)
+    for t in range(ni // 4):
+        quad(t, 0)
     pltpu.make_async_copy(ot, out.at[pl.ds(8, 4 * ni)], osem.at[0]).wait()
     pltpu.make_async_copy(ft, fg.at[pl.ds(8, 4 * ni)], osem.at[1]).wait()
 
@@ -398,8 +423,8 @@
 
 
 def last_kernel(
-    meta, cm, fxi, gxi, a1i, upa, dna, upb, dnb, wc, wb, wc2, wb1, a2i, si, g1i, gfi, _out, _fg, out, fg,
-    a1, g, f, fm, a2, st, es, g1, gf, ot, ft, sem, *, na, nj,
+    meta, cm, fxi, gxi, a1i, upa, dna, upb, dnb, wci, wbi, wc2i, wb1i, a2i, si, g1i, gfi, _out, _fg, out, fg,
+    a1, g, f, fm, a2, st, es, g1, gf, ot, ft, wc, wb, wc2, wb1, sem, *, na, nj,
 ):
     m0, m1, m2, w = 16 * nj, 16 * (nj + 2), 16 * (nj + 4), 16 * (nj + 6)
     jobs = []
@@ -418,7 +443,11 @@
     go(dnb.at[pl.ds(2, 1)], g.at[1, pl.ds(3, 1)])
     go(a1i.at[pl.ds(0, 1)], a1.at[0, pl.ds(3, 1)])
     go(a1i.at[pl.ds(na - 1, 1)], a1.at[1, pl.ds(0, 1)])
+    go(wci, wc)
+    go(wbi, wb)
     early = len(jobs)
+    go(wc2i, wc2)
+    go(wb1i, wb1)
     go(a2i.at[pl.ds(2, 6)], a2.at[0, pl.ds(2, 6)])
     go(a2i.at[pl.ds(na - 4, 6)], a2.at[1, pl.ds(0, 6)])
     go(g1i.at[pl.ds(1, 3)], g1.at[0, pl.ds(1, 3)])
@@ -482,6 +511,24 @@
     o_ref[...] = jnp.broadcast_to(total.astype(BF16)[None], o_ref.shape)
 
 
+def hold_kernel(x_ref, o_ref):
+    del x_ref, o_ref
+
+
+def after_kernel(x_ref, _out, o_ref):
+    o_ref[...] = x_ref[...]
+
+
+def join_kernel(meta, mine_ref, other_ref, o_ref):
+    mine = meta[3]
+    o_ref[mine] = mine_ref[...].astype(F32)
+    o_ref[1 - mine] = other_ref[...].astype(F32)
+
+
+def in_hbm(*arrays):
+    return [pltpu.with_memory_space_constraint(x, pltpu.HBM) for x in arrays]
+
+
 def shift(x, axis, step):
     n = lax.axis_size(axis)
     return lax.ppermute(x, axis, [(i, i + step) for i in range(n) if 0 <= i + step < n])
@@ -507,17 +554,22 @@
     outer_pairs = [(i, i + 1) for i in range(1, n - 1, 2)]
     od = lax.ppermute(edges(far), "col", outer_pairs + [(j, i) for i, j in outer_pairs])
     ev = lax.ppermute(edges(near), "col", inner)
-    w_one, w_one_back, w_two, w_two_back = pl.pallas_call(
-        pack_kernel,
-        in_specs=[VMEM],
-        out_specs=[VMEM] * 4,
-        out_shape=[sds((12 * C, 2 * C), BF16)] * 4,
-        compiler_params=params(56),
-        cost_estimate=cost(0, 8 << 20),
-    )(kernels)
+
+    def pack(conv_layer, back_layer, space):
+        return pl.pallas_call(
+            functools.partial(pack_kernel, conv_layer=conv_layer, back_layer=back_layer),
+            in_specs=[VMEM],
+            out_specs=[VMEM] * 2,
+            out_shape=[space((12 * C, 2 * C), BF16)] * 2,
+            compiler_params=params(12),
+            cost_estimate=cost(0, 8 << 20),
+        )(kernels)
+
+    w_one, w_two_back = pack(0, 1, sds)
+    w_two, w_one_back = pack(1, 0, pltpu.HBM)
     step = 4
     row_block = pl.BlockSpec((4 * step, cols, C), lambda i: (i, 0, 0))
-    shapes = [sds((na, w, C), BF16)] * 2 + [sds((3, w, C), BF16)] * 4
+    shapes = [pltpu.HBM((na, w, C), BF16)] * 2 + [pltpu.HBM((3, w, C), BF16)] * 4
     extended = pl.pallas_call(
         functools.partial(layout_kernel, step=step, nj=nj, na=na),
         grid=(na // step,),
@@ -527,34 +579,34 @@
         out_shape=shapes,
         compiler_params=params(56),
         cost_estimate=cost(0, 12 << 20),
-    )(meta, features, cotangent)
+    )(meta, *in_hbm(features, cotangent))
     fx, gx, ua, da, ub, db = pl.pallas_call(
         functools.partial(halo_kernel, nj=nj, na=na),
-        in_specs=[SMEM, VMEM, VMEM, ANY] + [ANY] * 6,
+        in_specs=[SMEM, VMEM, VMEM] + [ANY] * 6,
         out_specs=[ANY] * 6,
         out_shape=shapes,
         scratch_shapes=[pltpu.VMEM((2, 2, na, 16 * H, C), BF16), pltpu.SemaphoreType.DMA((20,))],
-        input_output_aliases={4 + i: i for i in range(6)},
-        compiler_params=params(56),
+        input_output_aliases={3 + i: i for i in range(6)},
+        compiler_params=params(12),
         cost_estimate=cost(0, 4 << 20),
-    )(meta, ev, od, w_one, *extended)
+    )(meta, ev, od, *extended)
     dna = shift(ua, "row", -1)
     upa = shift(da, "row", 1)
-    dnb = shift(ub, "row", -1)
-    upb = shift(db, "row", 1)
 
     conv_flops = 2 * rows * cols * 9 * C * C
-    a1, a2, st, g1, gf, acc = pl.pallas_call(
+    a1, a2, st, g1, gf, acc, ub, db = pl.pallas_call(
         functools.partial(inner_kernel, na=na, nj=nj),
-        in_specs=[SMEM] + [ANY] * 2 + [VMEM] * 2,
-        out_specs=[ANY] * 5 + [VMEM],
+        in_specs=[SMEM] + [ANY] * 2 + [VMEM] * 2 + [ANY] * 2,
+        out_specs=[ANY] * 5 + [VMEM] + [ANY] * 2,
         out_shape=[
-            sds((na, w, C), BF16),
-            sds((na + 4, m2, C), BF16),
-            sds((na, m0, C), F32),
-            sds((na + 2, m1, C), BF16),
-            sds((na, m0, C), F32),
+            pltpu.HBM((na, w, C), BF16),
+            pltpu.HBM((na + 4, m2, C), BF16),
+            pltpu.HBM((na, m0, C), F32),
+            pltpu.HBM((na + 2, m1, C), BF16),
+            pltpu.HBM((na, m0, C), F32),
             sds((2, 3 * C, 3 * C), F32),
+            pltpu.HBM((3, w, C), BF16),
+            pltpu.HBM((3, w, C), BF16),
         ],
         scratch_shapes=[
             pltpu.VMEM((na, w, C), BF16),
@@ -567,22 +619,26 @@
             pltpu.VMEM((ni, m0, C), F32),
             pltpu.VMEM((w, C), F32),
             pltpu.SemaphoreType.DMA((5,)),
-            pltpu.SemaphoreType.DMA((2,)),
+            pltpu.SemaphoreType.DMA((5,)),
         ],
-        compiler_params=params(56),
+        input_output_aliases={5: 6, 6: 7},
+        compiler_params=params(36),
         cost_estimate=cost(0, 1 << 20),
-    )(meta, fx, gx, w_one, w_two_back)
-
-    a2, st, g1, gf, kg = pl.pallas_call(
+    )(meta, *in_hbm(fx, gx), w_one, w_two_back, *in_hbm(ub, db))
+    dnb = shift(ub, "row", -1)
+    upb = shift(db, "row", 1)
+
+    a2, st, g1, gf, keep, send = pl.pallas_call(
         functools.partial(edge_kernel, na=na, nj=nj),
-        in_specs=[SMEM] + [ANY] * 2 + [ANY] + [ANY] * 2 + [VMEM] * 3 + [ANY] * 4,
-        out_specs=[ANY] * 4 + [VMEM],
+        in_specs=[SMEM] + [ANY] * 5 + [VMEM] * 3 + [ANY] * 4,
+        out_specs=[ANY] * 4 + [VMEM] * 2,
         out_shape=[
-            sds((na + 4, m2, C), BF16),
-            sds((na, m0, C), F32),
-            sds((na + 2, m1, C), BF16),
-            sds((na, m0, C), F32),
-            sds((2, 3, 3, C, C), BF16),
+            pltpu.HBM((na + 4, m2, C), BF16),
+            pltpu.HBM((na, m0, C), F32),
+            pltpu.HBM((na + 2, m1, C), BF16),
+            pltpu.HBM((na, m0, C), F32),
+            sds((9, C, C), F32),
+            sds((9, C, C), BF16),
         ],
         scratch_shapes=[
             pltpu.VMEM((2, 4, w, C), BF16),
@@ -595,18 +651,19 @@
             pltpu.VMEM((2, 2, m1, C), BF16),
             pltpu.VMEM((2, 2, m0, C), F32),
             pltpu.VMEM((w, C), F32),
+            pltpu.VMEM((2, 9, C, C), F32),
             pltpu.SemaphoreType.DMA((18,)),
         ],
         input_output_aliases={9: 0, 10: 1, 11: 2, 12: 3},
-        compiler_params=params(56),
+        compiler_params=params(24),
         cost_estimate=cost(0, 1 << 20),
-    )(meta, fx, gx, a1, upa, dna, w_one, w_two_back, acc, a2, st, g1, gf)
+    )(meta, *in_hbm(fx, gx, a1), upa, dna, w_one, w_two_back, acc, *in_hbm(a2, st, g1, gf))
 
     out, fg = pl.pallas_call(
         functools.partial(middle_kernel, na=na, nj=nj),
-        in_specs=[SMEM, ANY] + [VMEM] * 2 + [ANY] * 4,
+        in_specs=[SMEM] + [ANY] * 7,
         out_specs=[ANY] * 2,
-        out_shape=[sds(features.shape, BF16)] * 2,
+        out_shape=[pltpu.HBM(features.shape, BF16)] * 2,
         scratch_shapes=[
             pltpu.VMEM((ni, m0, C), BF16),
             pltpu.VMEM((na, m2, C), BF16),
@@ -616,39 +673,52 @@
             pltpu.VMEM((w, C), F32),
             pltpu.VMEM((4 * ni, cols, C), BF16),
             pltpu.VMEM((4 * ni, cols, C), BF16),
-            pltpu.SemaphoreType.DMA((5,)),
+            pltpu.VMEM((12 * C, 2 * C), BF16),
+            pltpu.VMEM((12 * C, 2 * C), BF16),
+            pltpu.SemaphoreType.DMA((2 + 5 * (ni // 4),)),
             pltpu.SemaphoreType.DMA((2,)),
         ],
-        compiler_params=params(56),
-        cost_estimate=cost(0, 1 << 20),
-    )(meta, fx, w_two, w_one_back, a2, st, g1, gf)
+        compiler_params=params(28),
+        cost_estimate=cost(20 * conv_flops, 24 << 20),
+    )(meta, *in_hbm(fx, w_two, w_one_back), *in_hbm(a2, st, g1, gf))
+    received = lax.ppermute(send, "col", inner)
     axes = ("row", "col")
-    parts = lax.axis_size(axes)
-    shares = lax.all_to_all(kg.reshape(parts, -1, C), axes, 0, 0, tiled=True)
+    groups = [
+        [r * n + c for r in range(lax.axis_size("row")) for c in range(side, n, 2)] for side in range(2)
+    ]
+    keep = pl.pallas_call(
+        hold_kernel,
+        in_specs=[ANY],
+        out_specs=ANY,
+        out_shape=sds((9, C, C), F32),
+        input_output_aliases={0: 0},
+        compiler_params=params(10),
+        cost_estimate=cost(20 * conv_flops, 1 << 20),
+    )(keep)
+    share = (keep + received.astype(F32)).astype(BF16).reshape(len(groups[0]), -1, C)
+    shares = lax.all_to_all(share, axes, 0, 0, axis_index_groups=groups, tiled=True)
     spread = pl.pallas_call(
         sum_kernel,
         in_specs=[SMEM, VMEM, ANY],
         out_specs=VMEM,
         out_shape=sds(shares.shape, BF16),
-        compiler_params=params(56),
+        compiler_params=params(10),
         cost_estimate=cost(0, 2 << 20),
-    )(meta, shares, out)
-    whole = lax.all_to_all(spread, axes, 0, 0, tiled=True)
-    kernel_gradient = whole.reshape(kernels.shape).astype(F32)
-
+    )(meta, shares, *in_hbm(out))
+    mine = lax.all_to_all(spread, axes, 0, 0, axis_index_groups=groups, tiled=True).reshape(9, C, C)
     cm = pl.pallas_call(
         functools.partial(mask_kernel, nj=nj),
         in_specs=[SMEM],
         out_specs=VMEM,
         out_shape=sds((w, C), F32),
-        compiler_params=params(56),
-        cost_estimate=cost(20 * conv_flops, 1 << 20),
+        compiler_params=params(8),
+        cost_estimate=cost(0, 1 << 20),
     )(meta)
     out, fg = pl.pallas_call(
         functools.partial(last_kernel, na=na, nj=nj),
-        in_specs=[SMEM, VMEM] + [ANY] * 7 + [VMEM] * 4 + [ANY] * 6,
+        in_specs=[SMEM, VMEM] + [ANY] * 17,
         out_specs=[ANY] * 2,
-        out_shape=[sds(features.shape, BF16)] * 2,
+        out_shape=[pltpu.HBM(features.shape, BF16)] * 2,
         scratch_shapes=[
             pltpu.VMEM((2, 4, w, C), BF16),
             pltpu.VMEM((2, 4, w, C), BF16),
@@ -661,12 +731,34 @@
             pltpu.VMEM((2, 2, m0, C), F32),
             pltpu.VMEM((2, 8, cols, C), BF16),
             pltpu.VMEM((2, 8, cols, C), BF16),
-            pltpu.SemaphoreType.DMA((28,)),
+            pltpu.VMEM((12 * C, 2 * C), BF16),
+            pltpu.VMEM((12 * C, 2 * C), BF16),
+            pltpu.VMEM((12 * C, 2 * C), BF16),
+            pltpu.VMEM((12 * C, 2 * C), BF16),
+            pltpu.SemaphoreType.DMA((32,)),
         ],
         input_output_aliases={17: 0, 18: 1},
-        compiler_params=params(56),
-        cost_estimate=cost(conv_flops, 12 << 20),
-    )(meta, cm, fx, gx, a1, upa, dna, upb, dnb, w_one, w_two_back, w_two, w_one_back, a2, st, g1, gf, out, fg)
+        compiler_params=params(24),
+        cost_estimate=cost(20 * conv_flops, 24 << 20),
+    )(meta, cm, *in_hbm(fx, gx, a1), upa, dna, upb, dnb, w_one, w_two_back, *in_hbm(w_two, w_one_back, a2, st, g1, gf, out, fg))
+    mine = pl.pallas_call(
+        after_kernel,
+        in_specs=[VMEM, ANY],
+        out_specs=VMEM,
+        out_shape=sds((9, C, C), BF16),
+        compiler_params=params(10),
+        cost_estimate=cost(0, 1 << 20),
+    )(mine, *in_hbm(out))
+    other = lax.ppermute(mine, "col", inner)
+    kernel_gradient = pl.pallas_call(
+        join_kernel,
+        in_specs=[SMEM, VMEM, VMEM],
+        out_specs=VMEM,
+        out_shape=sds((2, 9, C, C), F32),
+        compiler_params=params(10),
+        cost_estimate=cost(0, 2 << 20),
+    )(meta, mine, other).reshape(kernels.shape)
+
     return out, fg, kernel_gradient
 
 

time: 109 us -> 98.1 us (0.90)
  Pallas kernels: 68.1 us -> 57.6 us
  local copies, waits for them, and re-layouts: 5.09 us -> 1.41 us
  starting transfers between devices: 27.9 us -> 30.5 us
    unnamed x18 -> x4, local copies, waits for them, and re-layouts: 3.69 us -> 0.01 us
    ppermute x0 -> x2, waiting for transfers between devices: none -> 3.13 us  [the longest x1 1.57 us: body(): other = lax.ppermute(mine, 'col', inner)]
    pallas_call x1, Pallas kernels: 19 us -> 16.2 us  [body(): pl.pallas_call(functools.partial(inner_kernel, na=na, nj=nj), in_specs=[S...]
    pallas_call x1, Pallas kernels: 12.9 us -> 10.4 us  [body(): pl.pallas_call(functools.partial(middle_kernel, na=na, nj=nj), in_specs=[...]
    all_to_all x2, waiting for transfers between devices: 4.17 us -> 1.9 us  [the longest x1 1.3 us: body(): lax.all_to_all(spread, axes, 0, 0, axis_index_groups=groups, tiled=True)]
    pallas_call x1, Pallas kernels: 10.6 us -> 8.57 us  [body(): pl.pallas_call(functools.partial(edge_kernel, na=na, nj=nj), in_specs=[SM...]
    ppermute x4, starting transfers between devices: 10.1 us -> 11.5 us  [shift(): lax.ppermute(x, axis, [(i, i + step) for i in range(n) if 0 <= i + step <...]
    pallas_call x1 -> x5, Pallas kernels: 2.96 us -> 3.29 us  [the longest x2 1.63 us: pack(): pl.pallas_call(functools.partial(pack_kernel, conv_layer=conv_layer, back...]
  transfers between devices with their start and end apart: 8 -> 10, of which waited for: 1 -> 4; matrix products, arithmetic and copies ran while one was open for 1% -> 2% of each run, Pallas kernels for 50% -> 55%
where the time goes in v3:
time: 98.1 us; the launch traced here: 97.6 us
  Pallas kernels  57.6 us (59%)
  starting transfers between devices  30.5 us (31%)
  waiting for transfers between devices  5.04 us (5%)
  other arithmetic  1.54 us (2%)
  between operations  1.52 us (2%)
  local copies, waits for them, and re-layouts  1.41 us (1%)
    pallas_call x1, Pallas kernels, body(): pl.pallas_call(functools.partial(inner_kernel, na=na, nj=nj), in_specs=[S...  16.2 us
    ppermute x4, starting transfers between devices, shift(): lax.ppermute(x, axis, [(i, i + step) for i in range(n) if 0 <= i + step <...  11.5 us
    pallas_call x1, Pallas kernels, body(): pl.pallas_call(functools.partial(middle_kernel, na=na, nj=nj), in_specs=[...  10.4 us
    pallas_call x1, Pallas kernels, body(): pl.pallas_call(functools.partial(last_kernel, na=na, nj=nj), in_specs=[SM...  9.08 us
    pallas_call x1, Pallas kernels, body(): pl.pallas_call(functools.partial(edge_kernel, na=na, nj=nj), in_specs=[SM...  8.57 us
    all_to_all x1, starting transfers between devices, body(): lax.all_to_all(share, axes, 0, 0, axis_index_groups=groups, tiled=True)  7.43 us
    all_to_all x1, starting transfers between devices, body(): lax.all_to_all(spread, axes, 0, 0, axis_index_groups=groups, tiled=True)  6.33 us
    pallas_call x1, Pallas kernels, body(): pl.pallas_call(functools.partial(layout_kernel, step=step, nj=nj, na=na),...  6.15 us
  transfers between devices with their start and end apart: 10, of which 4 were waited for; matrix products, arithmetic and copies ran while one was open for 2% of the time, Pallas kernels for 55%

profile of v3, /device:TPU:0, one launch (start us, length us, event | category | flops | bytes accessed | tf_op | source)
XLA Modules:
  0.0 97.6 jit_solution(1265283040885824436)
XLA Ops:
  0.6 1.4 %dynamic-slice_bitcast_fusion = (bf16[1,64,16,128]{3,2,1,0:T(8,128)(2,1)S(1)}, bf16[1,64,16,128]{3,2,1,0:T(8,128)(2,1)S(1)}, bf16[1,64,16,128]{3,2,1,0:T(8,128)(2,1)S(1)}, bf16[1,64,16,128]{3,2,1,0:T(8,128)(2,1)S(1)}) fusion(bf16[64,128,128]{2,1,0:T(8,128)(2,1)} %g_ref.1, s32[]{:T(128)S(6)} %select_n.12, s32[]{:T(128)S(6)} %select_n.11, ...), kind=kLoop, calls=%fused_computation.3 | loop fusion | bytes 2097160 | tf_op jit(solution)/shard_map/stack | solution.py:550
  2.0 0.1 pad_maximum_fusion.1
  2.1 0.7 collective-permute-start.1
  2.8 0.1 pad_maximum_fusion
  2.9 4.4 %collective-permute-start = (bf16[2,64,16,128]{3,2,1,0:T(8,128)(2,1)S(1)}, bf16[2,64,16,128]{3,2,1,0:T(8,128)(2,1)S(1)}, u32[]{:S(2)}, u32[]{:S(2)}) collective-permute-start(bf16[2,64,16,128]{3,2,1,0:T(8,128)(2,1)S(1)} %pad_maximum_fusion), channel_id=1, source_target_pairs={{0,1},{1,0},{2,3},{3,2},{4,5},{5,4},{6,7},{7,6},{8,9},{9,8},{10,11... | collective-permute-start | bytes 1572872 | tf_op jit(solution)/shard_map/ppermute | solution.py:556
  7.9 0.7 pad_add_fusion.meta
  8.6 6.1 %shard_map.68 = (bf16[16,608,128]{2,1,0:T(8,128)(2,1)}, bf16[16,608,128]{2,1,0:T(8,128)(2,1)}, bf16[3,608,128]{2,1,0:T(8,128)(2,1)}, bf16[3,608,128]{2,1,0:T(8,1...) custom-call(s32[4]{0:T(128)} %pad_add_fusion.meta, bf16[64,128,128]{2,1,0:T(8,128)(2,1)} %f_ref.1, ...), custom_call_target="tpu_custom_call" | custom-call | bytes 12582912 | tf_op jit(solution)/shard_map/pallas_call | solution.py:573
  14.7 0.0 collective-permute-done.1.od_ref
  14.7 0.0 copy-start
  14.7 2.1 %shard_map.69 = (bf16[16,608,128]{2,1,0:T(8,128)(2,1)}, bf16[16,608,128]{2,1,0:T(8,128)(2,1)}, bf16[3,608,128]{2,1,0:T(8,128)(2,1)}, bf16[3,608,128]{2,1,0:T(8,1...) custom-call(s32[4]{0:T(128)S(1)} %copy-done.1, ...), custom_call_target="tpu_custom_call", output_to_operand_aliasing={{0}: (3, {}), {1}: (4, {}), {2}: (5, {}), {3}: (6, {}), {4}... | custom-call | bytes 4194304 | tf_op jit(solution)/shard_map/pallas_call | solution.py:583
  16.8 3.4 %collective-permute-start.2 = (bf16[3,608,128]{2,1,0:T(8,128)(2,1)}, bf16[3,608,128]{2,1,0:T(8,128)(2,1)S(1)}, u32[]{:S(2)}, u32[]{:S(2)}) collective-permute-start(bf16[3,608,128]{2,1,0:T(8,128)(2,1)} %get-tuple-element.50), channel_id=1, source_target_pairs={{0,4},{4,8},{8,12},{12,16},{16,20},{20,24},{24,28},{1,5},{5,9},{9,... | collective-permute-start | bytes 1400840 | tf_op jit(solution)/shard_map/ppermute | solution.py:534
  20.3 1.3 %collective-permute-start.3 = (bf16[3,608,128]{2,1,0:T(8,128)(2,1)}, bf16[3,608,128]{2,1,0:T(8,128)(2,1)S(1)}, u32[]{:S(2)}, u32[]{:S(2)}) collective-permute-start(bf16[3,608,128]{2,1,0:T(8,128)(2,1)} %get-tuple-element.51), channel_id=1, source_target_pairs={{4,0},{8,4},{12,8},{16,12},{20,16},{24,20},{28,24},{5,1},{9,5},{13... | collective-permute-start | bytes 1400840 | tf_op jit(solution)/shard_map/ppermute | solution.py:534
  21.6 0.2 shard_map.70
  21.8 1.4 %shard_map.72 = (bf16[1536,256]{1,0:T(8,128)(2,1)}, bf16[1536,256]{1,0:T(8,128)(2,1)}) custom-call(bf16[2,3,3,128,128]{4,3,2,1,0:T(8,128)(2,1)S(1)} %copy-done), custom_call_target="tpu_custom_call" | custom-call | bytes 8388608 | tf_op jit(solution)/shard_map/pallas_call | solution.py:559
  23.2 0.6 shard_map.67.cm
  23.8 16.2 %shard_map.71 = (bf16[16,608,128]{2,1,0:T(8,128)(2,1)}, bf16[20,576,128]{2,1,0:T(8,128)(2,1)}, f32[16,512,128]{2,1,0:T(8,128)}, bf16[18,544,128]{2,1,0:T(8,128)(...) custom-call(s32[4]{0:T(128)S(1)} %copy-done.1, ...), custom_call_target="tpu_custom_call", output_to_operand_aliasing={{6}: (5, {}), {7}: (6, {})} | custom-call | bytes 1048576 | tf_op jit(solution)/shard_map/pallas_call | solution.py:597
  40.0 5.3 %collective-permute-start.4 = (bf16[3,608,128]{2,1,0:T(8,128)(2,1)}, bf16[3,608,128]{2,1,0:T(8,128)(2,1)}, u32[]{:S(2)}, u32[]{:S(2)}) collective-permute-start(bf16[3,608,128]{2,1,0:T(8,128)(2,1)} %get-tuple-element.52), channel_id=1, source_target_pairs={{0,4},{4,8},{8,12},{12,16},{16,20},{20,24},{24,28},{1,5},{5,9},{9,... | collective-permute-start | bytes 1400840 | tf_op jit(solution)/shard_map/ppermute | solution.py:534
  45.3 1.5 %collective-permute-start.5 = (bf16[3,608,128]{2,1,0:T(8,128)(2,1)}, bf16[3,608,128]{2,1,0:T(8,128)(2,1)}, u32[]{:S(2)}, u32[]{:S(2)}) collective-permute-start(bf16[3,608,128]{2,1,0:T(8,128)(2,1)} %get-tuple-element.53), channel_id=1, source_target_pairs={{4,0},{8,4},{12,8},{16,12},{20,16},{24,20},{28,24},{5,1},{9,5},{13... | collective-permute-start | bytes 1400840 | tf_op jit(solution)/shard_map/ppermute | solution.py:534
  46.8 8.6 %shard_map.73 = (bf16[20,576,128]{2,1,0:T(8,128)(2,1)}, f32[16,512,128]{2,1,0:T(8,128)}, bf16[18,544,128]{2,1,0:T(8,128)(2,1)}, f32[16,512,128]{2,1,0:T(8,128)},...) custom-call(s32[4]{0:T(128)S(1)} %copy-done.1, ...), custom_call_target="tpu_custom_call", output_to_operand_aliasing={{0}: (9, {}), {1}: (10, {}), {2}: (11, {}), {3}: (12, {})} | custom-call | bytes 1048576 | tf_op jit(solution)/shard_map/pallas_call | solution.py:631
  55.4 0.1 collective-permute-start.6
  55.5 1.6 %collective-permute-done.6 = bf16[9,128,128]{2,1,0:T(8,128)(2,1)S(1)} collective-permute-done((bf16[9,128,128]{2,1,0:T(8,128)(2,1)S(1)}, bf16[9,128,128]{2,1,0:T(8,128)(2,1)S(1)}, u32[]{:S(2)}, u32[]{:S(2)}) %collective-permute-start.6) | collective-permute-done | bytes 294944 | tf_op jit(solution)/shard_map/ppermute | solution.py:684
  57.0 0.8 add_convert_fusion
  57.8 7.4 %all-to-all-start = ((bf16[16,72,128]{2,1,0:T(8,128)(2,1)}), bf16[16,72,128]{2,1,0:T(8,128)(2,1)S(1)}, u32[]{:S(2)}, u32[]{:S(2)}) async-start(bf16[16,72,128]{2,1,0:T(8,128)(2,1)} %bitcast.7), calls=%async_computation | async-start | bytes 589824 | tf_op jit(solution)/shard_map/all_to_all | solution.py:699
  65.2 10.4 %shard_map.74 = (bf16[64,128,128]{2,1,0:T(8,128)(2,1)}, bf16[64,128,128]{2,1,0:T(8,128)(2,1)}) custom-call(s32[4]{0:T(128)S(1)} %copy-done.1, bf16[16,608,128]{2,1,0:T(8,128)(2,1)} %get-tuple-element.43.fxi, bf16[1536,256]{1,0:T(8,128)(2,1)} %get-tuple-element.54.wc2i, bf16[1536,256]{1,0:T(8,128)(2,1)} %get-tuple-element.55.wb1i, ...), custom_call_target="tpu_custom_call" | custom-call | flops 48318382080 | bytes 25165824 | tf_op jit(solution)/shard_map/pallas_call | solution.py:662
  75.6 0.6 all-to-all-done.x_ref
  76.2 1.3 %shard_map.77 = bf16[16,72,128]{2,1,0:T(8,128)(2,1)} custom-call(s32[4]{0:T(128)S(1)} %copy-done.1, bf16[16,72,128]{2,1,0:T(8,128)(2,1)S(1)} %all-to-all-done.x_ref, bf16[64,128,128]{2,1,0:T(8,128)(2,1)} %get-tuple-element.65._out), custom_call_target="tpu_custom_call" | custom-call | bytes 2097152 | tf_op jit(solution)/shard_map/pallas_call | solution.py:700
  77.5 6.3 %all-to-all-start.1 = ((bf16[16,72,128]{2,1,0:T(8,128)(2,1)}), bf16[16,72,128]{2,1,0:T(8,128)(2,1)S(1)}, u32[]{:S(2)}, u32[]{:S(2)}) async-start(bf16[16,72,128]{2,1,0:T(8,128)(2,1)} %shard_map.77), calls=%async_computation.1 | async-start | bytes 589824 | tf_op jit(solution)/shard_map/all_to_all | solution.py:708
  83.9 9.1 %shard_map.75 = (bf16[64,128,128]{2,1,0:T(8,128)(2,1)}, bf16[64,128,128]{2,1,0:T(8,128)(2,1)}) custom-call(s32[4]{0:T(128)S(1)} %copy-done.1, f32[608,128]{1,0:T(8,128)S(1)} %shard_map.67.cm, bf16[16,608,128]{2,1,0:T(8,128)(2,1)} %get-tuple-element.43.fxi, ...), custom_call_target="tpu_custom_call", output_to_operand_aliasing={{0}: (17, {}), {1}: (18, {})} | custom-call | flops 48318382080 | bytes 25165824 | tf_op jit(solution)/shard_map/pallas_call | solution.py:717
  93.0 1.3 %all-to-all-done.1 = bf16[16,72,128]{2,1,0:T(8,128)(2,1)S(1)} async-done(((bf16[16,72,128]{2,1,0:T(8,128)(2,1)}), bf16[16,72,128]{2,1,0:T(8,128)(2,1)S(1)}, u32[]{:S(2)}, u32[]{:S(2)}) %all-to-all-start.1) | async-done | bytes 294944 | tf_op jit(solution)/shard_map/all_to_all | solution.py:708
  94.3 0.1 collective-permute-start.7
  94.4 1.6 %collective-permute-done.7.other_ref = bf16[9,128,128]{2,1,0:T(8,128)(2,1)S(1)} collective-permute-done((bf16[9,128,128]{2,1,0:T(8,128)(2,1)S(1)}, bf16[9,128,128]{2,1,0:T(8,128)(2,1)S(1)}, u32[]{:S(2)}, u32[]{:S(2)}) %collective-permute-start.7) | collective-permute-done | bytes 294944 | tf_op jit(solution)/shard_map/ppermute | solution.py:752
  95.9 1.6 %shard_map.79 = f32[2,9,128,128]{3,2,1,0:T(8,128)} custom-call(s32[4]{0:T(128)S(1)} %copy-done.1, bf16[9,128,128]{2,1,0:T(8,128)(2,1)S(1)} %shard_map.78.mine_ref, bf16[9,128,128]{2,1,0:T(8,128)(2,1)S(1)} %collective-permute-done.7.other_ref), custom_call_target="tpu_custom_call" | custom-call | bytes 2097152 | tf_op jit(solution)/shard_map/pallas_call | solution.py:753
  (10 shorter events, 0.0 us)
Async XLA Ops:
  2.1 12.6 %collective-permute-start.1 = (bf16[2,64,16,128]{3,2,1,0:T(8,128)(2,1)S(1)}, bf16[2,64,16,128]{3,2,1,0:T(8,128)(2,1)S(1)}, u32[]{:S(2)}, u32[]{:S(2)}) collective-permute-start(bf16[2,64,16,128]{3,2,1,0:T(8,128)(2,1)S(1)} %pad_maximum_fusion.1), channel_id=1, source_target_pairs={{1,2},{2,1},{5,6},{6,5},{9,10},{10,9},{13,14},{14,13},{17,18},{18,... | collective-permute-start | bytes 1572872 | tf_op jit(solution)/shard_map/ppermute | solution.py:555
  2.9 11.9 %collective-permute-start = (bf16[2,64,16,128]{3,2,1,0:T(8,128)(2,1)S(1)}, bf16[2,64,16,128]{3,2,1,0:T(8,128)(2,1)S(1)}, u32[]{:S(2)}, u32[]{:S(2)}) collective-permute-start(bf16[2,64,16,128]{3,2,1,0:T(8,128)(2,1)S(1)} %pad_maximum_fusion), channel_id=1, source_target_pairs={{0,1},{1,0},{2,3},{3,2},{4,5},{5,4},{6,7},{7,6},{8,9},{9,8},{10,11... | collective-permute-start | bytes 1572872 | tf_op jit(solution)/shard_map/ppermute | solution.py:556
  8.6 6.2 %copy-start.1 = (s32[4]{0:T(128)S(1)}, s32[4]{0:T(128)}, u32[]{:S(2)}) copy-start(s32[4]{0:T(128)} %pad_add_fusion.meta) | copy-start | bytes 52
  14.7 6.8 %copy-start = (bf16[2,3,3,128,128]{4,3,2,1,0:T(8,128)(2,1)S(1)}, bf16[2,3,3,128,128]{4,3,2,1,0:T(8,128)(2,1)}, u32[]{:S(2)}) copy-start(bf16[2,3,3,128,128]{4,3,2,1,0:T(8,128)(2,1)} %k_ref.3) | copy-start | bytes 1769476
  16.8 29.9 %collective-permute-start.2 = (bf16[3,608,128]{2,1,0:T(8,128)(2,1)}, bf16[3,608,128]{2,1,0:T(8,128)(2,1)S(1)}, u32[]{:S(2)}, u32[]{:S(2)}) collective-permute-start(bf16[3,608,128]{2,1,0:T(8,128)(2,1)} %get-tuple-element.50), channel_id=1, source_target_pairs={{0,4},{4,8},{8,12},{12,16},{16,20},{20,24},{24,28},{1,5},{5,9},{9,... | collective-permute-start | bytes 1400840 | tf_op jit(solution)/shard_map/ppermute | solution.py:534
  20.3 26.5 %collective-permute-start.3 = (bf16[3,608,128]{2,1,0:T(8,128)(2,1)}, bf16[3,608,128]{2,1,0:T(8,128)(2,1)S(1)}, u32[]{:S(2)}, u32[]{:S(2)}) collective-permute-start(bf16[3,608,128]{2,1,0:T(8,128)(2,1)} %get-tuple-element.51), channel_id=1, source_target_pairs={{4,0},{8,4},{12,8},{16,12},{20,16},{24,20},{28,24},{5,1},{9,5},{13... | collective-permute-start | bytes 1400840 | tf_op jit(solution)/shard_map/ppermute | solution.py:534
  40.0 43.9 %collective-permute-start.4 = (bf16[3,608,128]{2,1,0:T(8,128)(2,1)}, bf16[3,608,128]{2,1,0:T(8,128)(2,1)}, u32[]{:S(2)}, u32[]{:S(2)}) collective-permute-start(bf16[3,608,128]{2,1,0:T(8,128)(2,1)} %get-tuple-element.52), channel_id=1, source_target_pairs={{0,4},{4,8},{8,12},{12,16},{16,20},{20,24},{24,28},{1,5},{5,9},{9,... | collective-permute-start | bytes 1400840 | tf_op jit(solution)/shard_map/ppermute | solution.py:534
  45.3 38.6 %collective-permute-start.5 = (bf16[3,608,128]{2,1,0:T(8,128)(2,1)}, bf16[3,608,128]{2,1,0:T(8,128)(2,1)}, u32[]{:S(2)}, u32[]{:S(2)}) collective-permute-start(bf16[3,608,128]{2,1,0:T(8,128)(2,1)} %get-tuple-element.53), channel_id=1, source_target_pairs={{4,0},{8,4},{12,8},{16,12},{20,16},{24,20},{28,24},{5,1},{9,5},{13... | collective-permute-start | bytes 1400840 | tf_op jit(solution)/shard_map/ppermute | solution.py:534
  55.4 1.6 %collective-permute-start.6 = (bf16[9,128,128]{2,1,0:T(8,128)(2,1)S(1)}, bf16[9,128,128]{2,1,0:T(8,128)(2,1)S(1)}, u32[]{:S(2)}, u32[]{:S(2)}) collective-permute-start(bf16[9,128,128]{2,1,0:T(8,128)(2,1)S(1)} %get-tuple-element.70), channel_id=1, source_target_pairs={{0,1},{1,0},{2,3},{3,2},{4,5},{5,4},{6,7},{7,6},{8,9},{9,8},{10,11... | collective-permute-start | bytes 884744 | tf_op jit(solution)/shard_map/ppermute | solution.py:684
  57.8 18.4 %all-to-all-start = ((bf16[16,72,128]{2,1,0:T(8,128)(2,1)}), bf16[16,72,128]{2,1,0:T(8,128)(2,1)S(1)}, u32[]{:S(2)}, u32[]{:S(2)}) async-start(bf16[16,72,128]{2,1,0:T(8,128)(2,1)} %bitcast.7), calls=%async_computation | async-start | bytes 589824 | tf_op jit(solution)/shard_map/all_to_all | solution.py:699
  77.5 16.8 %all-to-all-start.1 = ((bf16[16,72,128]{2,1,0:T(8,128)(2,1)}), bf16[16,72,128]{2,1,0:T(8,128)(2,1)S(1)}, u32[]{:S(2)}, u32[]{:S(2)}) async-start(bf16[16,72,128]{2,1,0:T(8,128)(2,1)} %shard_map.77), calls=%async_computation.1 | async-start | bytes 589824 | tf_op jit(solution)/shard_map/all_to_all | solution.py:708
  94.3 1.6 %collective-permute-start.7 = (bf16[9,128,128]{2,1,0:T(8,128)(2,1)S(1)}, bf16[9,128,128]{2,1,0:T(8,128)(2,1)S(1)}, u32[]{:S(2)}, u32[]{:S(2)}) collective-permute-start(bf16[9,128,128]{2,1,0:T(8,128)(2,1)S(1)} %shard_map.78.mine_ref), channel_id=1, source_target_pairs={{0,1},{1,0},{2,3},{3,2},{4,5},{5,4},{6,7},{7,6},{8,9},{9,8},{10,11... | collective-permute-start | bytes 884744 | tf_op jit(solution)/shard_map/ppermute | solution.py:752

commit v4 on v3

v4 whole, which is shorter than its diff:
```python
import functools

import jax
import jax.numpy as jnp
from jax import lax
from jax.experimental import pallas as pl
from jax.experimental.pallas import tpu as pltpu
from jax.sharding import PartitionSpec as P

H = 3
C = 128
F32 = jnp.float32
BF16 = jnp.bfloat16
ANY = pl.BlockSpec(memory_space=pl.ANY)
VMEM = pl.BlockSpec(memory_space=pltpu.VMEM)
SMEM = pl.BlockSpec(memory_space=pltpu.SMEM)


def params(mib):
    return pltpu.CompilerParams(vmem_limit_bytes=mib << 20)


def cost(flops, nbytes):
    return pl.CostEstimate(flops=int(flops), bytes_accessed=int(nbytes), transcendentals=0)


def to_blocks(rows):
    cols = rows[0].shape[0]
    v = [r.reshape(cols // 8, 8, C) for r in rows]
    low = lax.broadcasted_iota(jnp.int32, v[0].shape, 1) < 4

    def swap(a, b):
        return jnp.where(low, a, pltpu.roll(b, 4, 1)), jnp.where(low, pltpu.roll(a, 4, 1), b)

    a, b = swap(v[0], v[1])
    c, d = swap(v[2], v[3])
    y = jnp.stack([jnp.concatenate([a, c], axis=1), jnp.concatenate([b, d], axis=1)], axis=1)
    return y.reshape(4 * cols, C)


def from_blocks(y):
    cols = y.shape[0] // 4
    y = y.reshape(cols // 8, 2, 2, 8, C)
    a, b, c, d = y[:, 0, 0], y[:, 1, 0], y[:, 0, 1], y[:, 1, 1]
    low = lax.broadcasted_iota(jnp.int32, a.shape, 1) < 4

    def swap(a, b):
        return jnp.where(low, a, pltpu.roll(b, 4, 1)), jnp.where(low, pltpu.roll(a, 4, 1), b)

    r0, r1 = swap(a, b)
    r2, r3 = swap(c, d)
    return [r.reshape(cols, C) for r in (r0, r1, r2, r3)]


def column_mask(meta, nj):
    shape = (nj + 2 * H, 16, C)
    j = lax.broadcasted_iota(jnp.int32, shape, 0)
    s = lax.broadcasted_iota(jnp.int32, shape, 1)
    col = meta[1] + 4 * (j - H) + (s & 3)
    return ((col >= 0) & (col < meta[2])).astype(F32).reshape(-1, C)


def live(meta, cm, a, start, size):
    s = lax.broadcasted_iota(jnp.int32, (1, 16, C), 1)
    row = meta[0] + 4 * a + (s >> 2)
    row_mask = ((row >= 0) & (row < meta[2])).astype(F32)
    return (cm[start : start + size, :].reshape(size // 16, 16, C) * row_mask).reshape(size, C)


def elu_parts(v):
    e = jnp.exp(jnp.minimum(v, 0.0))
    return jnp.maximum(v, 0.0) + (e - 1.0), e


def conv_pairs(read, pairs, d, weights):
    parts = []
    for a in pairs:
        cells = []
        for q in range(3):
            cells += [read(a, q), read(a + d, q), read(a - d, q), read(a + 2 * d, q)]
        parts.append(jnp.concatenate(cells, axis=1))
    left = jnp.concatenate(parts, axis=0) if len(parts) > 1 else parts[0]
    return jnp.dot(left, weights, preferred_element_type=F32)


def outer(left, right):
    return lax.dot_general(left, right, (((0,), (0,)), ((), ())), preferred_element_type=F32)


def pack_kernel(k_ref, conv_ref, back_ref, *, conv_layer, back_layer):
    zero = jnp.zeros((C, C), BF16)

    def conv_tap(p, q):
        return k_ref[conv_layer, p, q]

    def back_tap(p, q):
        return k_ref[back_layer, 2 - p, 2 - q].T

    for tap, w_ref in ((conv_tap, conv_ref), (back_tap, back_ref)):
        for q in range(3):
            t0, t1, t2 = tap(0, q), tap(1, q), tap(2, q)
            o = 4 * C * q
            blocks = ((t1, t0), (t2, t1), (t0, zero), (zero, t2))
            for i, (x, y) in enumerate(blocks):
                w_ref[o + C * i : o + C * (i + 1), :C] = x
                w_ref[o + C * i : o + C * (i + 1), C:] = y


def copier(sem, jobs):
    def go(src, dst):
        c = pltpu.make_async_copy(src, dst, sem.at[len(jobs)])
        c.start()
        jobs.append(c)

    return go


def columns_kernel(meta, f, g, near, far, sem, *, cols):
    last = cols - 16
    starts = pl.multiple_of((1 - meta[3]) * last, 16), pl.multiple_of(meta[3] * last, 16)
    jobs = []
    go = copier(sem, jobs)
    for out, start in zip((far, near), starts[::-1]):
        for n, x in enumerate((f, g)):
            go(x.at[:, pl.ds(start, 16)], out.at[n])
    for c in jobs:
        c.wait()


def layout_kernel(meta, fi, gi, fx, gx, f, g, sem, *, nj, na):
    m0 = 16 * nj
    jobs = []
    go = copier(sem, jobs)
    group = na // 4
    for t in range(4):
        rows = pl.ds(4 * group * t, 4 * group)
        go(fi.at[rows], f.at[rows])
        go(gi.at[rows], g.at[rows])
    shape = (nj, 16, C)
    s = lax.broadcasted_iota(jnp.int32, shape, 1)
    j = lax.broadcasted_iota(jnp.int32, shape, 0)
    cm = (meta[1] + 4 * j + (s & 3) < meta[2]).astype(F32)
    s1 = lax.broadcasted_iota(jnp.int32, (1, 16, C), 1)

    def blocks(ref, k):
        return to_blocks([ref[4 * k + t].astype(F32) for t in range(4)])

    for t in range(4):
        jobs[2 * t].wait()
        jobs[2 * t + 1].wait()
        for k in range(group * t, group * (t + 1)):
            fx[k] = blocks(f, k).astype(BF16)
            rm = (meta[0] + 4 * k + (s1 >> 2) < meta[2]).astype(F32)
            gx[k] = (blocks(g, k).reshape(shape) * (cm * rm)).reshape(m0, C).astype(BF16)


def halo_kernel(meta, ev_ref, od_ref, fo, go_ref, _w, _cm, fx, gx, ua, da, ub, db, sem, *, nj, na):
    m0 = 16 * nj
    odd = meta[3] == 1
    shape = (2 * H, 16, C)
    s = lax.broadcasted_iota(jnp.int32, shape, 1)
    j = lax.broadcasted_iota(jnp.int32, shape, 0) - H
    col = meta[1] + 4 * jnp.where(j < 0, j, j + nj) + (s & 3)
    cm = ((col >= 0) & (col < meta[2])).astype(F32)
    s1 = lax.broadcasted_iota(jnp.int32, (1, 16, C), 1)

    def halos(n, k):
        def blocks(ref):
            return to_blocks([ref[n, 4 * k + t].astype(F32) for t in range(4)])

        ev, od = blocks(ev_ref), blocks(od_ref)
        low = jnp.where(odd, ev, od)[16 * (4 - H) :]
        high = jnp.where(odd, od, ev)[: 16 * H]
        return jnp.concatenate([low, high], axis=0)

    def extend(k):
        f = halos(0, k).astype(BF16)
        rm = (meta[0] + 4 * k + (s1 >> 2) < meta[2]).astype(F32)
        g = (halos(1, k).reshape(shape) * (cm * rm)).reshape(2 * H * 16, C).astype(BF16)
        for v, own, ref in ((f, fo, fx), (g, go_ref, gx)):
            ref[k, : 16 * H] = v[: 16 * H]
            ref[k, 16 * H : 16 * H + m0] = own[k]
            ref[k, 16 * H + m0 :] = v[16 * H :]

    ends = [0, 1, 2, na - 3, na - 2, na - 1]
    for k in ends:
        extend(k)
    jobs = []
    go = copier(sem, jobs)
    go(fx.at[pl.ds(1, 2)], ub.at[pl.ds(0, 2)])
    go(gx.at[pl.ds(2, 1)], ub.at[pl.ds(2, 1)])
    go(fx.at[pl.ds(na - 3, 2)], db.at[pl.ds(0, 2)])
    go(gx.at[pl.ds(na - 3, 1)], db.at[pl.ds(2, 1)])
    ua[0], ua[1], ua[2] = fx[0], gx[0], gx[1]
    da[0], da[1], da[2] = fx[na - 1], gx[na - 2], gx[na - 1]
    for k in range(3, na - 3):
        extend(k)
    for c in jobs:
        c.wait()


def inner_kernel(
    meta, fx, gx, wc, wb, _ub, _db, a1, acc_o, wco, wbo, fxo, gxo, a1o, a2o, so, g1o, lo, _ubo, _dbo,
    a2, st, g1, rest, es, cm, sem, *, na, nj,
):
    m0, m1, m2, w = 16 * nj, 16 * (nj + 2), 16 * (nj + 4), 16 * (nj + 6)
    ni = na - 4
    out = []
    send = copier(sem, out)
    send(wc, wco)
    send(wb, wbo)
    send(fx.at[:, pl.ds(16 * H, m0)], fxo)
    for i, row in enumerate((1, 3, na - 4, na - 2)):
        send(gx.at[pl.ds(row, 1)], gxo.at[pl.ds(i, 1)])
    cm[...] = column_mask(meta, nj)

    def activate(a, _):
        v, _e = elu_parts(fx[a].astype(F32))
        a1[a] = (v * live(meta, cm, a, 0, w)).astype(BF16)
        return 0

    lax.fori_loop(0, na, activate, 0)

    for t in range(ni // 4):
        r = 2 + 4 * t
        acc = conv_pairs(lambda row, q: a1[row, 16 * q : 16 * q + m2, :], [r, r + 2], 1, wc[...])
        for k in range(2):
            for b in range(2):
                row = r + 2 * k + b
                v = fx[row, 16 : 16 + m2, :].astype(F32) + acc[k * m2 : (k + 1) * m2, b * C : (b + 1) * C]
                act, e = elu_parts(v)
                a2[row + 2] = (act * live(meta, cm, row, 16, m2)).astype(BF16)
                es[row - 2] = e[16 : 16 + m1]
                st[row - 2] = v[32 : 32 + m0]
        acc = conv_pairs(lambda row, q: gx[row, 32 * q : 32 * q + m1, :], [r, r + 1], 2, wb[...])
        for k in range(2):
            for b in range(2):
                row = r + k + 2 * b
                back = acc[k * m1 : (k + 1) * m1, b * C : (b + 1) * C]
                full = gx[row, 32 : 32 + m1, :].astype(F32) + live(meta, cm, row, 32, m1) * es[row - 2] * back
                rounded = full.astype(BF16)
                g1[row + 1] = rounded
                rest[row - 2] = (full - rounded.astype(F32))[16 : 16 + m0].astype(BF16)

    send(a2.at[pl.ds(4, ni)], a2o)
    send(st, so)
    send(g1.at[pl.ds(3, ni)], g1o)
    send(rest, lo)
    send(a1.at[pl.ds(0, 1)], a1o.at[pl.ds(0, 1)])
    send(a1.at[pl.ds(na - 1, 1)], a1o.at[pl.ds(1, 1)])
    for i in (0, 1, 2, 3):
        a2[i] = jnp.zeros((m2, C), BF16)
        a2[na + i] = jnp.zeros((m2, C), BF16)
    for i in (0, 1, 2):
        g1[i] = jnp.zeros((m1, C), BF16)
        g1[na - 1 + i] = jnp.zeros((m1, C), BF16)

    def second(rows):
        left = [jnp.concatenate([a2[b + 2 + s, 32 : 32 + m0] for s in (2, 0, -2)], axis=1) for b in rows]
        right = [jnp.concatenate([gx[b, 16 + 32 * q : 16 + 32 * q + m0] for q in range(3)], axis=1) for b in rows]
        return outer(jnp.concatenate(left, axis=0), jnp.concatenate(right, axis=0))

    def first(rows):
        left = [jnp.concatenate([g1[b + 1 + s, 16 : 16 + m0] for s in (1, 0, -1)], axis=1) for b in rows]
        right = [jnp.concatenate([a1[b, 32 + 16 * q : 32 + 16 * q + m0] for q in range(3)], axis=1) for b in rows]
        return outer(jnp.concatenate(left, axis=0), jnp.concatenate(right, axis=0))

    half = na // 2
    acc_o[1] = second(range(half))
    acc_o[1] += second(range(half, na))
    acc_o[0] = first(range(1, half))
    acc_o[0] += first(range(half, na - 1))
    for c in out:
        c.wait()


def edge_kernel(
    meta, fx, gx, a1, up, dn, wc, wb, acc_i, a2o, so, g1o, lo, keep, send,
    a2, st, g1, rest, ah, es, cm, kg, sem, *, na, nj,
):
    m0, m1, m2, w = 16 * nj, 16 * (nj + 2), 16 * (nj + 4), 16 * (nj + 6)
    cm[...] = column_mask(meta, nj)
    for i, (ref, row) in enumerate(((up, -1), (dn, na))):
        v, _e = elu_parts(ref[0].astype(F32))
        ah[i] = (v * live(meta, cm, row, 0, w)).astype(BF16)

    def act_one(row, start, size):
        part = slice(start, start + size)
        return ah[0, part] if row < 0 else ah[1, part] if row >= na else a1[row, part]

    def grad_two(row, start, size):
        part = slice(start, start + size)
        return up[3 + row, part] if row < 0 else dn[1 + row - na, part] if row >= na else gx[row, part]

    acc = conv_pairs(lambda row, q: act_one(row, 16 * q, m2), [0, na - 2], 1, wc[...])
    for s in range(2):
        for b in range(2):
            row = (na - 2) * s + b
            v = fx[row, 16 : 16 + m2].astype(F32) + acc[s * m2 : (s + 1) * m2, b * C : (b + 1) * C]
            act, e = elu_parts(v)
            a2[s, b] = (act * live(meta, cm, row, 16, m2)).astype(BF16)
            es[s, b] = e[16 : 16 + m1]
            st[s, b] = v[32 : 32 + m0]
    acc = conv_pairs(lambda row, q: grad_two(row, 32 * q, m1), [0, 1, na - 4, na - 3], 2, wb[...])
    for s in range(2):
        for b in range(2):
            row = (na - 2) * s + b
            k = 2 * s + b
            back = acc[k * m1 : (k + 1) * m1, s * C : (s + 1) * C]
            full = gx[row, 32 : 32 + m1].astype(F32) + live(meta, cm, row, 32, m1) * es[s, b] * back
            rounded = full.astype(BF16)
            g1[s, b] = rounded
            rest[s, b] = (full - rounded.astype(F32))[16 : 16 + m0].astype(BF16)
    jobs = []
    go = copier(sem, jobs)
    for src, dst in ((a2, a2o), (st, so), (g1, g1o), (rest, lo)):
        go(src, dst)

    rows = [(s, b, (na - 2) * s + b) for s in range(2) for b in range(2)]
    left = jnp.concatenate([a2[s, b, 32 : 32 + m0] for s, b, _ in rows], axis=0)
    for p in range(3):
        right = [
            jnp.concatenate([grad_two(row + 2 * (p - 1), 16 + 32 * q, m0) for q in range(3)], axis=1)
            for _, _, row in rows
        ]
        total = acc_i[1, C * p : C * (p + 1)] + outer(left, jnp.concatenate(right, axis=0))
        for q in range(3):
            kg[1, 3 * (2 - p) + 2 - q] = total[:, C * q : C * (q + 1)]
    left = jnp.concatenate([g1[s, b, 16 : 16 + m0] for s, b, _ in rows], axis=0)
    for p in range(3):
        right = [
            jnp.concatenate([act_one(row + p - 1, 32 + 16 * q, m0) for q in range(3)], axis=1) for _, _, row in rows
        ]
        total = acc_i[0, C * p : C * (p + 1)] + outer(left, jnp.concatenate(right, axis=0))
        for q in range(3):
            kg[0, 3 * p + q] = total[:, C * q : C * (q + 1)].T
    mine = meta[3]
    keep[...] = kg[mine]
    send[...] = kg[1 - mine].astype(BF16)
    for c in jobs:
        c.wait()


def finish_state(meta, cm, row, state, product):
    m0 = state.shape[0]
    return from_blocks((state + product) * live(meta, cm, row, 16 * H, m0))


def finish_gradient(meta, cm, row, rounded, rest, feats, product):
    m0 = rest.shape[0]
    slope = jnp.exp(jnp.minimum(feats.astype(F32), 0.0))
    grads = rounded.astype(F32) + rest.astype(F32)
    return from_blocks(grads + live(meta, cm, row, 16 * H, m0) * slope * product)


def middle_kernel(
    meta, wc2, wb1, fxi, a2i, a2e, si, g1i, g1e, loi, out, fg,
    fm, a2, st, g1, lo, cm, ot, ft, sem, osem, *, na, nj,
):
    m0 = 16 * nj
    ni = na - 4
    quads = ni // 4
    jobs = []
    go = copier(sem, jobs)

    def fetch(t, src, edge, dst, reach):
        low = 2 if t == 0 else 6 + reach + 4 * (t - 1)
        high = min(6 + reach + 4 * t, na - 2)
        go(src.at[pl.ds(low - 2, high - low)], dst.at[pl.ds(low, high - low)])
        if t == 0:
            go(edge.at[0], dst.at[pl.ds(0, 2)])
        if t == quads - 1:
            go(edge.at[1], dst.at[pl.ds(na - 2, 2)])

    fetch(0, a2i, a2e, a2, 2)
    fetch(0, g1i, g1e, g1, 1)
    for t in range(quads):
        if t > 0:
            fetch(t, a2i, a2e, a2, 2)
            fetch(t, g1i, g1e, g1, 1)
        here = pl.ds(4 * t, 4)
        go(si.at[here], st.at[here])
        go(fxi.at[pl.ds(2 + 4 * t, 4)], fm.at[here])
        go(loi.at[here], lo.at[here])
        if t == 0:
            stage_three = len(jobs)
    cm[...] = column_mask(meta, nj)

    def arrive(first, last):
        for c in jobs[first:last]:
            c.wait()

    for t in range(quads):
        r = 2 + 4 * t
        if t == 0:
            arrive(0, stage_three)
        elif t == 1:
            arrive(stage_three, len(jobs))
        acc2 = conv_pairs(lambda row, q: a2[row, 32 * q : 32 * q + m0], [r, r + 1], 2, wc2[...])
        acc1 = conv_pairs(lambda row, q: g1[row, 16 * q : 16 * q + m0], [r, r + 2], 1, wb1[...])
        for k in range(2):
            for b in range(2):
                row = r + k + 2 * b
                product = acc2[k * m0 : (k + 1) * m0, b * C : (b + 1) * C]
                for i, x in enumerate(finish_state(meta, cm, row, st[row - 2], product)):
                    ot[4 * (row - 2) + i] = x.astype(BF16)
                row = r + 2 * k + b
                product = acc1[k * m0 : (k + 1) * m0, b * C : (b + 1) * C]
                parts = finish_gradient(
                    meta, cm, row, g1[row, 16 : 16 + m0], lo[row - 2], fm[row - 2], product
                )
                for i, x in enumerate(parts):
                    ft[4 * (row - 2) + i] = x.astype(BF16)
        here, there = pl.ds(16 * t, 16), pl.ds(16 * t + 8, 16)
        pltpu.make_async_copy(ot.at[here], out.at[there], osem.at[0]).start()
        pltpu.make_async_copy(ft.at[here], fg.at[there], osem.at[1]).start()
    pltpu.make_async_copy(ot, out.at[pl.ds(8, 4 * ni)], osem.at[0]).wait()
    pltpu.make_async_copy(ft, fg.at[pl.ds(8, 4 * ni)], osem.at[1]).wait()


def mask_kernel(meta, cm, *, nj):
    cm[...] = column_mask(meta, nj)


def last_kernel(
    meta, cm, fxi, gxi, a1i, upa, dna, upb, dnb, wc2, wb1, wci, wbi, a2i, a2e, g1i, g1e, si, loi, _out, _fg, out, fg,
    own, near, a1, a2, g1, st, lo, ah, a2h, es, g1h, ot, ft, wc, wb, sem, *, na, nj,
):
    m0, m1, m2, w = 16 * nj, 16 * (nj + 2), 16 * (nj + 4), 16 * (nj + 6)
    jobs = []
    go = copier(sem, jobs)
    go(a1i, a1)
    go(wci, wc)
    go(gxi, near)
    go(wbi, wb)
    early = len(jobs)
    go(a2e.at[0], a2.at[0, pl.ds(0, 2)])
    go(a2i.at[pl.ds(0, 4)], a2.at[0, pl.ds(2, 4)])
    go(a2i.at[pl.ds(na - 8, 4)], a2.at[1, pl.ds(0, 4)])
    go(a2e.at[1], a2.at[1, pl.ds(4, 2)])
    go(g1e.at[0], g1.at[0, pl.ds(0, 2)])
    go(g1i.at[pl.ds(0, 1)], g1.at[0, pl.ds(2, 1)])
    go(g1i.at[pl.ds(na - 5, 1)], g1.at[1, pl.ds(0, 1)])
    go(g1e.at[1], g1.at[1, pl.ds(1, 2)])
    go(si, st)
    go(loi, lo)
    for s in range(2):
        go(fxi.at[pl.ds((na - 2) * s, 2)], own.at[s])
    feats = {-3: upb.at[0], -2: upb.at[1], -1: upa.at[0], na: dna.at[0], na + 1: dnb.at[0], na + 2: dnb.at[1]}
    grads = {-3: upb.at[2], -1: upa.at[2], na: dna.at[1], na + 2: dnb.at[2]}
    order = list(feats)
    for i, row in enumerate(order):
        v, _e = elu_parts(feats[row][...].astype(F32))
        ah[i] = (v * live(meta, cm, row, 0, w)).astype(BF16)

    def act_one(row, start):
        part = slice(start, start + m2)
        return ah[order.index(row), part] if row in feats else a1[0 if row == 0 else 1, part]

    def grad_two(row, start):
        part = slice(start, start + m1)
        return grads[row][part] if row in grads else near[(1, 3, na - 4, na - 2).index(row), part]

    def act_two(row, start):
        part = slice(start, start + m0)
        if row < 0 or row >= na:
            return a2h[row + 2 if row < 0 else row - na + 2, part]
        return a2[0, row, part] if row < 6 else a2[1, row - (na - 6), part]

    def grad_one(row, start):
        part = slice(start, start + m0)
        if row < 0 or row >= na:
            return g1h[0 if row < 0 else 1, part]
        return g1[0, row, part] if row < 3 else g1[1, row - (na - 3), part]

    for c in jobs[:early]:
        c.wait()
    acc = conv_pairs(lambda row, q: act_one(row, 16 * q), [-2, na], 1, wc[...])
    for s in range(2):
        for b in range(2):
            row = b - 2 if s == 0 else na + b
            v = feats[row][16 : 16 + m2].astype(F32) + acc[s * m2 : (s + 1) * m2, b * C : (b + 1) * C]
            act, e = elu_parts(v)
            a2h[2 * s + b] = (act * live(meta, cm, row, 16, m2)).astype(BF16)
            if b != s:
                es[s] = e[16 : 16 + m1]
    acc = conv_pairs(lambda row, q: grad_two(row, 32 * q), [-1, na - 2], 2, wb[...])
    for s in range(2):
        row = -1 if s == 0 else na
        back = acc[s * m1 : (s + 1) * m1, s * C : (s + 1) * C]
        full = grads[row][32 : 32 + m1].astype(F32) + live(meta, cm, row, 32, m1) * es[s] * back
        g1h[s] = full.astype(BF16)
    for c in jobs[early:]:
        c.wait()
    acc2 = conv_pairs(lambda row, q: act_two(row, 32 * q), [0, 1, na - 4, na - 3], 2, wc2[...])
    acc1 = conv_pairs(lambda row, q: grad_one(row, 16 * q), [0, na - 2], 1, wb1[...])
    for s in range(2):
        for b in range(2):
            row = (na - 2) * s + b
            k = 2 * s + b
            product = acc2[k * m0 : (k + 1) * m0, s * C : (s + 1) * C]
            for i, x in enumerate(finish_state(meta, cm, row, st[s, b], product)):
                ot[s, 4 * b + i] = x.astype(BF16)
            product = acc1[s * m0 : (s + 1) * m0, b * C : (b + 1) * C]
            rounded = g1[s, s + b, 16 : 16 + m0]
            for i, x in enumerate(finish_gradient(meta, cm, row, rounded, lo[s, b], own[s, b], product)):
                ft[s, 4 * b + i] = x.astype(BF16)
    done = len(jobs)
    for s in range(2):
        go(ot.at[s], out.at[pl.ds(4 * (na - 2) * s, 8)])
        go(ft.at[s], fg.at[pl.ds(4 * (na - 2) * s, 8)])
    for c in jobs[done:]:
        c.wait()


def sum_kernel(meta, x_ref, _out, o_ref):
    total = jnp.sum(x_ref[...].astype(F32), axis=0) / meta[2].astype(F32)
    o_ref[...] = jnp.broadcast_to(total.astype(BF16)[None], o_ref.shape)


def add_kernel(x_ref, y_ref, o_ref):
    o_ref[...] = (x_ref[...] + y_ref[...].astype(F32)).astype(BF16)


def hold_kernel(x_ref, o_ref):
    del x_ref, o_ref


def after_kernel(x_ref, _out, o_ref):
    o_ref[...] = x_ref[...]


def join_kernel(meta, mine_ref, other_ref, o_ref):
    mine = meta[3]
    o_ref[mine] = mine_ref[...].astype(F32)
    o_ref[1 - mine] = other_ref[...].astype(F32)


def in_hbm(*arrays):
    return [pltpu.with_memory_space_constraint(x, pltpu.HBM) for x in arrays]


def in_vmem(*arrays):
    return [pltpu.with_memory_space_constraint(x, pltpu.VMEM) for x in arrays]


def shift(x, axis, step):
    n = lax.axis_size(axis)
    return lax.ppermute(x, axis, [(i, i + step) for i in range(n) if 0 <= i + step < n])


def body(features, kernels, length, cotangent):
    rows, cols, _ = features.shape
    na, nj = rows // 4, cols // 4
    m0, m1, m2, w = 16 * nj, 16 * (nj + 2), 16 * (nj + 4), 16 * (nj + 6)
    ni = na - 4
    odd = lax.rem(lax.axis_index("col"), 2)
    meta = jnp.stack([lax.axis_index("row") * rows, lax.axis_index("col") * cols, length[0], odd]).astype(jnp.int32)
    sds = jax.ShapeDtypeStruct

    near, far = pl.pallas_call(
        functools.partial(columns_kernel, cols=cols),
        in_specs=[SMEM] + [ANY] * 2,
        out_specs=[VMEM] * 2,
        out_shape=[pltpu.VMEM((2, rows, 16, C), BF16)] * 2,
        scratch_shapes=[pltpu.SemaphoreType.DMA((4,))],
        compiler_params=params(8),
        cost_estimate=cost(0, 2 << 20),
    )(meta, *in_hbm(features, cotangent))
    n = lax.axis_size("col")
    inner = [(i, i ^ 1) for i in range(n)]
    outer_pairs = [(i, i + 1) for i in range(1, n - 1, 2)]
    od = lax.ppermute(far, "col", outer_pairs + [(j, i) for i, j in outer_pairs])
    ev = lax.ppermute(near, "col", inner)

    def pack(conv_layer, back_layer):
        return pl.pallas_call(
            functools.partial(pack_kernel, conv_layer=conv_layer, back_layer=back_layer),
            in_specs=[VMEM],
            out_specs=[VMEM] * 2,
            out_shape=[pltpu.VMEM((12 * C, 2 * C), BF16)] * 2,
            compiler_params=params(12),
            cost_estimate=cost(0, 8 << 20),
        )(kernels)

    w_one, w_two_back = pack(0, 1)
    w_two, w_one_back = pack(1, 0)
    cm = pl.pallas_call(
        functools.partial(mask_kernel, nj=nj),
        in_specs=[SMEM],
        out_specs=VMEM,
        out_shape=sds((w, C), F32),
        compiler_params=params(8),
        cost_estimate=cost(0, 1 << 20),
    )(meta)
    vm, hbm = pltpu.VMEM, pltpu.HBM
    fx, gx = pl.pallas_call(
        functools.partial(layout_kernel, nj=nj, na=na),
        in_specs=[SMEM] + [ANY] * 2,
        out_specs=[VMEM] * 2,
        out_shape=[vm((na, m0, C), BF16)] * 2,
        scratch_shapes=[vm(features.shape, BF16), vm(features.shape, BF16), pltpu.SemaphoreType.DMA((8,))],
        compiler_params=params(16),
        cost_estimate=cost(0, 12 << 20),
    )(meta, *in_hbm(features, cotangent))
    fx, gx, ua, da, ub, db = pl.pallas_call(
        functools.partial(halo_kernel, nj=nj, na=na),
        in_specs=[SMEM] + [VMEM] * 4 + [ANY] * 2,
        out_specs=[VMEM] * 4 + [ANY] * 2,
        out_shape=[vm((na, w, C), BF16)] * 2 + [vm((3, w, C), BF16)] * 2 + [hbm((3, w, C), BF16)] * 2,
        scratch_shapes=[pltpu.SemaphoreType.DMA((4,))],
        compiler_params=params(12),
        cost_estimate=cost(0, 4 << 20),
    )(meta, ev, od, *in_vmem(fx, gx), w_two, cm)
    dna = shift(ua, "row", -1)
    upa = shift(da, "row", 1)

    conv_flops = 2 * rows * cols * 9 * C * C
    a1, acc, w_one_far, w_two_back_far, fxo, gxo, a1o, a2, st, g1, lo, ub, db = pl.pallas_call(
        functools.partial(inner_kernel, na=na, nj=nj),
        in_specs=[SMEM] + [VMEM] * 4 + [ANY] * 2,
        out_specs=[VMEM] * 2 + [ANY] * 11,
        out_shape=[
            vm((na, w, C), BF16),
            vm((2, 3 * C, 3 * C), F32),
            hbm((12 * C, 2 * C), BF16),
            hbm((12 * C, 2 * C), BF16),
            hbm((na, m0, C), BF16),
            hbm((4, w, C), BF16),
            hbm((2, w, C), BF16),
            hbm((ni, m2, C), BF16),
            hbm((ni, m0, C), F32),
            hbm((ni, m1, C), BF16),
            hbm((ni, m0, C), BF16),
            hbm((3, w, C), BF16),
            hbm((3, w, C), BF16),
        ],
        scratch_shapes=[
            vm((na + 4, m2, C), BF16),
            vm((ni, m0, C), F32),
            vm((na + 2, m1, C), BF16),
            vm((ni, m0, C), BF16),
            vm((ni, m1, C), F32),
            vm((w, C), F32),
            pltpu.SemaphoreType.DMA((13,)),
        ],
        input_output_aliases={5: 11, 6: 12},
        compiler_params=params(30),
        cost_estimate=cost(0, 1 << 20),
    )(meta, *in_vmem(fx, gx, w_one, w_two_back), *in_hbm(ub, db))
    dnb = shift(ub, "row", -1)
    upb = shift(db, "row", 1)

    a2e, ste, g1e, loe, keep, send = pl.pallas_call(
        functools.partial(edge_kernel, na=na, nj=nj),
        in_specs=[SMEM] + [VMEM] * 8,
        out_specs=[ANY] * 4 + [VMEM] * 2,
        out_shape=[
            hbm((2, 2, m2, C), BF16),
            hbm((2, 2, m0, C), F32),
            hbm((2, 2, m1, C), BF16),
            hbm((2, 2, m0, C), BF16),
            sds((9, C, C), F32),
            sds((9, C, C), BF16),
        ],
        scratch_shapes=[
            vm((2, 2, m2, C), BF16),
            vm((2, 2, m0, C), F32),
            vm((2, 2, m1, C), BF16),
            vm((2, 2, m0, C), BF16),
            vm((2, w, C), BF16),
            vm((2, 2, m1, C), F32),
            vm((w, C), F32),
            vm((2, 9, C, C), F32),
            pltpu.SemaphoreType.DMA((4,)),
        ],
        compiler_params=params(20),
        cost_estimate=cost(0, 1 << 20),
    )(meta, *in_vmem(fx, gx, a1), upa, dna, *in_vmem(w_one, w_two_back, acc))

    out, fg = pl.pallas_call(
        functools.partial(middle_kernel, na=na, nj=nj),
        in_specs=[SMEM] + [VMEM] * 2 + [ANY] * 7,
        out_specs=[ANY] * 2,
        out_shape=[hbm(features.shape, BF16)] * 2,
        scratch_shapes=[
            vm((ni, m0, C), BF16),
            vm((na, m2, C), BF16),
            vm((ni, m0, C), F32),
            vm((na, m1, C), BF16),
            vm((ni, m0, C), BF16),
            vm((w, C), F32),
            vm((4 * ni, cols, C), BF16),
            vm((4 * ni, cols, C), BF16),
            pltpu.SemaphoreType.DMA((4 + 5 * (ni // 4),)),
            pltpu.SemaphoreType.DMA((2,)),
        ],
        compiler_params=params(28),
        cost_estimate=cost(20 * conv_flops, 24 << 20),
    )(meta, *in_vmem(w_two, w_one_back), *in_hbm(fxo, a2, a2e, st, g1, g1e, lo))

    received = lax.ppermute(send, "col", inner)
    axes = ("row", "col")
    groups = [
        [r * n + c for r in range(lax.axis_size("row")) for c in range(side, n, 2)] for side in range(2)
    ]
    keep = pl.pallas_call(
        hold_kernel,
        in_specs=[ANY],
        out_specs=ANY,
        out_shape=sds((9, C, C), F32),
        input_output_aliases={0: 0},
        compiler_params=params(10),
        cost_estimate=cost(20 * conv_flops, 1 << 20),
    )(keep)
    share = pl.pallas_call(
        add_kernel,
        in_specs=[VMEM] * 2,
        out_specs=VMEM,
        out_shape=sds((9, C, C), BF16),
        compiler_params=params(10),
        cost_estimate=cost(0, 1 << 20),
    )(keep, received).reshape(len(groups[0]), -1, C)
    shares = lax.all_to_all(share, axes, 0, 0, axis_index_groups=groups, tiled=True)
    spread = pl.pallas_call(
        sum_kernel,
        in_specs=[SMEM, VMEM, ANY],
        out_specs=VMEM,
        out_shape=sds(shares.shape, BF16),
        compiler_params=params(10),
        cost_estimate=cost(0, 2 << 20),
    )(meta, shares, *in_hbm(out))
    mine = lax.all_to_all(spread, axes, 0, 0, axis_index_groups=groups, tiled=True).reshape(9, C, C)
    out, fg = pl.pallas_call(
        functools.partial(last_kernel, na=na, nj=nj),
        in_specs=[SMEM, VMEM] + [ANY] * 3 + [VMEM] * 6 + [ANY] * 10,
        out_specs=[ANY] * 2,
        out_shape=[hbm(features.shape, BF16)] * 2,
        scratch_shapes=[
            vm((2, 2, m0, C), BF16),
            vm((4, w, C), BF16),
            vm((2, w, C), BF16),
            vm((2, 6, m2, C), BF16),
            vm((2, 3, m1, C), BF16),
            vm((2, 2, m0, C), F32),
            vm((2, 2, m0, C), BF16),
            vm((6, w, C), BF16),
            vm((4, m2, C), BF16),
            vm((2, m1, C), F32),
            vm((2, m1, C), BF16),
            vm((2, 8, cols, C), BF16),
            vm((2, 8, cols, C), BF16),
            vm((12 * C, 2 * C), BF16),
            vm((12 * C, 2 * C), BF16),
            pltpu.SemaphoreType.DMA((24,)),
        ],
        input_output_aliases={19: 0, 20: 1},
        compiler_params=params(24),
        cost_estimate=cost(20 * conv_flops, 24 << 20),
    )(
        meta, cm, *in_hbm(fxo, gxo, a1o), upa, dna, upb, dnb, *in_vmem(w_two, w_one_back),
        *in_hbm(w_one_far, w_two_back_far, a2, a2e, g1, g1e, ste, loe, out, fg),
    )
    mine = pl.pallas_call(
        after_kernel,
        in_specs=[VMEM, ANY],
        out_specs=VMEM,
        out_shape=sds((9, C, C), BF16),
        compiler_params=params(10),
        cost_estimate=cost(0, 1 << 20),
    )(mine, *in_hbm(out))
    other = lax.ppermute(mine, "col", inner)
    kernel_gradient = pl.pallas_call(
        join_kernel,
        in_specs=[SMEM, VMEM, VMEM],
        out_specs=VMEM,
        out_shape=sds((2, 9, C, C), F32),
        compiler_params=params(10),
        cost_estimate=cost(0, 2 << 20),
    )(meta, mine, other).reshape(kernels.shape)

    return out, fg, kernel_gradient


def solution(mesh):
    spec = P("row", "col", None)
    return jax.shard_map(
        body, mesh=mesh, in_specs=(spec, P(), P(), spec), out_specs=(spec, spec, P()), check_vma=False
    )
```

time: 98.1 us -> 94.7 us (0.965)
  Pallas kernels: 57.6 us -> 53.5 us
  starting transfers between devices: 30.5 us -> 34.3 us
  other arithmetic: 1.54 us -> 0.08 us
  local copies, waits for them, and re-layouts: 1.41 us -> 0.01 us
    ppermute x1, starting transfers between devices: 0.07 us -> 5.52 us  [body(): received = lax.ppermute(send, 'col', inner)]
    ppermute x2, starting transfers between devices: 5.06 us -> 1.2 us  [the longest x1 0.68 us: body(): lax.ppermute(far, 'col', outer_pairs + [(j, i) for i, j in outer_pairs])]
    pallas_call x1, Pallas kernels: 8.57 us -> 7.12 us  [body(): pl.pallas_call(functools.partial(edge_kernel, na=na, nj=nj), in_specs=[SM...]
    all_to_all x1, starting transfers between devices: 7.43 us -> 8.84 us  [body(): lax.all_to_all(share, axes, 0, 0, axis_index_groups=groups, tiled=True)]
    another operation x1 -> x0, local copies, waits for them, and re-layouts: 1.4 us -> none  [edges(): jnp.stack([lax.dynamic_slice_in_dim(x, start, 16, axis=1) for x in (featu...]
    ppermute x4, starting transfers between devices: 11.5 us -> 12.7 us  [shift(): lax.ppermute(x, axis, [(i, i + step) for i in range(n) if 0 <= i + step <...]
    pallas_call x2, Pallas kernels: 1.63 us -> 0.5 us  [pack(): pl.pallas_call(functools.partial(pack_kernel, conv_layer=conv_layer, back...]
    pallas_call x1 -> x3, Pallas kernels: 6.15 us -> 5.63 us  [the longest x1 3.07 us: body(): pl.pallas_call(functools.partial(layout_kernel, nj=nj, na=na), in_specs=[...]
  transfers between devices with their start and end apart: 10 -> 10, of which waited for: 4 -> 4; matrix products, arithmetic and copies ran while one was open for 2% -> 0% of each run, Pallas kernels for 55% -> 51%
where the time goes in v4:
time: 94.7 us; the launch traced here: 94.2 us
  Pallas kernels  53.5 us (56%)
  starting transfers between devices  34.3 us (36%)
  waiting for transfers between devices  4.9 us (5%)
  between operations  1.49 us (2%)
    pallas_call x1, Pallas kernels, body(): pl.pallas_call(functools.partial(inner_kernel, na=na, nj=nj), in_specs=[S...  15.6 us
    ppermute x4, starting transfers between devices, shift(): lax.ppermute(x, axis, [(i, i + step) for i in range(n) if 0 <= i + step <...  12.7 us
    pallas_call x1, Pallas kernels, body(): pl.pallas_call(functools.partial(middle_kernel, na=na, nj=nj), in_specs=[...  9.95 us
    pallas_call x1, Pallas kernels, body(): pl.pallas_call(functools.partial(last_kernel, na=na, nj=nj), in_specs=[SM...  9.31 us
    all_to_all x1, starting transfers between devices, body(): lax.all_to_all(share, axes, 0, 0, axis_index_groups=groups, tiled=True)  8.84 us
    pallas_call x1, Pallas kernels, body(): pl.pallas_call(functools.partial(edge_kernel, na=na, nj=nj), in_specs=[SM...  7.12 us
    all_to_all x1, starting transfers between devices, body(): lax.all_to_all(spread, axes, 0, 0, axis_index_groups=groups, tiled=True)  5.89 us
    ppermute x1, starting transfers between devices, body(): received = lax.ppermute(send, 'col', inner)  5.52 us
  transfers between devices with their start and end apart: 10, of which 4 were waited for; matrix products, arithmetic and copies ran while one was open for 0% of the time, Pallas kernels for 51%

profile of v4, /device:TPU:0, one launch (start us, length us, event | category | flops | bytes accessed | tf_op | source)
XLA Modules:
  0.0 94.2 jit_solution(3328547409541757370)
XLA Ops:
  1.3 0.1 pad_add_fusion.meta
  1.4 1.8 %shard_map.68 = (bf16[2,64,16,128]{3,2,1,0:T(8,128)(2,1)S(1)}, bf16[2,64,16,128]{3,2,1,0:T(8,128)(2,1)S(1)}) custom-call(s32[4]{0:T(128)S(1)} %pad_add_fusion.meta, bf16[64,128,128]{2,1,0:T(8,128)(2,1)} %fi.1, bf16[64,128,128]{2,1,0:T(8,128)(2,1)} %gi.1), custom_call_target="tpu_custom_call" | custom-call | bytes 2097152 | tf_op jit(solution)/shard_map/pallas_call | solution.py:561
  3.1 0.5 collective-permute-start
  3.7 0.7 collective-permute-start.1
  4.4 0.6 shard_map.67._cm.cm
  5.0 0.0 copy-start
  5.0 3.1 %shard_map.69 = (bf16[16,512,128]{2,1,0:T(8,128)(2,1)S(1)}, bf16[16,512,128]{2,1,0:T(8,128)(2,1)S(1)}) custom-call(s32[4]{0:T(128)S(1)} %pad_add_fusion.meta, bf16[64,128,128]{2,1,0:T(8,128)(2,1)} %fi.1, bf16[64,128,128]{2,1,0:T(8,128)(2,1)} %gi.1), custom_call_target="tpu_custom_call" | custom-call | bytes 12582912 | tf_op jit(solution)/shard_map/pallas_call | solution.py:597
  8.1 0.2 shard_map.70
  8.3 0.0 collective-permute-done.ev_ref
  8.3 1.8 %shard_map.71 = (bf16[16,608,128]{2,1,0:T(8,128)(2,1)S(1)}, bf16[16,608,128]{2,1,0:T(8,128)(2,1)S(1)}, bf16[3,608,128]{2,1,0:T(8,128)(2,1)S(1)}, bf16[3,608,128]...) custom-call(s32[4]{0:T(128)S(1)} %pad_add_fusion.meta, ...), custom_call_target="tpu_custom_call" | custom-call | bytes 4194304 | tf_op jit(solution)/shard_map/pallas_call | solution.py:606
  10.1 4.4 %collective-permute-start.2 = (bf16[3,608,128]{2,1,0:T(8,128)(2,1)S(1)}, bf16[3,608,128]{2,1,0:T(8,128)(2,1)S(1)}, u32[]{:S(2)}, u32[]{:S(2)}) collective-permute-start(bf16[3,608,128]{2,1,0:T(8,128)(2,1)S(1)} %get-tuple-element.54), channel_id=1, source_target_pairs={{0,4},{4,8},{8,12},{12,16},{16,20},{20,24},{24,28},{1,5},{5,9},{9,... | collective-permute-start | bytes 1400840 | tf_op jit(solution)/shard_map/ppermute | solution.py:549
  14.6 1.5 %collective-permute-start.3 = (bf16[3,608,128]{2,1,0:T(8,128)(2,1)S(1)}, bf16[3,608,128]{2,1,0:T(8,128)(2,1)S(1)}, u32[]{:S(2)}, u32[]{:S(2)}) collective-permute-start(bf16[3,608,128]{2,1,0:T(8,128)(2,1)S(1)} %get-tuple-element.55), channel_id=1, source_target_pairs={{4,0},{8,4},{12,8},{16,12},{20,16},{24,20},{28,24},{5,1},{9,5},{13... | collective-permute-start | bytes 1400840 | tf_op jit(solution)/shard_map/ppermute | solution.py:549
  16.0 0.2 shard_map.72
  16.3 15.6 %shard_map.73 = (bf16[16,608,128]{2,1,0:T(8,128)(2,1)S(1)}, f32[2,384,384]{2,1,0:T(8,128)S(1)}, bf16[1536,256]{1,0:T(8,128)(2,1)}, bf16[1536,256]{1,0:T(8,128)(2...) custom-call(s32[4]{0:T(128)S(1)} %pad_add_fusion.meta, ...), custom_call_target="tpu_custom_call", output_to_operand_aliasing={{11}: (5, {}), {12}: (6, {})} | custom-call | bytes 1048576 | tf_op jit(solution)/shard_map/pallas_call | solution.py:619
  31.9 5.3 %collective-permute-start.4 = (bf16[3,608,128]{2,1,0:T(8,128)(2,1)}, bf16[3,608,128]{2,1,0:T(8,128)(2,1)}, u32[]{:S(2)}, u32[]{:S(2)}) collective-permute-start(bf16[3,608,128]{2,1,0:T(8,128)(2,1)} %get-tuple-element.56), channel_id=1, source_target_pairs={{0,4},{4,8},{8,12},{12,16},{16,20},{20,24},{24,28},{1,5},{5,9},{9,... | collective-permute-start | bytes 1400840 | tf_op jit(solution)/shard_map/ppermute | solution.py:549
  37.3 1.5 %collective-permute-start.5 = (bf16[3,608,128]{2,1,0:T(8,128)(2,1)}, bf16[3,608,128]{2,1,0:T(8,128)(2,1)}, u32[]{:S(2)}, u32[]{:S(2)}) collective-permute-start(bf16[3,608,128]{2,1,0:T(8,128)(2,1)} %get-tuple-element.57), channel_id=1, source_target_pairs={{4,0},{8,4},{12,8},{16,12},{20,16},{24,20},{28,24},{5,1},{9,5},{13... | collective-permute-start | bytes 1400840 | tf_op jit(solution)/shard_map/ppermute | solution.py:549
  38.8 0.0 collective-permute-done.2.up.upa
  38.8 7.1 %shard_map.74 = (bf16[2,2,576,128]{3,2,1,0:T(8,128)(2,1)}, f32[2,2,512,128]{3,2,1,0:T(8,128)}, bf16[2,2,544,128]{3,2,1,0:T(8,128)(2,1)}, bf16[2,2,512,128]{3,2,1...) custom-call(s32[4]{0:T(128)S(1)} %pad_add_fusion.meta, ...), custom_call_target="tpu_custom_call" | custom-call | bytes 1048576 | tf_op jit(solution)/shard_map/pallas_call | solution.py:654
  45.9 5.5 %collective-permute-start.6 = (bf16[9,128,128]{2,1,0:T(8,128)(2,1)S(1)}, bf16[9,128,128]{2,1,0:T(8,128)(2,1)S(1)}, u32[]{:S(2)}, u32[]{:S(2)}) collective-permute-start(bf16[9,128,128]{2,1,0:T(8,128)(2,1)S(1)} %get-tuple-element.76), channel_id=1, source_target_pairs={{0,1},{1,0},{2,3},{3,2},{4,5},{5,4},{6,7},{7,6},{8,9},{9,8},{10,11... | collective-permute-start | bytes 884744 | tf_op jit(solution)/shard_map/ppermute | solution.py:702
  51.5 1.2 %collective-permute-done.6.y_ref = bf16[9,128,128]{2,1,0:T(8,128)(2,1)S(1)} collective-permute-done((bf16[9,128,128]{2,1,0:T(8,128)(2,1)S(1)}, bf16[9,128,128]{2,1,0:T(8,128)(2,1)S(1)}, u32[]{:S(2)}, u32[]{:S(2)}) %collective-permute-start.6) | collective-permute-done | bytes 294944 | tf_op jit(solution)/shard_map/ppermute | solution.py:702
  52.7 0.8 shard_map.78
  53.5 8.8 %all-to-all-start = ((bf16[16,72,128]{2,1,0:T(8,128)(2,1)}), bf16[16,72,128]{2,1,0:T(8,128)(2,1)S(1)}, u32[]{:S(2)}, u32[]{:S(2)}) async-start(bf16[16,72,128]{2,1,0:T(8,128)(2,1)} %bitcast.3), calls=%async_computation | async-start | bytes 589824 | tf_op jit(solution)/shard_map/all_to_all | solution.py:724
  62.3 9.9 %shard_map.75 = (bf16[64,128,128]{2,1,0:T(8,128)(2,1)}, bf16[64,128,128]{2,1,0:T(8,128)(2,1)}) custom-call(s32[4]{0:T(128)S(1)} %pad_add_fusion.meta, bf16[1536,256]{1,0:T(8,128)(2,1)S(1)} %get-tuple-element.44._w.wc2, bf16[1536,256]{1,0:T(8,128)(2,1)S(1)} %get-tuple-element.58.wb1, bf16[16,512,128]{2,1,0:T(8,128)(2,1)} %get-tuple-element.51.fxi, ...), custom_call_target="tpu_custom_call" | custom-call | flops 48318382080 | bytes 25165824 | tf_op jit(solution)/shard_map/pallas_call | solution.py:681
  72.3 1.0 %all-to-all-done.x_ref = bf16[16,72,128]{2,1,0:T(8,128)(2,1)S(1)} async-done(((bf16[16,72,128]{2,1,0:T(8,128)(2,1)}), bf16[16,72,128]{2,1,0:T(8,128)(2,1)S(1)}, u32[]{:S(2)}, u32[]{:S(2)}) %all-to-all-start) | async-done | bytes 294944 | tf_op jit(solution)/shard_map/all_to_all | solution.py:724
  73.3 1.3 %shard_map.79 = bf16[16,72,128]{2,1,0:T(8,128)(2,1)} custom-call(s32[4]{0:T(128)S(1)} %pad_add_fusion.meta, bf16[16,72,128]{2,1,0:T(8,128)(2,1)S(1)} %all-to-all-done.x_ref, bf16[64,128,128]{2,1,0:T(8,128)(2,1)} %get-tuple-element.71._out), custom_call_target="tpu_custom_call" | custom-call | bytes 2097152 | tf_op jit(solution)/shard_map/pallas_call | solution.py:725
  74.6 5.9 %all-to-all-start.1 = ((bf16[16,72,128]{2,1,0:T(8,128)(2,1)}), bf16[16,72,128]{2,1,0:T(8,128)(2,1)S(1)}, u32[]{:S(2)}, u32[]{:S(2)}) async-start(bf16[16,72,128]{2,1,0:T(8,128)(2,1)} %shard_map.79), calls=%async_computation.1 | async-start | bytes 589824 | tf_op jit(solution)/shard_map/all_to_all | solution.py:733
  80.5 0.0 collective-permute-done.5.dnb
  80.5 9.3 %shard_map.76 = (bf16[64,128,128]{2,1,0:T(8,128)(2,1)}, bf16[64,128,128]{2,1,0:T(8,128)(2,1)}) custom-call(s32[4]{0:T(128)S(1)} %pad_add_fusion.meta, f32[608,128]{1,0:T(8,128)S(1)} %shard_map.67._cm.cm, bf16[16,512,128]{2,1,0:T(8,128)(2,1)} %get-tuple-element.51.fxi, ...), custom_call_target="tpu_custom_call", output_to_operand_aliasing={{0}: (19, {}), {1}: (20, {})} | custom-call | flops 48318382080 | bytes 25165824 | tf_op jit(solution)/shard_map/pallas_call | solution.py:734
  89.9 1.1 %all-to-all-done.1 = bf16[16,72,128]{2,1,0:T(8,128)(2,1)S(1)} async-done(((bf16[16,72,128]{2,1,0:T(8,128)(2,1)}), bf16[16,72,128]{2,1,0:T(8,128)(2,1)S(1)}, u32[]{:S(2)}, u32[]{:S(2)}) %all-to-all-start.1) | async-done | bytes 294944 | tf_op jit(solution)/shard_map/all_to_all | solution.py:733
  91.0 0.1 collective-permute-start.7
  91.0 1.6 %collective-permute-done.7.other_ref = bf16[9,128,128]{2,1,0:T(8,128)(2,1)S(1)} collective-permute-done((bf16[9,128,128]{2,1,0:T(8,128)(2,1)S(1)}, bf16[9,128,128]{2,1,0:T(8,128)(2,1)S(1)}, u32[]{:S(2)}, u32[]{:S(2)}) %collective-permute-start.7) | collective-permute-done | bytes 294944 | tf_op jit(solution)/shard_map/ppermute | solution.py:772
  92.6 1.6 %shard_map.81 = f32[2,9,128,128]{3,2,1,0:T(8,128)} custom-call(s32[4]{0:T(128)S(1)} %pad_add_fusion.meta, bf16[9,128,128]{2,1,0:T(8,128)(2,1)S(1)} %shard_map.80.mine_ref, bf16[9,128,128]{2,1,0:T(8,128)(2,1)S(1)} %collective-permute-done.7.other_ref), custom_call_target="tpu_custom_call" | custom-call | bytes 2097152 | tf_op jit(solution)/shard_map/pallas_call | solution.py:773
  (6 shorter events, 0.0 us)
Async XLA Ops:
  3.1 5.2 %collective-permute-start = (bf16[2,64,16,128]{3,2,1,0:T(8,128)(2,1)S(1)}, bf16[2,64,16,128]{3,2,1,0:T(8,128)(2,1)S(1)}, u32[]{:S(2)}, u32[]{:S(2)}) collective-permute-start(bf16[2,64,16,128]{3,2,1,0:T(8,128)(2,1)S(1)} %get-tuple-element.40), channel_id=1, source_target_pairs={{0,1},{1,0},{2,3},{3,2},{4,5},{5,4},{6,7},{7,6},{8,9},{9,8},{10,11... | collective-permute-start | bytes 1572872 | tf_op jit(solution)/shard_map/ppermute | solution.py:574
  3.7 4.7 %collective-permute-start.1 = (bf16[2,64,16,128]{3,2,1,0:T(8,128)(2,1)S(1)}, bf16[2,64,16,128]{3,2,1,0:T(8,128)(2,1)S(1)}, u32[]{:S(2)}, u32[]{:S(2)}) collective-permute-start(bf16[2,64,16,128]{3,2,1,0:T(8,128)(2,1)S(1)} %get-tuple-element.41), channel_id=1, source_target_pairs={{1,2},{2,1},{5,6},{6,5},{9,10},{10,9},{13,14},{14,13},{17,18},{18,... | collective-permute-start | bytes 1572872 | tf_op jit(solution)/shard_map/ppermute | solution.py:573
  5.0 3.1 %copy-start = (bf16[2,3,3,128,128]{4,3,2,1,0:T(8,128)(2,1)S(1)}, bf16[2,3,3,128,128]{4,3,2,1,0:T(8,128)(2,1)}, u32[]{:S(2)}) copy-start(bf16[2,3,3,128,128]{4,3,2,1,0:T(8,128)(2,1)} %k_ref.3) | copy-start | bytes 1769476
  10.1 28.7 %collective-permute-start.2 = (bf16[3,608,128]{2,1,0:T(8,128)(2,1)S(1)}, bf16[3,608,128]{2,1,0:T(8,128)(2,1)S(1)}, u32[]{:S(2)}, u32[]{:S(2)}) collective-permute-start(bf16[3,608,128]{2,1,0:T(8,128)(2,1)S(1)} %get-tuple-element.54), channel_id=1, source_target_pairs={{0,4},{4,8},{8,12},{12,16},{16,20},{20,24},{24,28},{1,5},{5,9},{9,... | collective-permute-start | bytes 1400840 | tf_op jit(solution)/shard_map/ppermute | solution.py:549
  14.6 24.2 %collective-permute-start.3 = (bf16[3,608,128]{2,1,0:T(8,128)(2,1)S(1)}, bf16[3,608,128]{2,1,0:T(8,128)(2,1)S(1)}, u32[]{:S(2)}, u32[]{:S(2)}) collective-permute-start(bf16[3,608,128]{2,1,0:T(8,128)(2,1)S(1)} %get-tuple-element.55), channel_id=1, source_target_pairs={{4,0},{8,4},{12,8},{16,12},{20,16},{24,20},{28,24},{5,1},{9,5},{13... | collective-permute-start | bytes 1400840 | tf_op jit(solution)/shard_map/ppermute | solution.py:549
  31.9 48.6 %collective-permute-start.4 = (bf16[3,608,128]{2,1,0:T(8,128)(2,1)}, bf16[3,608,128]{2,1,0:T(8,128)(2,1)}, u32[]{:S(2)}, u32[]{:S(2)}) collective-permute-start(bf16[3,608,128]{2,1,0:T(8,128)(2,1)} %get-tuple-element.56), channel_id=1, source_target_pairs={{0,4},{4,8},{8,12},{12,16},{16,20},{20,24},{24,28},{1,5},{5,9},{9,... | collective-permute-start | bytes 1400840 | tf_op jit(solution)/shard_map/ppermute | solution.py:549
  37.3 43.3 %collective-permute-start.5 = (bf16[3,608,128]{2,1,0:T(8,128)(2,1)}, bf16[3,608,128]{2,1,0:T(8,128)(2,1)}, u32[]{:S(2)}, u32[]{:S(2)}) collective-permute-start(bf16[3,608,128]{2,1,0:T(8,128)(2,1)} %get-tuple-element.57), channel_id=1, source_target_pairs={{4,0},{8,4},{12,8},{16,12},{20,16},{24,20},{28,24},{5,1},{9,5},{13... | collective-permute-start | bytes 1400840 | tf_op jit(solution)/shard_map/ppermute | solution.py:549
  45.9 6.7 %collective-permute-start.6 = (bf16[9,128,128]{2,1,0:T(8,128)(2,1)S(1)}, bf16[9,128,128]{2,1,0:T(8,128)(2,1)S(1)}, u32[]{:S(2)}, u32[]{:S(2)}) collective-permute-start(bf16[9,128,128]{2,1,0:T(8,128)(2,1)S(1)} %get-tuple-element.76), channel_id=1, source_target_pairs={{0,1},{1,0},{2,3},{3,2},{4,5},{5,4},{6,7},{7,6},{8,9},{9,8},{10,11... | collective-permute-start | bytes 884744 | tf_op jit(solution)/shard_map/ppermute | solution.py:702
  53.5 19.8 %all-to-all-start = ((bf16[16,72,128]{2,1,0:T(8,128)(2,1)}), bf16[16,72,128]{2,1,0:T(8,128)(2,1)S(1)}, u32[]{:S(2)}, u32[]{:S(2)}) async-start(bf16[16,72,128]{2,1,0:T(8,128)(2,1)} %bitcast.3), calls=%async_computation | async-start | bytes 589824 | tf_op jit(solution)/shard_map/all_to_all | solution.py:724
  74.6 16.3 %all-to-all-start.1 = ((bf16[16,72,128]{2,1,0:T(8,128)(2,1)}), bf16[16,72,128]{2,1,0:T(8,128)(2,1)S(1)}, u32[]{:S(2)}, u32[]{:S(2)}) async-start(bf16[16,72,128]{2,1,0:T(8,128)(2,1)} %shard_map.79), calls=%async_computation.1 | async-start | bytes 589824 | tf_op jit(solution)/shard_map/all_to_all | solution.py:733
  91.0 1.6 %collective-permute-start.7 = (bf16[9,128,128]{2,1,0:T(8,128)(2,1)S(1)}, bf16[9,128,128]{2,1,0:T(8,128)(2,1)S(1)}, u32[]{:S(2)}, u32[]{:S(2)}) collective-permute-start(bf16[9,128,128]{2,1,0:T(8,128)(2,1)S(1)} %shard_map.80.mine_ref), channel_id=1, source_target_pairs={{0,1},{1,0},{2,3},{3,2},{4,5},{5,4},{6,7},{7,6},{8,9},{9,8},{10,11... | collective-permute-start | bytes 884744 | tf_op jit(solution)/shard_map/ppermute | solution.py:772

commit v5 on v4

--- a/solution.py
+++ b/solution.py
@@ -87,6 +87,20 @@
     return lax.dot_general(left, right, (((0,), (0,)), ((), ())), preferred_element_type=F32)
 
 
+def gather(total, lefts, rights, inside, reach):
+    runs = {}
+    for b in range(min(inside) - reach, max(inside) + reach + 1):
+        taps = tuple(p for p in range(3) if b - reach * (p - 1) in inside)
+        if taps:
+            runs.setdefault(taps, []).append(b)
+    for taps, rows in runs.items():
+        left = [jnp.concatenate([lefts(b - reach * (p - 1)) for p in taps], axis=1) for b in rows]
+        right = [jnp.concatenate([rights(b, q) for q in range(3)], axis=1) for b in rows]
+        product = outer(jnp.concatenate(left, axis=0), jnp.concatenate(right, axis=0))
+        for i, p in enumerate(taps):
+            total[C * p : C * (p + 1)] += product[C * i : C * (i + 1)]
+
+
 def pack_kernel(k_ref, conv_ref, back_ref, *, conv_layer, back_layer):
     zero = jnp.zeros((C, C), BF16)
 
@@ -115,16 +129,22 @@
     return go
 
 
-def columns_kernel(meta, f, g, near, far, sem, *, cols):
+def columns_kernel(meta, f, g, near, far, raw, sem, *, cols, na):
     last = cols - 16
-    starts = pl.multiple_of((1 - meta[3]) * last, 16), pl.multiple_of(meta[3] * last, 16)
     jobs = []
     go = copier(sem, jobs)
-    for out, start in zip((far, near), starts[::-1]):
+    for i in range(2):
+        start = pl.multiple_of((meta[3] if i == 0 else 1 - meta[3]) * last, 16)
         for n, x in enumerate((f, g)):
-            go(x.at[:, pl.ds(start, 16)], out.at[n])
+            go(x.at[:, pl.ds(start, 16)], raw.at[i, n])
     for c in jobs:
         c.wait()
+    for i, out in enumerate((far, near)):
+        right = meta[3] == 1 - i
+        for n in range(2):
+            for k in range(na):
+                v = to_blocks([raw[i, n, 4 * k + t].astype(F32) for t in range(4)])
+                out[n, k] = jnp.where(right, v[16 * (4 - H) :], v[: 16 * H]).astype(BF16)
 
 
 def layout_kernel(meta, fi, gi, fx, gx, f, g, sem, *, nj, na):
@@ -165,13 +185,8 @@
     s1 = lax.broadcasted_iota(jnp.int32, (1, 16, C), 1)
 
     def halos(n, k):
-        def blocks(ref):
-            return to_blocks([ref[n, 4 * k + t].astype(F32) for t in range(4)])
-
-        ev, od = blocks(ev_ref), blocks(od_ref)
-        low = jnp.where(odd, ev, od)[16 * (4 - H) :]
-        high = jnp.where(odd, od, ev)[: 16 * H]
-        return jnp.concatenate([low, high], axis=0)
+        ev, od = ev_ref[n, k].astype(F32), od_ref[n, k].astype(F32)
+        return jnp.concatenate([jnp.where(odd, ev, od), jnp.where(odd, od, ev)], axis=0)
 
     def extend(k):
         f = halos(0, k).astype(BF16)
@@ -248,35 +263,21 @@
     send(rest, lo)
     send(a1.at[pl.ds(0, 1)], a1o.at[pl.ds(0, 1)])
     send(a1.at[pl.ds(na - 1, 1)], a1o.at[pl.ds(1, 1)])
-    for i in (0, 1, 2, 3):
-        a2[i] = jnp.zeros((m2, C), BF16)
-        a2[na + i] = jnp.zeros((m2, C), BF16)
-    for i in (0, 1, 2):
-        g1[i] = jnp.zeros((m1, C), BF16)
-        g1[na - 1 + i] = jnp.zeros((m1, C), BF16)
-
-    def second(rows):
-        left = [jnp.concatenate([a2[b + 2 + s, 32 : 32 + m0] for s in (2, 0, -2)], axis=1) for b in rows]
-        right = [jnp.concatenate([gx[b, 16 + 32 * q : 16 + 32 * q + m0] for q in range(3)], axis=1) for b in rows]
-        return outer(jnp.concatenate(left, axis=0), jnp.concatenate(right, axis=0))
-
-    def first(rows):
-        left = [jnp.concatenate([g1[b + 1 + s, 16 : 16 + m0] for s in (1, 0, -1)], axis=1) for b in rows]
-        right = [jnp.concatenate([a1[b, 32 + 16 * q : 32 + 16 * q + m0] for q in range(3)], axis=1) for b in rows]
-        return outer(jnp.concatenate(left, axis=0), jnp.concatenate(right, axis=0))
-
-    half = na // 2
-    acc_o[1] = second(range(half))
-    acc_o[1] += second(range(half, na))
-    acc_o[0] = first(range(1, half))
-    acc_o[0] += first(range(half, na - 1))
+    acc_o[...] = jnp.zeros_like(acc_o)
+    inside = range(2, na - 2)
+    gather(
+        acc_o.at[1], lambda l: a2[l + 2, 32 : 32 + m0], lambda b, q: gx[b, 16 + 32 * q : 16 + 32 * q + m0], inside, 2
+    )
+    gather(
+        acc_o.at[0], lambda l: g1[l + 1, 16 : 16 + m0], lambda b, q: a1[b, 32 + 16 * q : 32 + 16 * q + m0], inside, 1
+    )
     for c in out:
         c.wait()
 
 
 def edge_kernel(
     meta, fx, gx, a1, up, dn, wc, wb, acc_i, a2o, so, g1o, lo, keep, send,
-    a2, st, g1, rest, ah, es, cm, kg, sem, *, na, nj,
+    a2, st, g1, rest, ah, es, cm, total, kg, sem, *, na, nj,
 ):
     m0, m1, m2, w = 16 * nj, 16 * (nj + 2), 16 * (nj + 4), 16 * (nj + 6)
     cm[...] = column_mask(meta, nj)
@@ -316,24 +317,23 @@
     for src, dst in ((a2, a2o), (st, so), (g1, g1o), (rest, lo)):
         go(src, dst)
 
-    rows = [(s, b, (na - 2) * s + b) for s in range(2) for b in range(2)]
-    left = jnp.concatenate([a2[s, b, 32 : 32 + m0] for s, b, _ in rows], axis=0)
+    total[...] = acc_i[...]
+    inside = (0, 1, na - 2, na - 1)
+
+    def slot(row):
+        return (0, row) if row < 2 else (1, row - (na - 2))
+
+    gather(
+        total.at[1], lambda l: a2[*slot(l), 32 : 32 + m0], lambda b, q: grad_two(b, 16 + 32 * q, m0), inside, 2
+    )
+    gather(
+        total.at[0], lambda l: g1[*slot(l), 16 : 16 + m0], lambda b, q: act_one(b, 32 + 16 * q, m0), inside, 1
+    )
     for p in range(3):
-        right = [
-            jnp.concatenate([grad_two(row + 2 * (p - 1), 16 + 32 * q, m0) for q in range(3)], axis=1)
-            for _, _, row in rows
-        ]
-        total = acc_i[1, C * p : C * (p + 1)] + outer(left, jnp.concatenate(right, axis=0))
         for q in range(3):
-            kg[1, 3 * (2 - p) + 2 - q] = total[:, C * q : C * (q + 1)]
-    left = jnp.concatenate([g1[s, b, 16 : 16 + m0] for s, b, _ in rows], axis=0)
-    for p in range(3):
-        right = [
-            jnp.concatenate([act_one(row + p - 1, 32 + 16 * q, m0) for q in range(3)], axis=1) for _, _, row in rows
-        ]
-        total = acc_i[0, C * p : C * (p + 1)] + outer(left, jnp.concatenate(right, axis=0))
-        for q in range(3):
-            kg[0, 3 * p + q] = total[:, C * q : C * (q + 1)].T
+            block = slice(C * p, C * (p + 1)), slice(C * q, C * (q + 1))
+            kg[1, 3 * (2 - p) + 2 - q] = total[1, *block]
+            kg[0, 3 * p + q] = total[0, *block].T
     mine = meta[3]
     keep[...] = kg[mine]
     send[...] = kg[1 - mine].astype(BF16)
@@ -559,12 +559,12 @@
     sds = jax.ShapeDtypeStruct
 
     near, far = pl.pallas_call(
-        functools.partial(columns_kernel, cols=cols),
+        functools.partial(columns_kernel, cols=cols, na=na),
         in_specs=[SMEM] + [ANY] * 2,
         out_specs=[VMEM] * 2,
-        out_shape=[pltpu.VMEM((2, rows, 16, C), BF16)] * 2,
-        scratch_shapes=[pltpu.SemaphoreType.DMA((4,))],
-        compiler_params=params(8),
+        out_shape=[pltpu.VMEM((2, na, 16 * H, C), BF16)] * 2,
+        scratch_shapes=[pltpu.VMEM((2, 2, rows, 16, C), BF16), pltpu.SemaphoreType.DMA((4,))],
+        compiler_params=params(10),
         cost_estimate=cost(0, 2 << 20),
     )(meta, *in_hbm(features, cotangent))
     n = lax.axis_size("col")
@@ -671,6 +671,7 @@
             vm((2, w, C), BF16),
             vm((2, 2, m1, C), F32),
             vm((w, C), F32),
+            vm((2, 3 * C, 3 * C), F32),
             vm((2, 9, C, C), F32),
             pltpu.SemaphoreType.DMA((4,)),
         ],

time: 94.7 us -> 92.1 us (0.973)
  starting transfers between devices: 34.3 us -> 32.9 us
  Pallas kernels: 53.5 us -> 52.3 us
    ppermute x1, starting transfers between devices: 5.52 us -> 4.13 us  [body(): received = lax.ppermute(send, 'col', inner)]
    pallas_call x1, Pallas kernels: 15.6 us -> 14.3 us  [body(): pl.pallas_call(functools.partial(inner_kernel, na=na, nj=nj), in_specs=[S...]
where the time goes in v5:
time: 92.1 us; the launch traced here: 91.6 us
  Pallas kernels  52.3 us (57%)
  starting transfers between devices  32.9 us (36%)
  waiting for transfers between devices  4.89 us (5%)
  between operations  1.49 us (2%)
    pallas_call x1, Pallas kernels, body(): pl.pallas_call(functools.partial(inner_kernel, na=na, nj=nj), in_specs=[S...  14.3 us
    ppermute x4, starting transfers between devices, shift(): lax.ppermute(x, axis, [(i, i + step) for i in range(n) if 0 <= i + step <...  12.7 us
    pallas_call x1, Pallas kernels, body(): pl.pallas_call(functools.partial(middle_kernel, na=na, nj=nj), in_specs=[...  9.95 us
    pallas_call x1, Pallas kernels, body(): pl.pallas_call(functools.partial(last_kernel, na=na, nj=nj), in_specs=[SM...  9.31 us
    all_to_all x1, starting transfers between devices, body(): lax.all_to_all(share, axes, 0, 0, axis_index_groups=groups, tiled=True)  8.84 us
    pallas_call x1, Pallas kernels, body(): pl.pallas_call(functools.partial(edge_kernel, na=na, nj=nj), in_specs=[SM...  7.11 us
    all_to_all x1, starting transfers between devices, body(): lax.all_to_all(spread, axes, 0, 0, axis_index_groups=groups, tiled=True)  5.89 us
    ppermute x1, starting transfers between devices, body(): received = lax.ppermute(send, 'col', inner)  4.13 us
  transfers between devices with their start and end apart: 10, of which 4 were waited for; matrix products, arithmetic and copies ran while one was open for 0% of the time, Pallas kernels for 51%

profile of v5, /device:TPU:0, one launch (start us, length us, event | category | flops | bytes accessed | tf_op | source)
XLA Modules:
  0.0 91.6 jit_solution(10798948058776578671)
XLA Ops:
  1.3 0.1 pad_add_fusion.meta
  1.4 2.1 %shard_map.68 = (bf16[2,16,48,128]{3,2,1,0:T(8,128)(2,1)S(1)}, bf16[2,16,48,128]{3,2,1,0:T(8,128)(2,1)S(1)}) custom-call(s32[4]{0:T(128)S(1)} %pad_add_fusion.meta, bf16[64,128,128]{2,1,0:T(8,128)(2,1)} %fi.1, bf16[64,128,128]{2,1,0:T(8,128)(2,1)} %gi.1), custom_call_target="tpu_custom_call" | custom-call | bytes 2097152 | tf_op jit(solution)/shard_map/pallas_call | solution.py:561
  3.4 0.5 collective-permute-start
  3.9 0.7 collective-permute-start.1
  4.6 0.6 shard_map.67._cm.cm
  5.2 0.0 copy-start
  5.2 3.1 %shard_map.69 = (bf16[16,512,128]{2,1,0:T(8,128)(2,1)S(1)}, bf16[16,512,128]{2,1,0:T(8,128)(2,1)S(1)}) custom-call(s32[4]{0:T(128)S(1)} %pad_add_fusion.meta, bf16[64,128,128]{2,1,0:T(8,128)(2,1)} %fi.1, bf16[64,128,128]{2,1,0:T(8,128)(2,1)} %gi.1), custom_call_target="tpu_custom_call" | custom-call | bytes 12582912 | tf_op jit(solution)/shard_map/pallas_call | solution.py:597
  8.3 0.2 shard_map.70
  8.6 0.0 collective-permute-done.ev_ref
  8.6 0.0 collective-permute-done.1.od_ref
  8.6 1.6 %shard_map.71 = (bf16[16,608,128]{2,1,0:T(8,128)(2,1)S(1)}, bf16[16,608,128]{2,1,0:T(8,128)(2,1)S(1)}, bf16[3,608,128]{2,1,0:T(8,128)(2,1)S(1)}, bf16[3,608,128]...) custom-call(s32[4]{0:T(128)S(1)} %pad_add_fusion.meta, ...), custom_call_target="tpu_custom_call" | custom-call | bytes 4194304 | tf_op jit(solution)/shard_map/pallas_call | solution.py:606
  10.3 4.4 %collective-permute-start.2 = (bf16[3,608,128]{2,1,0:T(8,128)(2,1)S(1)}, bf16[3,608,128]{2,1,0:T(8,128)(2,1)S(1)}, u32[]{:S(2)}, u32[]{:S(2)}) collective-permute-start(bf16[3,608,128]{2,1,0:T(8,128)(2,1)S(1)} %get-tuple-element.54), channel_id=1, source_target_pairs={{0,4},{4,8},{8,12},{12,16},{16,20},{20,24},{24,28},{1,5},{5,9},{9,... | collective-permute-start | bytes 1400840 | tf_op jit(solution)/shard_map/ppermute | solution.py:549
  14.7 1.5 %collective-permute-start.3 = (bf16[3,608,128]{2,1,0:T(8,128)(2,1)S(1)}, bf16[3,608,128]{2,1,0:T(8,128)(2,1)S(1)}, u32[]{:S(2)}, u32[]{:S(2)}) collective-permute-start(bf16[3,608,128]{2,1,0:T(8,128)(2,1)S(1)} %get-tuple-element.55), channel_id=1, source_target_pairs={{4,0},{8,4},{12,8},{16,12},{20,16},{24,20},{28,24},{5,1},{9,5},{13... | collective-permute-start | bytes 1400840 | tf_op jit(solution)/shard_map/ppermute | solution.py:549
  16.2 0.2 shard_map.72
  16.5 14.3 %shard_map.73 = (bf16[16,608,128]{2,1,0:T(8,128)(2,1)S(1)}, f32[2,384,384]{2,1,0:T(8,128)S(1)}, bf16[1536,256]{1,0:T(8,128)(2,1)}, bf16[1536,256]{1,0:T(8,128)(2...) custom-call(s32[4]{0:T(128)S(1)} %pad_add_fusion.meta, ...), custom_call_target="tpu_custom_call", output_to_operand_aliasing={{11}: (5, {}), {12}: (6, {})} | custom-call | bytes 1048576 | tf_op jit(solution)/shard_map/pallas_call | solution.py:619
  30.7 5.3 %collective-permute-start.4 = (bf16[3,608,128]{2,1,0:T(8,128)(2,1)}, bf16[3,608,128]{2,1,0:T(8,128)(2,1)}, u32[]{:S(2)}, u32[]{:S(2)}) collective-permute-start(bf16[3,608,128]{2,1,0:T(8,128)(2,1)} %get-tuple-element.56), channel_id=1, source_target_pairs={{0,4},{4,8},{8,12},{12,16},{16,20},{20,24},{24,28},{1,5},{5,9},{9,... | collective-permute-start | bytes 1400840 | tf_op jit(solution)/shard_map/ppermute | solution.py:549
  36.1 1.5 %collective-permute-start.5 = (bf16[3,608,128]{2,1,0:T(8,128)(2,1)}, bf16[3,608,128]{2,1,0:T(8,128)(2,1)}, u32[]{:S(2)}, u32[]{:S(2)}) collective-permute-start(bf16[3,608,128]{2,1,0:T(8,128)(2,1)} %get-tuple-element.57), channel_id=1, source_target_pairs={{4,0},{8,4},{12,8},{16,12},{20,16},{24,20},{28,24},{5,1},{9,5},{13... | collective-permute-start | bytes 1400840 | tf_op jit(solution)/shard_map/ppermute | solution.py:549
  37.6 7.1 %shard_map.74 = (bf16[2,2,576,128]{3,2,1,0:T(8,128)(2,1)}, f32[2,2,512,128]{3,2,1,0:T(8,128)}, bf16[2,2,544,128]{3,2,1,0:T(8,128)(2,1)}, bf16[2,2,512,128]{3,2,1...) custom-call(s32[4]{0:T(128)S(1)} %pad_add_fusion.meta, ...), custom_call_target="tpu_custom_call" | custom-call | bytes 1048576 | tf_op jit(solution)/shard_map/pallas_call | solution.py:654
  44.7 4.1 %collective-permute-start.6 = (bf16[9,128,128]{2,1,0:T(8,128)(2,1)S(1)}, bf16[9,128,128]{2,1,0:T(8,128)(2,1)S(1)}, u32[]{:S(2)}, u32[]{:S(2)}) collective-permute-start(bf16[9,128,128]{2,1,0:T(8,128)(2,1)S(1)} %get-tuple-element.76), channel_id=1, source_target_pairs={{0,1},{1,0},{2,3},{3,2},{4,5},{5,4},{6,7},{7,6},{8,9},{9,8},{10,11... | collective-permute-start | bytes 884744 | tf_op jit(solution)/shard_map/ppermute | solution.py:703
  48.8 1.2 %collective-permute-done.6.y_ref = bf16[9,128,128]{2,1,0:T(8,128)(2,1)S(1)} collective-permute-done((bf16[9,128,128]{2,1,0:T(8,128)(2,1)S(1)}, bf16[9,128,128]{2,1,0:T(8,128)(2,1)S(1)}, u32[]{:S(2)}, u32[]{:S(2)}) %collective-permute-start.6) | collective-permute-done | bytes 294944 | tf_op jit(solution)/shard_map/ppermute | solution.py:703
  50.0 0.8 shard_map.78
  50.8 8.8 %all-to-all-start = ((bf16[16,72,128]{2,1,0:T(8,128)(2,1)}), bf16[16,72,128]{2,1,0:T(8,128)(2,1)S(1)}, u32[]{:S(2)}, u32[]{:S(2)}) async-start(bf16[16,72,128]{2,1,0:T(8,128)(2,1)} %bitcast.3), calls=%async_computation | async-start | bytes 589824 | tf_op jit(solution)/shard_map/all_to_all | solution.py:725
  59.7 9.9 %shard_map.75 = (bf16[64,128,128]{2,1,0:T(8,128)(2,1)}, bf16[64,128,128]{2,1,0:T(8,128)(2,1)}) custom-call(s32[4]{0:T(128)S(1)} %pad_add_fusion.meta, bf16[1536,256]{1,0:T(8,128)(2,1)S(1)} %get-tuple-element.44._w.wc2, bf16[1536,256]{1,0:T(8,128)(2,1)S(1)} %get-tuple-element.58.wb1, bf16[16,512,128]{2,1,0:T(8,128)(2,1)} %get-tuple-element.51.fxi, ...), custom_call_target="tpu_custom_call" | custom-call | flops 48318382080 | bytes 25165824 | tf_op jit(solution)/shard_map/pallas_call | solution.py:682
  69.6 1.0 %all-to-all-done.x_ref = bf16[16,72,128]{2,1,0:T(8,128)(2,1)S(1)} async-done(((bf16[16,72,128]{2,1,0:T(8,128)(2,1)}), bf16[16,72,128]{2,1,0:T(8,128)(2,1)S(1)}, u32[]{:S(2)}, u32[]{:S(2)}) %all-to-all-start) | async-done | bytes 294944 | tf_op jit(solution)/shard_map/all_to_all | solution.py:725
  70.7 1.3 %shard_map.79 = bf16[16,72,128]{2,1,0:T(8,128)(2,1)} custom-call(s32[4]{0:T(128)S(1)} %pad_add_fusion.meta, bf16[16,72,128]{2,1,0:T(8,128)(2,1)S(1)} %all-to-all-done.x_ref, bf16[64,128,128]{2,1,0:T(8,128)(2,1)} %get-tuple-element.71._out), custom_call_target="tpu_custom_call" | custom-call | bytes 2097152 | tf_op jit(solution)/shard_map/pallas_call | solution.py:726
  72.0 5.9 %all-to-all-start.1 = ((bf16[16,72,128]{2,1,0:T(8,128)(2,1)}), bf16[16,72,128]{2,1,0:T(8,128)(2,1)S(1)}, u32[]{:S(2)}, u32[]{:S(2)}) async-start(bf16[16,72,128]{2,1,0:T(8,128)(2,1)} %shard_map.79), calls=%async_computation.1 | async-start | bytes 589824 | tf_op jit(solution)/shard_map/all_to_all | solution.py:734
  77.9 0.0 collective-permute-done.5.dnb
  77.9 9.3 %shard_map.76 = (bf16[64,128,128]{2,1,0:T(8,128)(2,1)}, bf16[64,128,128]{2,1,0:T(8,128)(2,1)}) custom-call(s32[4]{0:T(128)S(1)} %pad_add_fusion.meta, f32[608,128]{1,0:T(8,128)S(1)} %shard_map.67._cm.cm, bf16[16,512,128]{2,1,0:T(8,128)(2,1)} %get-tuple-element.51.fxi, ...), custom_call_target="tpu_custom_call", output_to_operand_aliasing={{0}: (19, {}), {1}: (20, {})} | custom-call | flops 48318382080 | bytes 25165824 | tf_op jit(solution)/shard_map/pallas_call | solution.py:735
  87.2 1.1 %all-to-all-done.1 = bf16[16,72,128]{2,1,0:T(8,128)(2,1)S(1)} async-done(((bf16[16,72,128]{2,1,0:T(8,128)(2,1)}), bf16[16,72,128]{2,1,0:T(8,128)(2,1)S(1)}, u32[]{:S(2)}, u32[]{:S(2)}) %all-to-all-start.1) | async-done | bytes 294944 | tf_op jit(solution)/shard_map/all_to_all | solution.py:734
  88.3 0.1 collective-permute-start.7
  88.4 1.6 %collective-permute-done.7.other_ref = bf16[9,128,128]{2,1,0:T(8,128)(2,1)S(1)} collective-permute-done((bf16[9,128,128]{2,1,0:T(8,128)(2,1)S(1)}, bf16[9,128,128]{2,1,0:T(8,128)(2,1)S(1)}, u32[]{:S(2)}, u32[]{:S(2)}) %collective-permute-start.7) | collective-permute-done | bytes 294944 | tf_op jit(solution)/shard_map/ppermute | solution.py:773
  90.0 1.6 %shard_map.81 = f32[2,9,128,128]{3,2,1,0:T(8,128)} custom-call(s32[4]{0:T(128)S(1)} %pad_add_fusion.meta, bf16[9,128,128]{2,1,0:T(8,128)(2,1)S(1)} %shard_map.80.mine_ref, bf16[9,128,128]{2,1,0:T(8,128)(2,1)S(1)} %collective-permute-done.7.other_ref), custom_call_target="tpu_custom_call" | custom-call | bytes 2097152 | tf_op jit(solution)/shard_map/pallas_call | solution.py:774
  (6 shorter events, 0.0 us)
Async XLA Ops:
  3.4 5.2 %collective-permute-start = (bf16[2,16,48,128]{3,2,1,0:T(8,128)(2,1)S(1)}, bf16[2,16,48,128]{3,2,1,0:T(8,128)(2,1)S(1)}, u32[]{:S(2)}, u32[]{:S(2)}) collective-permute-start(bf16[2,16,48,128]{3,2,1,0:T(8,128)(2,1)S(1)} %get-tuple-element.40), channel_id=1, source_target_pairs={{0,1},{1,0},{2,3},{3,2},{4,5},{5,4},{6,7},{7,6},{8,9},{9,8},{10,11... | collective-permute-start | bytes 1179656 | tf_op jit(solution)/shard_map/ppermute | solution.py:574
  3.9 4.7 %collective-permute-start.1 = (bf16[2,16,48,128]{3,2,1,0:T(8,128)(2,1)S(1)}, bf16[2,16,48,128]{3,2,1,0:T(8,128)(2,1)S(1)}, u32[]{:S(2)}, u32[]{:S(2)}) collective-permute-start(bf16[2,16,48,128]{3,2,1,0:T(8,128)(2,1)S(1)} %get-tuple-element.41), channel_id=1, source_target_pairs={{1,2},{2,1},{5,6},{6,5},{9,10},{10,9},{13,14},{14,13},{17,18},{18,... | collective-permute-start | bytes 1179656 | tf_op jit(solution)/shard_map/ppermute | solution.py:573
  5.2 3.1 %copy-start = (bf16[2,3,3,128,128]{4,3,2,1,0:T(8,128)(2,1)S(1)}, bf16[2,3,3,128,128]{4,3,2,1,0:T(8,128)(2,1)}, u32[]{:S(2)}) copy-start(bf16[2,3,3,128,128]{4,3,2,1,0:T(8,128)(2,1)} %k_ref.3) | copy-start | bytes 1769476
  10.3 27.3 %collective-permute-start.2 = (bf16[3,608,128]{2,1,0:T(8,128)(2,1)S(1)}, bf16[3,608,128]{2,1,0:T(8,128)(2,1)S(1)}, u32[]{:S(2)}, u32[]{:S(2)}) collective-permute-start(bf16[3,608,128]{2,1,0:T(8,128)(2,1)S(1)} %get-tuple-element.54), channel_id=1, source_target_pairs={{0,4},{4,8},{8,12},{12,16},{16,20},{20,24},{24,28},{1,5},{5,9},{9,... | collective-permute-start | bytes 1400840 | tf_op jit(solution)/shard_map/ppermute | solution.py:549
  14.7 22.9 %collective-permute-start.3 = (bf16[3,608,128]{2,1,0:T(8,128)(2,1)S(1)}, bf16[3,608,128]{2,1,0:T(8,128)(2,1)S(1)}, u32[]{:S(2)}, u32[]{:S(2)}) collective-permute-start(bf16[3,608,128]{2,1,0:T(8,128)(2,1)S(1)} %get-tuple-element.55), channel_id=1, source_target_pairs={{4,0},{8,4},{12,8},{16,12},{20,16},{24,20},{28,24},{5,1},{9,5},{13... | collective-permute-start | bytes 1400840 | tf_op jit(solution)/shard_map/ppermute | solution.py:549
  30.7 47.1 %collective-permute-start.4 = (bf16[3,608,128]{2,1,0:T(8,128)(2,1)}, bf16[3,608,128]{2,1,0:T(8,128)(2,1)}, u32[]{:S(2)}, u32[]{:S(2)}) collective-permute-start(bf16[3,608,128]{2,1,0:T(8,128)(2,1)} %get-tuple-element.56), channel_id=1, source_target_pairs={{0,4},{4,8},{8,12},{12,16},{16,20},{20,24},{24,28},{1,5},{5,9},{9,... | collective-permute-start | bytes 1400840 | tf_op jit(solution)/shard_map/ppermute | solution.py:549
  36.1 41.8 %collective-permute-start.5 = (bf16[3,608,128]{2,1,0:T(8,128)(2,1)}, bf16[3,608,128]{2,1,0:T(8,128)(2,1)}, u32[]{:S(2)}, u32[]{:S(2)}) collective-permute-start(bf16[3,608,128]{2,1,0:T(8,128)(2,1)} %get-tuple-element.57), channel_id=1, source_target_pairs={{4,0},{8,4},{12,8},{16,12},{20,16},{24,20},{28,24},{5,1},{9,5},{13... | collective-permute-start | bytes 1400840 | tf_op jit(solution)/shard_map/ppermute | solution.py:549
  44.7 5.3 %collective-permute-start.6 = (bf16[9,128,128]{2,1,0:T(8,128)(2,1)S(1)}, bf16[9,128,128]{2,1,0:T(8,128)(2,1)S(1)}, u32[]{:S(2)}, u32[]{:S(2)}) collective-permute-start(bf16[9,128,128]{2,1,0:T(8,128)(2,1)S(1)} %get-tuple-element.76), channel_id=1, source_target_pairs={{0,1},{1,0},{2,3},{3,2},{4,5},{5,4},{6,7},{7,6},{8,9},{9,8},{10,11... | collective-permute-start | bytes 884744 | tf_op jit(solution)/shard_map/ppermute | solution.py:703
  50.8 19.8 %all-to-all-start = ((bf16[16,72,128]{2,1,0:T(8,128)(2,1)}), bf16[16,72,128]{2,1,0:T(8,128)(2,1)S(1)}, u32[]{:S(2)}, u32[]{:S(2)}) async-start(bf16[16,72,128]{2,1,0:T(8,128)(2,1)} %bitcast.3), calls=%async_computation | async-start | bytes 589824 | tf_op jit(solution)/shard_map/all_to_all | solution.py:725
  72.0 16.3 %all-to-all-start.1 = ((bf16[16,72,128]{2,1,0:T(8,128)(2,1)}), bf16[16,72,128]{2,1,0:T(8,128)(2,1)S(1)}, u32[]{:S(2)}, u32[]{:S(2)}) async-start(bf16[16,72,128]{2,1,0:T(8,128)(2,1)} %shard_map.79), calls=%async_computation.1 | async-start | bytes 589824 | tf_op jit(solution)/shard_map/all_to_all | solution.py:734
  88.3 1.6 %collective-permute-start.7 = (bf16[9,128,128]{2,1,0:T(8,128)(2,1)S(1)}, bf16[9,128,128]{2,1,0:T(8,128)(2,1)S(1)}, u32[]{:S(2)}, u32[]{:S(2)}) collective-permute-start(bf16[9,128,128]{2,1,0:T(8,128)(2,1)S(1)} %shard_map.80.mine_ref), channel_id=1, source_target_pairs={{0,1},{1,0},{2,3},{3,2},{4,5},{5,4},{6,7},{7,6},{8,9},{9,8},{10,11... | collective-permute-start | bytes 884744 | tf_op jit(solution)/shard_map/ppermute | solution.py:773

commit v6 on v5

--- a/solution.py
+++ b/solution.py
@@ -147,7 +147,7 @@
                 out[n, k] = jnp.where(right, v[16 * (4 - H) :], v[: 16 * H]).astype(BF16)
 
 
-def layout_kernel(meta, fi, gi, fx, gx, f, g, sem, *, nj, na):
+def layout_kernel(meta, fi, gi, fx, gx, ax, f, g, sem, *, nj, na):
     m0 = 16 * nj
     jobs = []
     go = copier(sem, jobs)
@@ -169,12 +169,14 @@
         jobs[2 * t].wait()
         jobs[2 * t + 1].wait()
         for k in range(group * t, group * (t + 1)):
-            fx[k] = blocks(f, k).astype(BF16)
-            rm = (meta[0] + 4 * k + (s1 >> 2) < meta[2]).astype(F32)
-            gx[k] = (blocks(g, k).reshape(shape) * (cm * rm)).reshape(m0, C).astype(BF16)
-
-
-def halo_kernel(meta, ev_ref, od_ref, fo, go_ref, _w, _cm, fx, gx, ua, da, ub, db, sem, *, nj, na):
+            mask = (cm * (meta[0] + 4 * k + (s1 >> 2) < meta[2]).astype(F32)).reshape(m0, C)
+            v = blocks(f, k)
+            fx[k] = v.astype(BF16)
+            ax[k] = (elu_parts(v)[0] * mask).astype(BF16)
+            gx[k] = (blocks(g, k) * mask).astype(BF16)
+
+
+def halo_kernel(meta, ev_ref, od_ref, fo, go_ref, ao, _w, _cm, fx, gx, ax, ua, da, ub, db, sem, *, nj, na):
     m0 = 16 * nj
     odd = meta[3] == 1
     shape = (2 * H, 16, C)
@@ -189,10 +191,11 @@
         return jnp.concatenate([jnp.where(odd, ev, od), jnp.where(odd, od, ev)], axis=0)
 
     def extend(k):
-        f = halos(0, k).astype(BF16)
-        rm = (meta[0] + 4 * k + (s1 >> 2) < meta[2]).astype(F32)
-        g = (halos(1, k).reshape(shape) * (cm * rm)).reshape(2 * H * 16, C).astype(BF16)
-        for v, own, ref in ((f, fo, fx), (g, go_ref, gx)):
+        mask = (cm * (meta[0] + 4 * k + (s1 >> 2) < meta[2]).astype(F32)).reshape(2 * H * 16, C)
+        v = halos(0, k)
+        f, a = v.astype(BF16), (elu_parts(v)[0] * mask).astype(BF16)
+        g = (halos(1, k) * mask).astype(BF16)
+        for v, own, ref in ((f, fo, fx), (g, go_ref, gx), (a, ao, ax)):
             ref[k, : 16 * H] = v[: 16 * H]
             ref[k, 16 * H : 16 * H + m0] = own[k]
             ref[k, 16 * H + m0 :] = v[16 * H :]
@@ -215,8 +218,8 @@
 
 
 def inner_kernel(
-    meta, fx, gx, wc, wb, _ub, _db, a1, acc_o, wco, wbo, fxo, gxo, a1o, a2o, so, g1o, lo, _ubo, _dbo,
-    a2, st, g1, rest, es, cm, sem, *, na, nj,
+    meta, fx, gx, a1, wc, wb, wc2, wb1, _ub, _db, acc_o, wco, wbo, fxo, gxo, a1o, a2o, so, g1o, lo, _ubo, _dbo, o, fg,
+    a2, st, g1, rest, es, cm, ot, ft, sem, *, na, nj,
 ):
     m0, m1, m2, w = 16 * nj, 16 * (nj + 2), 16 * (nj + 4), 16 * (nj + 6)
     ni = na - 4
@@ -228,13 +231,6 @@
     for i, row in enumerate((1, 3, na - 4, na - 2)):
         send(gx.at[pl.ds(row, 1)], gxo.at[pl.ds(i, 1)])
     cm[...] = column_mask(meta, nj)
-
-    def activate(a, _):
-        v, _e = elu_parts(fx[a].astype(F32))
-        a1[a] = (v * live(meta, cm, a, 0, w)).astype(BF16)
-        return 0
-
-    lax.fori_loop(0, na, activate, 0)
 
     for t in range(ni // 4):
         r = 2 + 4 * t
@@ -263,6 +259,16 @@
     send(rest, lo)
     send(a1.at[pl.ds(0, 1)], a1o.at[pl.ds(0, 1)])
     send(a1.at[pl.ds(na - 1, 1)], a1o.at[pl.ds(1, 1)])
+    for i, t in enumerate(middle_quads(na)):
+        r = 2 + 4 * t
+        acc2 = conv_pairs(lambda row, q: a2[row + 2, 32 * q : 32 * q + m0], [r, r + 1], 2, wc2[...])
+        acc1 = conv_pairs(lambda row, q: g1[row + 1, 16 * q : 16 * q + m0], [r, r + 2], 1, wb1[...])
+        finish_quad(
+            meta, cm, r, acc2, acc1, lambda row: st[row - 2], lambda row: g1[row + 1, 16 : 16 + m0],
+            lambda row: rest[row - 2], lambda row: fx[row, 16 * H : 16 * H + m0], ot, ft, 16 * i,
+        )
+        send(ot.at[pl.ds(16 * i, 16)], o.at[pl.ds(4 * r, 16)])
+        send(ft.at[pl.ds(16 * i, 16)], fg.at[pl.ds(4 * r, 16)])
     acc_o[...] = jnp.zeros_like(acc_o)
     inside = range(2, na - 2)
     gather(
@@ -353,9 +359,28 @@
     return from_blocks(grads + live(meta, cm, row, 16 * H, m0) * slope * product)
 
 
+def middle_quads(na):
+    return [t for t in range((na - 4) // 4) if 2 + 4 * t >= 4 and 2 + 4 * t + 5 <= na - 3]
+
+
+def finish_quad(meta, cm, r, acc2, acc1, state, rounded, rest, feats, ot, ft, at):
+    m0 = acc2.shape[0] // 2
+    for k in range(2):
+        for b in range(2):
+            row = r + k + 2 * b
+            product = acc2[k * m0 : (k + 1) * m0, b * C : (b + 1) * C]
+            for i, x in enumerate(finish_state(meta, cm, row, state(row), product)):
+                ot[at + 4 * (row - r) + i] = x.astype(BF16)
+            row = r + 2 * k + b
+            product = acc1[k * m0 : (k + 1) * m0, b * C : (b + 1) * C]
+            parts = finish_gradient(meta, cm, row, rounded(row), rest(row), feats(row), product)
+            for i, x in enumerate(parts):
+                ft[at + 4 * (row - r) + i] = x.astype(BF16)
+
+
 def middle_kernel(
-    meta, wc2, wb1, fxi, a2i, a2e, si, g1i, g1e, loi, out, fg,
-    fm, a2, st, g1, lo, cm, ot, ft, sem, osem, *, na, nj,
+    meta, wc2, wb1, fxi, a2i, a2e, si, g1i, g1e, loi, _out, _fg, out, fg,
+    fm, a2, st, g1, lo, cm, ot, ft, sem, *, na, nj,
 ):
     m0 = 16 * nj
     ni = na - 4
@@ -379,43 +404,36 @@
             fetch(t, a2i, a2e, a2, 2)
             fetch(t, g1i, g1e, g1, 1)
         here = pl.ds(4 * t, 4)
-        go(si.at[here], st.at[here])
-        go(fxi.at[pl.ds(2 + 4 * t, 4)], fm.at[here])
-        go(loi.at[here], lo.at[here])
+        if t not in middle_quads(na):
+            go(si.at[here], st.at[here])
+            go(fxi.at[pl.ds(2 + 4 * t, 4)], fm.at[here])
+            go(loi.at[here], lo.at[here])
         if t == 0:
             stage_three = len(jobs)
     cm[...] = column_mask(meta, nj)
+    loads = len(jobs)
+    rest_of = [t for t in range(quads) if t not in middle_quads(na)]
 
     def arrive(first, last):
         for c in jobs[first:last]:
             c.wait()
 
-    for t in range(quads):
+    for t in rest_of:
         r = 2 + 4 * t
         if t == 0:
             arrive(0, stage_three)
-        elif t == 1:
-            arrive(stage_three, len(jobs))
+        elif t == rest_of[1]:
+            arrive(stage_three, loads)
         acc2 = conv_pairs(lambda row, q: a2[row, 32 * q : 32 * q + m0], [r, r + 1], 2, wc2[...])
         acc1 = conv_pairs(lambda row, q: g1[row, 16 * q : 16 * q + m0], [r, r + 2], 1, wb1[...])
-        for k in range(2):
-            for b in range(2):
-                row = r + k + 2 * b
-                product = acc2[k * m0 : (k + 1) * m0, b * C : (b + 1) * C]
-                for i, x in enumerate(finish_state(meta, cm, row, st[row - 2], product)):
-                    ot[4 * (row - 2) + i] = x.astype(BF16)
-                row = r + 2 * k + b
-                product = acc1[k * m0 : (k + 1) * m0, b * C : (b + 1) * C]
-                parts = finish_gradient(
-                    meta, cm, row, g1[row, 16 : 16 + m0], lo[row - 2], fm[row - 2], product
-                )
-                for i, x in enumerate(parts):
-                    ft[4 * (row - 2) + i] = x.astype(BF16)
+        finish_quad(
+            meta, cm, r, acc2, acc1, lambda row: st[row - 2], lambda row: g1[row, 16 : 16 + m0],
+            lambda row: lo[row - 2], lambda row: fm[row - 2], ot, ft, 16 * t,
+        )
         here, there = pl.ds(16 * t, 16), pl.ds(16 * t + 8, 16)
-        pltpu.make_async_copy(ot.at[here], out.at[there], osem.at[0]).start()
-        pltpu.make_async_copy(ft.at[here], fg.at[there], osem.at[1]).start()
-    pltpu.make_async_copy(ot, out.at[pl.ds(8, 4 * ni)], osem.at[0]).wait()
-    pltpu.make_async_copy(ft, fg.at[pl.ds(8, 4 * ni)], osem.at[1]).wait()
+        go(ot.at[here], out.at[there])
+        go(ft.at[here], fg.at[there])
+    arrive(loads, len(jobs))
 
 
 def mask_kernel(meta, cm, *, nj):
@@ -594,34 +612,33 @@
         cost_estimate=cost(0, 1 << 20),
     )(meta)
     vm, hbm = pltpu.VMEM, pltpu.HBM
-    fx, gx = pl.pallas_call(
+    fx, gx, a1 = pl.pallas_call(
         functools.partial(layout_kernel, nj=nj, na=na),
         in_specs=[SMEM] + [ANY] * 2,
-        out_specs=[VMEM] * 2,
-        out_shape=[vm((na, m0, C), BF16)] * 2,
+        out_specs=[VMEM] * 3,
+        out_shape=[vm((na, m0, C), BF16)] * 3,
         scratch_shapes=[vm(features.shape, BF16), vm(features.shape, BF16), pltpu.SemaphoreType.DMA((8,))],
         compiler_params=params(16),
         cost_estimate=cost(0, 12 << 20),
     )(meta, *in_hbm(features, cotangent))
-    fx, gx, ua, da, ub, db = pl.pallas_call(
+    fx, gx, a1, ua, da, ub, db = pl.pallas_call(
         functools.partial(halo_kernel, nj=nj, na=na),
-        in_specs=[SMEM] + [VMEM] * 4 + [ANY] * 2,
-        out_specs=[VMEM] * 4 + [ANY] * 2,
-        out_shape=[vm((na, w, C), BF16)] * 2 + [vm((3, w, C), BF16)] * 2 + [hbm((3, w, C), BF16)] * 2,
+        in_specs=[SMEM] + [VMEM] * 5 + [ANY] * 2,
+        out_specs=[VMEM] * 5 + [ANY] * 2,
+        out_shape=[vm((na, w, C), BF16)] * 3 + [vm((3, w, C), BF16)] * 2 + [hbm((3, w, C), BF16)] * 2,
         scratch_shapes=[pltpu.SemaphoreType.DMA((4,))],
         compiler_params=params(12),
         cost_estimate=cost(0, 4 << 20),
-    )(meta, ev, od, *in_vmem(fx, gx), w_two, cm)
+    )(meta, ev, od, *in_vmem(fx, gx, a1), w_two, cm)
     dna = shift(ua, "row", -1)
     upa = shift(da, "row", 1)
 
     conv_flops = 2 * rows * cols * 9 * C * C
-    a1, acc, w_one_far, w_two_back_far, fxo, gxo, a1o, a2, st, g1, lo, ub, db = pl.pallas_call(
+    acc, w_one_far, w_two_back_far, fxo, gxo, a1o, a2, st, g1, lo, ub, db, out, fg = pl.pallas_call(
         functools.partial(inner_kernel, na=na, nj=nj),
-        in_specs=[SMEM] + [VMEM] * 4 + [ANY] * 2,
-        out_specs=[VMEM] * 2 + [ANY] * 11,
+        in_specs=[SMEM] + [VMEM] * 7 + [ANY] * 2,
+        out_specs=[VMEM] + [ANY] * 13,
         out_shape=[
-            vm((na, w, C), BF16),
             vm((2, 3 * C, 3 * C), F32),
             hbm((12 * C, 2 * C), BF16),
             hbm((12 * C, 2 * C), BF16),
@@ -634,6 +651,8 @@
             hbm((ni, m0, C), BF16),
             hbm((3, w, C), BF16),
             hbm((3, w, C), BF16),
+            hbm(features.shape, BF16),
+            hbm(features.shape, BF16),
         ],
         scratch_shapes=[
             vm((na + 4, m2, C), BF16),
@@ -642,12 +661,14 @@
             vm((ni, m0, C), BF16),
             vm((ni, m1, C), F32),
             vm((w, C), F32),
-            pltpu.SemaphoreType.DMA((13,)),
+            vm((16 * max(1, len(middle_quads(na))), cols, C), BF16),
+            vm((16 * max(1, len(middle_quads(na))), cols, C), BF16),
+            pltpu.SemaphoreType.DMA((13 + 2 * len(middle_quads(na)),)),
         ],
-        input_output_aliases={5: 11, 6: 12},
+        input_output_aliases={8: 10, 9: 11},
         compiler_params=params(30),
         cost_estimate=cost(0, 1 << 20),
-    )(meta, *in_vmem(fx, gx, w_one, w_two_back), *in_hbm(ub, db))
+    )(meta, *in_vmem(fx, gx, a1, w_one, w_two_back, w_two, w_one_back), *in_hbm(ub, db))
     dnb = shift(ub, "row", -1)
     upb = shift(db, "row", 1)
 
@@ -681,7 +702,7 @@
 
     out, fg = pl.pallas_call(
         functools.partial(middle_kernel, na=na, nj=nj),
-        in_specs=[SMEM] + [VMEM] * 2 + [ANY] * 7,
+        in_specs=[SMEM] + [VMEM] * 2 + [ANY] * 9,
         out_specs=[ANY] * 2,
         out_shape=[hbm(features.shape, BF16)] * 2,
         scratch_shapes=[
@@ -693,12 +714,12 @@
             vm((w, C), F32),
             vm((4 * ni, cols, C), BF16),
             vm((4 * ni, cols, C), BF16),
-            pltpu.SemaphoreType.DMA((4 + 5 * (ni // 4),)),
-            pltpu.SemaphoreType.DMA((2,)),
+            pltpu.SemaphoreType.DMA((4 + 7 * (ni // 4),)),
         ],
+        input_output_aliases={10: 0, 11: 1},
         compiler_params=params(28),
         cost_estimate=cost(20 * conv_flops, 24 << 20),
-    )(meta, *in_vmem(w_two, w_one_back), *in_hbm(fxo, a2, a2e, st, g1, g1e, lo))
+    )(meta, *in_vmem(w_two, w_one_back), *in_hbm(fxo, a2, a2e, st, g1, g1e, lo, out, fg))
 
     received = lax.ppermute(send, "col", inner)
     axes = ("row", "col")

time: 92.1 us -> 90.9 us (0.987)
  starting transfers between devices: 32.9 us -> 29.9 us
  waiting for transfers between devices: 4.89 us -> 6.79 us
    pallas_call x1, Pallas kernels: 9.95 us -> 8.07 us  [body(): pl.pallas_call(functools.partial(middle_kernel, na=na, nj=nj), in_specs=[...]
    all_to_all x1, waiting for transfers between devices: 1.03 us -> 2.91 us  [body(): lax.all_to_all(share, axes, 0, 0, axis_index_groups=groups, tiled=True)]
    all_to_all x1, starting transfers between devices: 5.89 us -> 4.02 us  [body(): lax.all_to_all(spread, axes, 0, 0, axis_index_groups=groups, tiled=True)]
    ppermute x1, starting transfers between devices: 4.13 us -> 3.06 us  [body(): received = lax.ppermute(send, 'col', inner)]
    pallas_call x1, Pallas kernels: 3.07 us -> 4.13 us  [body(): pl.pallas_call(functools.partial(layout_kernel, nj=nj, na=na), in_specs=[...]
  transfers between devices with their start and end apart: 10 -> 10, of which waited for: 4 -> 4; matrix products, arithmetic and copies ran while one was open for 0% -> 0% of each run, Pallas kernels for 51% -> 52%
where the time goes in v6:
time: 90.9 us; the launch traced here: 90.5 us
  Pallas kernels  52.2 us (57%)
  starting transfers between devices  29.9 us (33%)
  waiting for transfers between devices  6.79 us (7%)
  between operations  1.49 us (2%)
    pallas_call x1, Pallas kernels, body(): pl.pallas_call(functools.partial(inner_kernel, na=na, nj=nj), in_specs=[S...  14.9 us
    ppermute x4, starting transfers between devices, shift(): lax.ppermute(x, axis, [(i, i + step) for i in range(n) if 0 <= i + step <...  12.7 us
    pallas_call x1, Pallas kernels, body(): pl.pallas_call(functools.partial(last_kernel, na=na, nj=nj), in_specs=[SM...  9.3 us
    all_to_all x1, starting transfers between devices, body(): lax.all_to_all(share, axes, 0, 0, axis_index_groups=groups, tiled=True)  8.84 us
    pallas_call x1, Pallas kernels, body(): pl.pallas_call(functools.partial(middle_kernel, na=na, nj=nj), in_specs=[...  8.07 us
    pallas_call x1, Pallas kernels, body(): pl.pallas_call(functools.partial(edge_kernel, na=na, nj=nj), in_specs=[SM...  7.11 us
    pallas_call x1, Pallas kernels, body(): pl.pallas_call(functools.partial(layout_kernel, nj=nj, na=na), in_specs=[...  4.13 us
    all_to_all x1, starting transfers between devices, body(): lax.all_to_all(spread, axes, 0, 0, axis_index_groups=groups, tiled=True)  4.02 us
  transfers between devices with their start and end apart: 10, of which 4 were waited for; matrix products, arithmetic and copies ran while one was open for 0% of the time, Pallas kernels for 52%

profile of v6, /device:TPU:0, one launch (start us, length us, event | category | flops | bytes accessed | tf_op | source)
XLA Modules:
  0.0 90.5 jit_solution(9646310139872308398)
XLA Ops:
  1.3 0.1 pad_add_fusion.meta
  1.4 2.1 %shard_map.68 = (bf16[2,16,48,128]{3,2,1,0:T(8,128)(2,1)S(1)}, bf16[2,16,48,128]{3,2,1,0:T(8,128)(2,1)S(1)}) custom-call(s32[4]{0:T(128)S(1)} %pad_add_fusion.meta, bf16[64,128,128]{2,1,0:T(8,128)(2,1)} %fi.1, bf16[64,128,128]{2,1,0:T(8,128)(2,1)} %gi.1), custom_call_target="tpu_custom_call" | custom-call | bytes 2097152 | tf_op jit(solution)/shard_map/pallas_call | solution.py:579
  3.4 0.5 collective-permute-start
  3.9 0.7 collective-permute-start.1
  4.6 0.6 shard_map.67._cm.cm
  5.2 0.0 copy-start
  5.2 4.1 %shard_map.69 = (bf16[16,512,128]{2,1,0:T(8,128)(2,1)S(1)}, bf16[16,512,128]{2,1,0:T(8,128)(2,1)S(1)}, bf16[16,512,128]{2,1,0:T(8,128)(2,1)S(1)}) custom-call(s32[4]{0:T(128)S(1)} %pad_add_fusion.meta, bf16[64,128,128]{2,1,0:T(8,128)(2,1)} %fi.1, bf16[64,128,128]{2,1,0:T(8,128)(2,1)} %gi.1), custom_call_target="tpu_custom_call" | custom-call | bytes 12582912 | tf_op jit(solution)/shard_map/pallas_call | solution.py:615
  9.4 0.2 shard_map.70
  9.7 0.0 collective-permute-done.1.od_ref
  9.7 1.8 %shard_map.71 = (bf16[16,608,128]{2,1,0:T(8,128)(2,1)S(1)}, bf16[16,608,128]{2,1,0:T(8,128)(2,1)S(1)}, bf16[16,608,128]{2,1,0:T(8,128)(2,1)S(1)}, bf16[3,608,128...) custom-call(s32[4]{0:T(128)S(1)} %pad_add_fusion.meta, ...), custom_call_target="tpu_custom_call" | custom-call | bytes 4194304 | tf_op jit(solution)/shard_map/pallas_call | solution.py:624
  11.4 4.4 %collective-permute-start.2 = (bf16[3,608,128]{2,1,0:T(8,128)(2,1)S(1)}, bf16[3,608,128]{2,1,0:T(8,128)(2,1)S(1)}, u32[]{:S(2)}, u32[]{:S(2)}) collective-permute-start(bf16[3,608,128]{2,1,0:T(8,128)(2,1)S(1)} %get-tuple-element.60), channel_id=1, source_target_pairs={{0,4},{4,8},{8,12},{12,16},{16,20},{20,24},{24,28},{1,5},{5,9},{9,... | collective-permute-start | bytes 1400840 | tf_op jit(solution)/shard_map/ppermute | solution.py:567
  15.9 1.5 %collective-permute-start.3 = (bf16[3,608,128]{2,1,0:T(8,128)(2,1)S(1)}, bf16[3,608,128]{2,1,0:T(8,128)(2,1)S(1)}, u32[]{:S(2)}, u32[]{:S(2)}) collective-permute-start(bf16[3,608,128]{2,1,0:T(8,128)(2,1)S(1)} %get-tuple-element.61), channel_id=1, source_target_pairs={{4,0},{8,4},{12,8},{16,12},{20,16},{24,20},{28,24},{5,1},{9,5},{13... | collective-permute-start | bytes 1400840 | tf_op jit(solution)/shard_map/ppermute | solution.py:567
  17.4 0.2 shard_map.72
  17.6 14.9 %shard_map.73 = (f32[2,384,384]{2,1,0:T(8,128)S(1)}, bf16[1536,256]{1,0:T(8,128)(2,1)}, bf16[1536,256]{1,0:T(8,128)(2,1)}, bf16[16,512,128]{2,1,0:T(8,128)(2,1)}...) custom-call(s32[4]{0:T(128)S(1)} %pad_add_fusion.meta, ...), custom_call_target="tpu_custom_call", output_to_operand_aliasing={{10}: (8, {}), {11}: (9, {})} | custom-call | bytes 1048576 | tf_op jit(solution)/shard_map/pallas_call | solution.py:637
  32.5 5.3 %collective-permute-start.4 = (bf16[3,608,128]{2,1,0:T(8,128)(2,1)}, bf16[3,608,128]{2,1,0:T(8,128)(2,1)}, u32[]{:S(2)}, u32[]{:S(2)}) collective-permute-start(bf16[3,608,128]{2,1,0:T(8,128)(2,1)} %get-tuple-element.62), channel_id=1, source_target_pairs={{0,4},{4,8},{8,12},{12,16},{16,20},{20,24},{24,28},{1,5},{5,9},{9,... | collective-permute-start | bytes 1400840 | tf_op jit(solution)/shard_map/ppermute | solution.py:567
  37.9 1.5 %collective-permute-start.5 = (bf16[3,608,128]{2,1,0:T(8,128)(2,1)}, bf16[3,608,128]{2,1,0:T(8,128)(2,1)}, u32[]{:S(2)}, u32[]{:S(2)}) collective-permute-start(bf16[3,608,128]{2,1,0:T(8,128)(2,1)} %get-tuple-element.63), channel_id=1, source_target_pairs={{4,0},{8,4},{12,8},{16,12},{20,16},{24,20},{28,24},{5,1},{9,5},{13... | collective-permute-start | bytes 1400840 | tf_op jit(solution)/shard_map/ppermute | solution.py:567
  39.4 0.0 collective-permute-done.2.up.upa
  39.4 0.0 collective-permute-done.3.dn.dna
  39.4 7.1 %shard_map.74 = (bf16[2,2,576,128]{3,2,1,0:T(8,128)(2,1)}, f32[2,2,512,128]{3,2,1,0:T(8,128)}, bf16[2,2,544,128]{3,2,1,0:T(8,128)(2,1)}, bf16[2,2,512,128]{3,2,1...) custom-call(s32[4]{0:T(128)S(1)} %pad_add_fusion.meta, ...), custom_call_target="tpu_custom_call" | custom-call | bytes 1048576 | tf_op jit(solution)/shard_map/pallas_call | solution.py:675
  46.5 3.1 %collective-permute-start.6 = (bf16[9,128,128]{2,1,0:T(8,128)(2,1)S(1)}, bf16[9,128,128]{2,1,0:T(8,128)(2,1)S(1)}, u32[]{:S(2)}, u32[]{:S(2)}) collective-permute-start(bf16[9,128,128]{2,1,0:T(8,128)(2,1)S(1)} %get-tuple-element.82), channel_id=1, source_target_pairs={{0,1},{1,0},{2,3},{3,2},{4,5},{5,4},{6,7},{7,6},{8,9},{9,8},{10,11... | collective-permute-start | bytes 884744 | tf_op jit(solution)/shard_map/ppermute | solution.py:724
  49.6 1.2 %collective-permute-done.6.y_ref = bf16[9,128,128]{2,1,0:T(8,128)(2,1)S(1)} collective-permute-done((bf16[9,128,128]{2,1,0:T(8,128)(2,1)S(1)}, bf16[9,128,128]{2,1,0:T(8,128)(2,1)S(1)}, u32[]{:S(2)}, u32[]{:S(2)}) %collective-permute-start.6) | collective-permute-done | bytes 294944 | tf_op jit(solution)/shard_map/ppermute | solution.py:724
  50.8 0.8 shard_map.78
  51.6 8.8 %all-to-all-start = ((bf16[16,72,128]{2,1,0:T(8,128)(2,1)}), bf16[16,72,128]{2,1,0:T(8,128)(2,1)S(1)}, u32[]{:S(2)}, u32[]{:S(2)}) async-start(bf16[16,72,128]{2,1,0:T(8,128)(2,1)} %bitcast.3), calls=%async_computation | async-start | bytes 589824 | tf_op jit(solution)/shard_map/all_to_all | solution.py:746
  60.4 8.1 %shard_map.75 = (bf16[64,128,128]{2,1,0:T(8,128)(2,1)}, bf16[64,128,128]{2,1,0:T(8,128)(2,1)}) custom-call(s32[4]{0:T(128)S(1)} %pad_add_fusion.meta, bf16[1536,256]{1,0:T(8,128)(2,1)S(1)} %get-tuple-element.48._w.wc2, bf16[1536,256]{1,0:T(8,128)(2,1)S(1)} %get-tuple-element.54.wb1, ...), custom_call_target="tpu_custom_call", output_to_operand_aliasing={{0}: (10, {}), {1}: (11, {})} | custom-call | flops 48318382080 | bytes 25165824 | tf_op jit(solution)/shard_map/pallas_call | solution.py:703
  68.5 2.9 %all-to-all-done.x_ref = bf16[16,72,128]{2,1,0:T(8,128)(2,1)S(1)} async-done(((bf16[16,72,128]{2,1,0:T(8,128)(2,1)}), bf16[16,72,128]{2,1,0:T(8,128)(2,1)S(1)}, u32[]{:S(2)}, u32[]{:S(2)}) %all-to-all-start) | async-done | bytes 294944 | tf_op jit(solution)/shard_map/all_to_all | solution.py:746
  71.4 1.3 %shard_map.79 = bf16[16,72,128]{2,1,0:T(8,128)(2,1)} custom-call(s32[4]{0:T(128)S(1)} %pad_add_fusion.meta, bf16[16,72,128]{2,1,0:T(8,128)(2,1)S(1)} %all-to-all-done.x_ref, bf16[64,128,128]{2,1,0:T(8,128)(2,1)} %get-tuple-element.77._out), custom_call_target="tpu_custom_call" | custom-call | bytes 2097152 | tf_op jit(solution)/shard_map/pallas_call | solution.py:747
  72.7 4.0 %all-to-all-start.1 = ((bf16[16,72,128]{2,1,0:T(8,128)(2,1)}), bf16[16,72,128]{2,1,0:T(8,128)(2,1)S(1)}, u32[]{:S(2)}, u32[]{:S(2)}) async-start(bf16[16,72,128]{2,1,0:T(8,128)(2,1)} %shard_map.79), calls=%async_computation.1 | async-start | bytes 589824 | tf_op jit(solution)/shard_map/all_to_all | solution.py:755
  76.8 9.3 %shard_map.76 = (bf16[64,128,128]{2,1,0:T(8,128)(2,1)}, bf16[64,128,128]{2,1,0:T(8,128)(2,1)}) custom-call(s32[4]{0:T(128)S(1)} %pad_add_fusion.meta, f32[608,128]{1,0:T(8,128)S(1)} %shard_map.67._cm.cm, bf16[16,512,128]{2,1,0:T(8,128)(2,1)} %get-tuple-element.57.fxi, ...), custom_call_target="tpu_custom_call", output_to_operand_aliasing={{0}: (19, {}), {1}: (20, {})} | custom-call | flops 48318382080 | bytes 25165824 | tf_op jit(solution)/shard_map/pallas_call | solution.py:756
  86.1 1.1 %all-to-all-done.1 = bf16[16,72,128]{2,1,0:T(8,128)(2,1)S(1)} async-done(((bf16[16,72,128]{2,1,0:T(8,128)(2,1)}), bf16[16,72,128]{2,1,0:T(8,128)(2,1)S(1)}, u32[]{:S(2)}, u32[]{:S(2)}) %all-to-all-start.1) | async-done | bytes 294944 | tf_op jit(solution)/shard_map/all_to_all | solution.py:755
  87.2 0.1 collective-permute-start.7
  87.3 1.6 %collective-permute-done.7.other_ref = bf16[9,128,128]{2,1,0:T(8,128)(2,1)S(1)} collective-permute-done((bf16[9,128,128]{2,1,0:T(8,128)(2,1)S(1)}, bf16[9,128,128]{2,1,0:T(8,128)(2,1)S(1)}, u32[]{:S(2)}, u32[]{:S(2)}) %collective-permute-start.7) | collective-permute-done | bytes 294944 | tf_op jit(solution)/shard_map/ppermute | solution.py:794
  88.8 1.6 %shard_map.81 = f32[2,9,128,128]{3,2,1,0:T(8,128)} custom-call(s32[4]{0:T(128)S(1)} %pad_add_fusion.meta, bf16[9,128,128]{2,1,0:T(8,128)(2,1)S(1)} %shard_map.80.mine_ref, bf16[9,128,128]{2,1,0:T(8,128)(2,1)S(1)} %collective-permute-done.7.other_ref), custom_call_target="tpu_custom_call" | custom-call | bytes 2097152 | tf_op jit(solution)/shard_map/pallas_call | solution.py:795
  (6 shorter events, 0.0 us)
Async XLA Ops:
  3.4 6.2 %collective-permute-start = (bf16[2,16,48,128]{3,2,1,0:T(8,128)(2,1)S(1)}, bf16[2,16,48,128]{3,2,1,0:T(8,128)(2,1)S(1)}, u32[]{:S(2)}, u32[]{:S(2)}) collective-permute-start(bf16[2,16,48,128]{3,2,1,0:T(8,128)(2,1)S(1)} %get-tuple-element.43), channel_id=1, source_target_pairs={{0,1},{1,0},{2,3},{3,2},{4,5},{5,4},{6,7},{7,6},{8,9},{9,8},{10,11... | collective-permute-start | bytes 1179656 | tf_op jit(solution)/shard_map/ppermute | solution.py:592
  3.9 5.7 %collective-permute-start.1 = (bf16[2,16,48,128]{3,2,1,0:T(8,128)(2,1)S(1)}, bf16[2,16,48,128]{3,2,1,0:T(8,128)(2,1)S(1)}, u32[]{:S(2)}, u32[]{:S(2)}) collective-permute-start(bf16[2,16,48,128]{3,2,1,0:T(8,128)(2,1)S(1)} %get-tuple-element.44), channel_id=1, source_target_pairs={{1,2},{2,1},{5,6},{6,5},{9,10},{10,9},{13,14},{14,13},{17,18},{18,... | collective-permute-start | bytes 1179656 | tf_op jit(solution)/shard_map/ppermute | solution.py:591
  5.2 4.1 %copy-start = (bf16[2,3,3,128,128]{4,3,2,1,0:T(8,128)(2,1)S(1)}, bf16[2,3,3,128,128]{4,3,2,1,0:T(8,128)(2,1)}, u32[]{:S(2)}) copy-start(bf16[2,3,3,128,128]{4,3,2,1,0:T(8,128)(2,1)} %k_ref.3) | copy-start | bytes 1769476
  11.4 27.9 %collective-permute-start.2 = (bf16[3,608,128]{2,1,0:T(8,128)(2,1)S(1)}, bf16[3,608,128]{2,1,0:T(8,128)(2,1)S(1)}, u32[]{:S(2)}, u32[]{:S(2)}) collective-permute-start(bf16[3,608,128]{2,1,0:T(8,128)(2,1)S(1)} %get-tuple-element.60), channel_id=1, source_target_pairs={{0,4},{4,8},{8,12},{12,16},{16,20},{20,24},{24,28},{1,5},{5,9},{9,... | collective-permute-start | bytes 1400840 | tf_op jit(solution)/shard_map/ppermute | solution.py:567
  15.9 23.5 %collective-permute-start.3 = (bf16[3,608,128]{2,1,0:T(8,128)(2,1)S(1)}, bf16[3,608,128]{2,1,0:T(8,128)(2,1)S(1)}, u32[]{:S(2)}, u32[]{:S(2)}) collective-permute-start(bf16[3,608,128]{2,1,0:T(8,128)(2,1)S(1)} %get-tuple-element.61), channel_id=1, source_target_pairs={{4,0},{8,4},{12,8},{16,12},{20,16},{24,20},{28,24},{5,1},{9,5},{13... | collective-permute-start | bytes 1400840 | tf_op jit(solution)/shard_map/ppermute | solution.py:567
  32.5 44.2 %collective-permute-start.4 = (bf16[3,608,128]{2,1,0:T(8,128)(2,1)}, bf16[3,608,128]{2,1,0:T(8,128)(2,1)}, u32[]{:S(2)}, u32[]{:S(2)}) collective-permute-start(bf16[3,608,128]{2,1,0:T(8,128)(2,1)} %get-tuple-element.62), channel_id=1, source_target_pairs={{0,4},{4,8},{8,12},{12,16},{16,20},{20,24},{24,28},{1,5},{5,9},{9,... | collective-permute-start | bytes 1400840 | tf_op jit(solution)/shard_map/ppermute | solution.py:567
  37.9 38.9 %collective-permute-start.5 = (bf16[3,608,128]{2,1,0:T(8,128)(2,1)}, bf16[3,608,128]{2,1,0:T(8,128)(2,1)}, u32[]{:S(2)}, u32[]{:S(2)}) collective-permute-start(bf16[3,608,128]{2,1,0:T(8,128)(2,1)} %get-tuple-element.63), channel_id=1, source_target_pairs={{4,0},{8,4},{12,8},{16,12},{20,16},{24,20},{28,24},{5,1},{9,5},{13... | collective-permute-start | bytes 1400840 | tf_op jit(solution)/shard_map/ppermute | solution.py:567
  46.5 4.3 %collective-permute-start.6 = (bf16[9,128,128]{2,1,0:T(8,128)(2,1)S(1)}, bf16[9,128,128]{2,1,0:T(8,128)(2,1)S(1)}, u32[]{:S(2)}, u32[]{:S(2)}) collective-permute-start(bf16[9,128,128]{2,1,0:T(8,128)(2,1)S(1)} %get-tuple-element.82), channel_id=1, source_target_pairs={{0,1},{1,0},{2,3},{3,2},{4,5},{5,4},{6,7},{7,6},{8,9},{9,8},{10,11... | collective-permute-start | bytes 884744 | tf_op jit(solution)/shard_map/ppermute | solution.py:724
  51.6 19.8 %all-to-all-start = ((bf16[16,72,128]{2,1,0:T(8,128)(2,1)}), bf16[16,72,128]{2,1,0:T(8,128)(2,1)S(1)}, u32[]{:S(2)}, u32[]{:S(2)}) async-start(bf16[16,72,128]{2,1,0:T(8,128)(2,1)} %bitcast.3), calls=%async_computation | async-start | bytes 589824 | tf_op jit(solution)/shard_map/all_to_all | solution.py:746
  72.7 14.4 %all-to-all-start.1 = ((bf16[16,72,128]{2,1,0:T(8,128)(2,1)}), bf16[16,72,128]{2,1,0:T(8,128)(2,1)S(1)}, u32[]{:S(2)}, u32[]{:S(2)}) async-start(bf16[16,72,128]{2,1,0:T(8,128)(2,1)} %shard_map.79), calls=%async_computation.1 | async-start | bytes 589824 | tf_op jit(solution)/shard_map/all_to_all | solution.py:755
  87.2 1.6 %collective-permute-start.7 = (bf16[9,128,128]{2,1,0:T(8,128)(2,1)S(1)}, bf16[9,128,128]{2,1,0:T(8,128)(2,1)S(1)}, u32[]{:S(2)}, u32[]{:S(2)}) collective-permute-start(bf16[9,128,128]{2,1,0:T(8,128)(2,1)S(1)} %shard_map.80.mine_ref), channel_id=1, source_target_pairs={{0,1},{1,0},{2,3},{3,2},{4,5},{5,4},{6,7},{7,6},{8,9},{9,8},{10,11... | collective-permute-start | bytes 884744 | tf_op jit(solution)/shard_map/ppermute | solution.py:794

commit v7 on v6

--- a/solution.py
+++ b/solution.py
@@ -129,22 +129,18 @@
     return go
 
 
-def columns_kernel(meta, f, g, near, far, raw, sem, *, cols, na):
-    last = cols - 16
+def columns_kernel(meta, f, g, out, raw, sem, *, cols, na, near):
+    right = meta[3] == (0 if near else 1)
+    start = pl.multiple_of((1 - meta[3] if near else meta[3]) * (cols - 16), 16)
     jobs = []
     go = copier(sem, jobs)
-    for i in range(2):
-        start = pl.multiple_of((meta[3] if i == 0 else 1 - meta[3]) * last, 16)
-        for n, x in enumerate((f, g)):
-            go(x.at[:, pl.ds(start, 16)], raw.at[i, n])
-    for c in jobs:
-        c.wait()
-    for i, out in enumerate((far, near)):
-        right = meta[3] == 1 - i
-        for n in range(2):
-            for k in range(na):
-                v = to_blocks([raw[i, n, 4 * k + t].astype(F32) for t in range(4)])
-                out[n, k] = jnp.where(right, v[16 * (4 - H) :], v[: 16 * H]).astype(BF16)
+    for n, x in enumerate((f, g)):
+        go(x.at[:, pl.ds(start, 16)], raw.at[n])
+    for n in range(2):
+        jobs[n].wait()
+        for k in range(na):
+            v = to_blocks([raw[n, 4 * k + t].astype(F32) for t in range(4)])
+            out[n, k] = jnp.where(right, v[16 * (4 - H) :], v[: 16 * H]).astype(BF16)
 
 
 def layout_kernel(meta, fi, gi, fx, gx, ax, f, g, sem, *, nj, na):
@@ -576,20 +572,22 @@
     meta = jnp.stack([lax.axis_index("row") * rows, lax.axis_index("col") * cols, length[0], odd]).astype(jnp.int32)
     sds = jax.ShapeDtypeStruct
 
-    near, far = pl.pallas_call(
-        functools.partial(columns_kernel, cols=cols, na=na),
-        in_specs=[SMEM] + [ANY] * 2,
-        out_specs=[VMEM] * 2,
-        out_shape=[pltpu.VMEM((2, na, 16 * H, C), BF16)] * 2,
-        scratch_shapes=[pltpu.VMEM((2, 2, rows, 16, C), BF16), pltpu.SemaphoreType.DMA((4,))],
-        compiler_params=params(10),
-        cost_estimate=cost(0, 2 << 20),
-    )(meta, *in_hbm(features, cotangent))
+    def columns(near):
+        return pl.pallas_call(
+            functools.partial(columns_kernel, cols=cols, na=na, near=near),
+            in_specs=[SMEM] + [ANY] * 2,
+            out_specs=VMEM,
+            out_shape=pltpu.VMEM((2, na, 16 * H, C), BF16),
+            scratch_shapes=[pltpu.VMEM((2, rows, 16, C), BF16), pltpu.SemaphoreType.DMA((2,))],
+            compiler_params=params(10),
+            cost_estimate=cost(0, 2 << 20),
+        )(meta, *in_hbm(features, cotangent))
+
     n = lax.axis_size("col")
     inner = [(i, i ^ 1) for i in range(n)]
     outer_pairs = [(i, i + 1) for i in range(1, n - 1, 2)]
-    od = lax.ppermute(far, "col", outer_pairs + [(j, i) for i, j in outer_pairs])
-    ev = lax.ppermute(near, "col", inner)
+    od = lax.ppermute(columns(False), "col", outer_pairs + [(j, i) for i, j in outer_pairs])
+    ev = lax.ppermute(columns(True), "col", inner)
 
     def pack(conv_layer, back_layer):
         return pl.pallas_call(

time: 90.9 us -> 90.7 us (level)
  starting transfers between devices: 29.9 us -> 28.1 us
  Pallas kernels: 52.2 us -> 53.5 us
    ppermute x2, starting transfers between devices: 1.19 us -> 5.06 us  [the longest x1 4.37 us: body(): ev = lax.ppermute(columns(True), 'col', inner)]
    ppermute x1, starting transfers between devices: 3.06 us -> 0.07 us  [body(): received = lax.ppermute(send, 'col', inner)]
    all_to_all x1, starting transfers between devices: 8.84 us -> 7.15 us  [body(): lax.all_to_all(share, axes, 0, 0, axis_index_groups=groups, tiled=True)]
    pallas_call x1 -> x2, Pallas kernels: 2.06 us -> 3.34 us  [columns(): pl.pallas_call(functools.partial(columns_kernel, cols=cols, na=na, near=n...]
    ppermute x4, starting transfers between devices: 12.7 us -> 11.7 us  [shift(): lax.ppermute(x, axis, [(i, i + step) for i in range(n) if 0 <= i + step <...]
  transfers between devices with their start and end apart: 10 -> 10, of which waited for: 4 -> 4; matrix products, arithmetic and copies ran while one was open for 0% -> 0% of each run, Pallas kernels for 52% -> 54%
where the time goes in v7:
time: 90.7 us; the launch traced here: 90.3 us
  Pallas kernels  53.5 us (59%)
  starting transfers between devices  28.1 us (31%)
  waiting for transfers between devices  7.14 us (8%)
  between operations  1.51 us (2%)
    pallas_call x1, Pallas kernels, body(): pl.pallas_call(functools.partial(inner_kernel, na=na, nj=nj), in_specs=[S...  14.9 us
    ppermute x4, starting transfers between devices, shift(): lax.ppermute(x, axis, [(i, i + step) for i in range(n) if 0 <= i + step <...  11.7 us
    pallas_call x1, Pallas kernels, body(): pl.pallas_call(functools.partial(last_kernel, na=na, nj=nj), in_specs=[SM...  9.3 us
    pallas_call x1, Pallas kernels, body(): pl.pallas_call(functools.partial(middle_kernel, na=na, nj=nj), in_specs=[...  8.07 us
    all_to_all x1, starting transfers between devices, body(): lax.all_to_all(share, axes, 0, 0, axis_index_groups=groups, tiled=True)  7.15 us
    pallas_call x1, Pallas kernels, body(): pl.pallas_call(functools.partial(edge_kernel, na=na, nj=nj), in_specs=[SM...  7.11 us
    ppermute x1, starting transfers between devices, body(): ev = lax.ppermute(columns(True), 'col', inner)  4.37 us
    pallas_call x1, Pallas kernels, body(): pl.pallas_call(functools.partial(layout_kernel, nj=nj, na=na), in_specs=[...  4.13 us
  transfers between devices with their start and end apart: 10, of which 4 were waited for; matrix products, arithmetic and copies ran while one was open for 0% of the time, Pallas kernels for 54%

profile of v7, /device:TPU:0, one launch (start us, length us, event | category | flops | bytes accessed | tf_op | source)
XLA Modules:
  0.0 90.3 jit_solution(12469650145814580056)
XLA Ops:
  1.3 0.1 pad_add_fusion.meta
  1.4 1.7 %shard_map.69 = bf16[2,16,48,128]{3,2,1,0:T(8,128)(2,1)S(1)} custom-call(s32[4]{0:T(128)S(1)} %pad_add_fusion.meta, bf16[64,128,128]{2,1,0:T(8,128)(2,1)} %fi.1, bf16[64,128,128]{2,1,0:T(8,128)(2,1)} %gi.1), custom_call_target="tpu_custom_call" | custom-call | bytes 2097152 | tf_op jit(solution)/shard_map/pallas_call | solution.py:576
  3.0 0.7 collective-permute-start.1
  3.7 1.7 %shard_map.68 = bf16[2,16,48,128]{3,2,1,0:T(8,128)(2,1)S(1)} custom-call(s32[4]{0:T(128)S(1)} %pad_add_fusion.meta, bf16[64,128,128]{2,1,0:T(8,128)(2,1)} %fi.1, bf16[64,128,128]{2,1,0:T(8,128)(2,1)} %gi.1), custom_call_target="tpu_custom_call" | custom-call | bytes 2097152 | tf_op jit(solution)/shard_map/pallas_call | solution.py:576
  5.4 4.4 %collective-permute-start = (bf16[2,16,48,128]{3,2,1,0:T(8,128)(2,1)S(1)}, bf16[2,16,48,128]{3,2,1,0:T(8,128)(2,1)S(1)}, u32[]{:S(2)}, u32[]{:S(2)}) collective-permute-start(bf16[2,16,48,128]{3,2,1,0:T(8,128)(2,1)S(1)} %shard_map.68), channel_id=1, source_target_pairs={{0,1},{1,0},{2,3},{3,2},{4,5},{5,4},{6,7},{7,6},{8,9},{9,8},{10,11... | collective-permute-start | bytes 1179656 | tf_op jit(solution)/shard_map/ppermute | solution.py:590
  9.8 0.6 shard_map.67._cm.cm
  10.4 0.0 copy-start
  10.4 4.1 %shard_map.70 = (bf16[16,512,128]{2,1,0:T(8,128)(2,1)S(1)}, bf16[16,512,128]{2,1,0:T(8,128)(2,1)S(1)}, bf16[16,512,128]{2,1,0:T(8,128)(2,1)S(1)}) custom-call(s32[4]{0:T(128)S(1)} %pad_add_fusion.meta, bf16[64,128,128]{2,1,0:T(8,128)(2,1)} %fi.1, bf16[64,128,128]{2,1,0:T(8,128)(2,1)} %gi.1), custom_call_target="tpu_custom_call" | custom-call | bytes 12582912 | tf_op jit(solution)/shard_map/pallas_call | solution.py:613
  14.5 0.2 shard_map.71
  14.8 0.0 collective-permute-done.ev_ref
  14.8 1.7 %shard_map.72 = (bf16[16,608,128]{2,1,0:T(8,128)(2,1)S(1)}, bf16[16,608,128]{2,1,0:T(8,128)(2,1)S(1)}, bf16[16,608,128]{2,1,0:T(8,128)(2,1)S(1)}, bf16[3,608,128...) custom-call(s32[4]{0:T(128)S(1)} %pad_add_fusion.meta, ...), custom_call_target="tpu_custom_call" | custom-call | bytes 4194304 | tf_op jit(solution)/shard_map/pallas_call | solution.py:622
  16.6 3.4 %collective-permute-start.2 = (bf16[3,608,128]{2,1,0:T(8,128)(2,1)S(1)}, bf16[3,608,128]{2,1,0:T(8,128)(2,1)S(1)}, u32[]{:S(2)}, u32[]{:S(2)}) collective-permute-start(bf16[3,608,128]{2,1,0:T(8,128)(2,1)S(1)} %get-tuple-element.56), channel_id=1, source_target_pairs={{0,4},{4,8},{8,12},{12,16},{16,20},{20,24},{24,28},{1,5},{5,9},{9,... | collective-permute-start | bytes 1400840 | tf_op jit(solution)/shard_map/ppermute | solution.py:563
  20.0 1.5 %collective-permute-start.3 = (bf16[3,608,128]{2,1,0:T(8,128)(2,1)S(1)}, bf16[3,608,128]{2,1,0:T(8,128)(2,1)S(1)}, u32[]{:S(2)}, u32[]{:S(2)}) collective-permute-start(bf16[3,608,128]{2,1,0:T(8,128)(2,1)S(1)} %get-tuple-element.57), channel_id=1, source_target_pairs={{4,0},{8,4},{12,8},{16,12},{20,16},{24,20},{28,24},{5,1},{9,5},{13... | collective-permute-start | bytes 1400840 | tf_op jit(solution)/shard_map/ppermute | solution.py:563
  21.5 0.2 shard_map.73
  21.7 14.9 %shard_map.74 = (f32[2,384,384]{2,1,0:T(8,128)S(1)}, bf16[1536,256]{1,0:T(8,128)(2,1)}, bf16[1536,256]{1,0:T(8,128)(2,1)}, bf16[16,512,128]{2,1,0:T(8,128)(2,1)}...) custom-call(s32[4]{0:T(128)S(1)} %pad_add_fusion.meta, ...), custom_call_target="tpu_custom_call", output_to_operand_aliasing={{10}: (8, {}), {11}: (9, {})} | custom-call | bytes 1048576 | tf_op jit(solution)/shard_map/pallas_call | solution.py:635
  36.6 5.3 %collective-permute-start.4 = (bf16[3,608,128]{2,1,0:T(8,128)(2,1)}, bf16[3,608,128]{2,1,0:T(8,128)(2,1)}, u32[]{:S(2)}, u32[]{:S(2)}) collective-permute-start(bf16[3,608,128]{2,1,0:T(8,128)(2,1)} %get-tuple-element.58), channel_id=1, source_target_pairs={{0,4},{4,8},{8,12},{12,16},{16,20},{20,24},{24,28},{1,5},{5,9},{9,... | collective-permute-start | bytes 1400840 | tf_op jit(solution)/shard_map/ppermute | solution.py:563
  42.0 1.5 %collective-permute-start.5 = (bf16[3,608,128]{2,1,0:T(8,128)(2,1)}, bf16[3,608,128]{2,1,0:T(8,128)(2,1)}, u32[]{:S(2)}, u32[]{:S(2)}) collective-permute-start(bf16[3,608,128]{2,1,0:T(8,128)(2,1)} %get-tuple-element.59), channel_id=1, source_target_pairs={{4,0},{8,4},{12,8},{16,12},{20,16},{24,20},{28,24},{5,1},{9,5},{13... | collective-permute-start | bytes 1400840 | tf_op jit(solution)/shard_map/ppermute | solution.py:563
  43.5 0.0 collective-permute-done.2.up.upa
  43.5 7.1 %shard_map.75 = (bf16[2,2,576,128]{3,2,1,0:T(8,128)(2,1)}, f32[2,2,512,128]{3,2,1,0:T(8,128)}, bf16[2,2,544,128]{3,2,1,0:T(8,128)(2,1)}, bf16[2,2,512,128]{3,2,1...) custom-call(s32[4]{0:T(128)S(1)} %pad_add_fusion.meta, ...), custom_call_target="tpu_custom_call" | custom-call | bytes 1048576 | tf_op jit(solution)/shard_map/pallas_call | solution.py:673
  50.6 0.1 collective-permute-start.6
  50.7 1.6 %collective-permute-done.6.y_ref = bf16[9,128,128]{2,1,0:T(8,128)(2,1)S(1)} collective-permute-done((bf16[9,128,128]{2,1,0:T(8,128)(2,1)S(1)}, bf16[9,128,128]{2,1,0:T(8,128)(2,1)S(1)}, u32[]{:S(2)}, u32[]{:S(2)}) %collective-permute-start.6) | collective-permute-done | bytes 294944 | tf_op jit(solution)/shard_map/ppermute | solution.py:722
  52.3 0.8 shard_map.79
  53.0 7.1 %all-to-all-start = ((bf16[16,72,128]{2,1,0:T(8,128)(2,1)}), bf16[16,72,128]{2,1,0:T(8,128)(2,1)S(1)}, u32[]{:S(2)}, u32[]{:S(2)}) async-start(bf16[16,72,128]{2,1,0:T(8,128)(2,1)} %bitcast.3), calls=%async_computation | async-start | bytes 589824 | tf_op jit(solution)/shard_map/all_to_all | solution.py:744
  60.2 8.1 %shard_map.76 = (bf16[64,128,128]{2,1,0:T(8,128)(2,1)}, bf16[64,128,128]{2,1,0:T(8,128)(2,1)}) custom-call(s32[4]{0:T(128)S(1)} %pad_add_fusion.meta, bf16[1536,256]{1,0:T(8,128)(2,1)S(1)} %get-tuple-element.44._w.wc2, bf16[1536,256]{1,0:T(8,128)(2,1)S(1)} %get-tuple-element.50.wb1, ...), custom_call_target="tpu_custom_call", output_to_operand_aliasing={{0}: (10, {}), {1}: (11, {})} | custom-call | flops 48318382080 | bytes 25165824 | tf_op jit(solution)/shard_map/pallas_call | solution.py:701
  68.3 2.9 %all-to-all-done.x_ref = bf16[16,72,128]{2,1,0:T(8,128)(2,1)S(1)} async-done(((bf16[16,72,128]{2,1,0:T(8,128)(2,1)}), bf16[16,72,128]{2,1,0:T(8,128)(2,1)S(1)}, u32[]{:S(2)}, u32[]{:S(2)}) %all-to-all-start) | async-done | bytes 294944 | tf_op jit(solution)/shard_map/all_to_all | solution.py:744
  71.2 1.3 %shard_map.80 = bf16[16,72,128]{2,1,0:T(8,128)(2,1)} custom-call(s32[4]{0:T(128)S(1)} %pad_add_fusion.meta, bf16[16,72,128]{2,1,0:T(8,128)(2,1)S(1)} %all-to-all-done.x_ref, bf16[64,128,128]{2,1,0:T(8,128)(2,1)} %get-tuple-element.73._out), custom_call_target="tpu_custom_call" | custom-call | bytes 2097152 | tf_op jit(solution)/shard_map/pallas_call | solution.py:745
  72.5 4.0 %all-to-all-start.1 = ((bf16[16,72,128]{2,1,0:T(8,128)(2,1)}), bf16[16,72,128]{2,1,0:T(8,128)(2,1)S(1)}, u32[]{:S(2)}, u32[]{:S(2)}) async-start(bf16[16,72,128]{2,1,0:T(8,128)(2,1)} %shard_map.80), calls=%async_computation.1 | async-start | bytes 589824 | tf_op jit(solution)/shard_map/all_to_all | solution.py:753
  76.6 9.3 %shard_map.77 = (bf16[64,128,128]{2,1,0:T(8,128)(2,1)}, bf16[64,128,128]{2,1,0:T(8,128)(2,1)}) custom-call(s32[4]{0:T(128)S(1)} %pad_add_fusion.meta, f32[608,128]{1,0:T(8,128)S(1)} %shard_map.67._cm.cm, bf16[16,512,128]{2,1,0:T(8,128)(2,1)} %get-tuple-element.53.fxi, ...), custom_call_target="tpu_custom_call", output_to_operand_aliasing={{0}: (19, {}), {1}: (20, {})} | custom-call | flops 48318382080 | bytes 25165824 | tf_op jit(solution)/shard_map/pallas_call | solution.py:754
  85.9 1.1 %all-to-all-done.1 = bf16[16,72,128]{2,1,0:T(8,128)(2,1)S(1)} async-done(((bf16[16,72,128]{2,1,0:T(8,128)(2,1)}), bf16[16,72,128]{2,1,0:T(8,128)(2,1)S(1)}, u32[]{:S(2)}, u32[]{:S(2)}) %all-to-all-start.1) | async-done | bytes 294944 | tf_op jit(solution)/shard_map/all_to_all | solution.py:753
  87.0 0.1 collective-permute-start.7
  87.1 1.6 %collective-permute-done.7.other_ref = bf16[9,128,128]{2,1,0:T(8,128)(2,1)S(1)} collective-permute-done((bf16[9,128,128]{2,1,0:T(8,128)(2,1)S(1)}, bf16[9,128,128]{2,1,0:T(8,128)(2,1)S(1)}, u32[]{:S(2)}, u32[]{:S(2)}) %collective-permute-start.7) | collective-permute-done | bytes 294944 | tf_op jit(solution)/shard_map/ppermute | solution.py:792
  88.6 1.6 %shard_map.82 = f32[2,9,128,128]{3,2,1,0:T(8,128)} custom-call(s32[4]{0:T(128)S(1)} %pad_add_fusion.meta, bf16[9,128,128]{2,1,0:T(8,128)(2,1)S(1)} %shard_map.81.mine_ref, bf16[9,128,128]{2,1,0:T(8,128)(2,1)S(1)} %collective-permute-done.7.other_ref), custom_call_target="tpu_custom_call" | custom-call | bytes 2097152 | tf_op jit(solution)/shard_map/pallas_call | solution.py:793
  (7 shorter events, 0.0 us)
Async XLA Ops:
  3.0 11.8 %collective-permute-start.1 = (bf16[2,16,48,128]{3,2,1,0:T(8,128)(2,1)S(1)}, bf16[2,16,48,128]{3,2,1,0:T(8,128)(2,1)S(1)}, u32[]{:S(2)}, u32[]{:S(2)}) collective-permute-start(bf16[2,16,48,128]{3,2,1,0:T(8,128)(2,1)S(1)} %shard_map.69), channel_id=1, source_target_pairs={{1,2},{2,1},{5,6},{6,5},{9,10},{10,9},{13,14},{14,13},{17,18},{18,... | collective-permute-start | bytes 1179656 | tf_op jit(solution)/shard_map/ppermute | solution.py:589
  5.4 9.4 %collective-permute-start = (bf16[2,16,48,128]{3,2,1,0:T(8,128)(2,1)S(1)}, bf16[2,16,48,128]{3,2,1,0:T(8,128)(2,1)S(1)}, u32[]{:S(2)}, u32[]{:S(2)}) collective-permute-start(bf16[2,16,48,128]{3,2,1,0:T(8,128)(2,1)S(1)} %shard_map.68), channel_id=1, source_target_pairs={{0,1},{1,0},{2,3},{3,2},{4,5},{5,4},{6,7},{7,6},{8,9},{9,8},{10,11... | collective-permute-start | bytes 1179656 | tf_op jit(solution)/shard_map/ppermute | solution.py:590
  10.4 4.1 %copy-start = (bf16[2,3,3,128,128]{4,3,2,1,0:T(8,128)(2,1)S(1)}, bf16[2,3,3,128,128]{4,3,2,1,0:T(8,128)(2,1)}, u32[]{:S(2)}) copy-start(bf16[2,3,3,128,128]{4,3,2,1,0:T(8,128)(2,1)} %k_ref.3) | copy-start | bytes 1769476
  16.6 26.9 %collective-permute-start.2 = (bf16[3,608,128]{2,1,0:T(8,128)(2,1)S(1)}, bf16[3,608,128]{2,1,0:T(8,128)(2,1)S(1)}, u32[]{:S(2)}, u32[]{:S(2)}) collective-permute-start(bf16[3,608,128]{2,1,0:T(8,128)(2,1)S(1)} %get-tuple-element.56), channel_id=1, source_target_pairs={{0,4},{4,8},{8,12},{12,16},{16,20},{20,24},{24,28},{1,5},{5,9},{9,... | collective-permute-start | bytes 1400840 | tf_op jit(solution)/shard_map/ppermute | solution.py:563
  20.0 23.5 %collective-permute-start.3 = (bf16[3,608,128]{2,1,0:T(8,128)(2,1)S(1)}, bf16[3,608,128]{2,1,0:T(8,128)(2,1)S(1)}, u32[]{:S(2)}, u32[]{:S(2)}) collective-permute-start(bf16[3,608,128]{2,1,0:T(8,128)(2,1)S(1)} %get-tuple-element.57), channel_id=1, source_target_pairs={{4,0},{8,4},{12,8},{16,12},{20,16},{24,20},{28,24},{5,1},{9,5},{13... | collective-permute-start | bytes 1400840 | tf_op jit(solution)/shard_map/ppermute | solution.py:563
  36.6 39.9 %collective-permute-start.4 = (bf16[3,608,128]{2,1,0:T(8,128)(2,1)}, bf16[3,608,128]{2,1,0:T(8,128)(2,1)}, u32[]{:S(2)}, u32[]{:S(2)}) collective-permute-start(bf16[3,608,128]{2,1,0:T(8,128)(2,1)} %get-tuple-element.58), channel_id=1, source_target_pairs={{0,4},{4,8},{8,12},{12,16},{16,20},{20,24},{24,28},{1,5},{5,9},{9,... | collective-permute-start | bytes 1400840 | tf_op jit(solution)/shard_map/ppermute | solution.py:563
  42.0 34.6 %collective-permute-start.5 = (bf16[3,608,128]{2,1,0:T(8,128)(2,1)}, bf16[3,608,128]{2,1,0:T(8,128)(2,1)}, u32[]{:S(2)}, u32[]{:S(2)}) collective-permute-start(bf16[3,608,128]{2,1,0:T(8,128)(2,1)} %get-tuple-element.59), channel_id=1, source_target_pairs={{4,0},{8,4},{12,8},{16,12},{20,16},{24,20},{28,24},{5,1},{9,5},{13... | collective-permute-start | bytes 1400840 | tf_op jit(solution)/shard_map/ppermute | solution.py:563
  50.6 1.6 %collective-permute-start.6 = (bf16[9,128,128]{2,1,0:T(8,128)(2,1)S(1)}, bf16[9,128,128]{2,1,0:T(8,128)(2,1)S(1)}, u32[]{:S(2)}, u32[]{:S(2)}) collective-permute-start(bf16[9,128,128]{2,1,0:T(8,128)(2,1)S(1)} %get-tuple-element.78), channel_id=1, source_target_pairs={{0,1},{1,0},{2,3},{3,2},{4,5},{5,4},{6,7},{7,6},{8,9},{9,8},{10,11... | collective-permute-start | bytes 884744 | tf_op jit(solution)/shard_map/ppermute | solution.py:722
  53.0 18.1 %all-to-all-start = ((bf16[16,72,128]{2,1,0:T(8,128)(2,1)}), bf16[16,72,128]{2,1,0:T(8,128)(2,1)S(1)}, u32[]{:S(2)}, u32[]{:S(2)}) async-start(bf16[16,72,128]{2,1,0:T(8,128)(2,1)} %bitcast.3), calls=%async_computation | async-start | bytes 589824 | tf_op jit(solution)/shard_map/all_to_all | solution.py:744
  72.5 14.4 %all-to-all-start.1 = ((bf16[16,72,128]{2,1,0:T(8,128)(2,1)}), bf16[16,72,128]{2,1,0:T(8,128)(2,1)S(1)}, u32[]{:S(2)}, u32[]{:S(2)}) async-start(bf16[16,72,128]{2,1,0:T(8,128)(2,1)} %shard_map.80), calls=%async_computation.1 | async-start | bytes 589824 | tf_op jit(solution)/shard_map/all_to_all | solution.py:753
  87.0 1.6 %collective-permute-start.7 = (bf16[9,128,128]{2,1,0:T(8,128)(2,1)S(1)}, bf16[9,128,128]{2,1,0:T(8,128)(2,1)S(1)}, u32[]{:S(2)}, u32[]{:S(2)}) collective-permute-start(bf16[9,128,128]{2,1,0:T(8,128)(2,1)S(1)} %shard_map.81.mine_ref), channel_id=1, source_target_pairs={{0,1},{1,0},{2,3},{3,2},{4,5},{5,4},{6,7},{7,6},{8,9},{9,8},{10,11... | collective-permute-start | bytes 884744 | tf_op jit(solution)/shard_map/ppermute | solution.py:792
